TPU v7x, 32 devices: a whole 2x2x4 slice. The times are simulated.
32 devices in a mesh: section: 2 (over core), dp: 16 (over z, y, x).
Axes of the slice: x: 2, y: 2, z: 4, core: 2. Of those that a mesh axis runs over, the one named last changes fastest.
Arguments:
- frames: bfloat16 [2, 1024, 84, 336], P(None, 'dp'), may hold values from -4 to 4
- options: int32 [2, 1024, 3], P(None, 'dp'), may hold values from 0 to 17
- legal: int32 [2, 1024, 18], P(None, 'dp'), may hold values from 0 to 1, as said below
- games: int32 [2, 1024], P(None, 'dp'), may hold values from 0 to 7
- valid: int32 [2, 1024, 3], P(None, 'dp'), may hold values from 0 to 1, as said below
- rewards: float32 [2, 1024, 3], P(None, 'dp'), may hold values from -5 to 5
- returns: float32 [2, 1024, 4], P(None, 'dp'), may hold values from -5 to 5
- conv_kernels: float32 [256, 48], P('dp'), may hold values from -0.375 to 0.375
- enc_linear: float32 [2592, 128], P(None, 'dp'), may hold values from -0.125 to 0.125
- plan_mats: float32 [3, 128, 128], P(None, None, 'dp'), may hold values from -0.5 to 0.5
- option_emb: float32 [18, 128], P(None, 'dp'), may hold values from -3 to 3
- heads: float32 [3, 8, 128], P(None, None, 'dp'), may hold values from -0.5 to 0.5
- biases: float32 [304], replicated, may hold values from -0.5 to 0.5
- conv_moment: float32 [256, 48], P('dp'), may hold values from 1.5668244e-09 to 6.267298e-09
- lin_rows: float32 [2592], replicated, may hold values from 1.5668244e-09 to 6.267298e-09
- lin_cols: float32 [128], P('dp'), may hold values from 1.5668244e-09 to 6.267298e-09
- mats_rows: float32 [3, 128], replicated, may hold values from 1.5668244e-09 to 6.267298e-09
- mats_cols: float32 [3, 128], P(None, 'dp'), may hold values from 1.5668244e-09 to 6.267298e-09
- emb_moment: float32 [18, 128], P(None, 'dp'), may hold values from 1.5668244e-09 to 6.267298e-09
- head_moment: float32 [3, 8, 128], P(None, None, 'dp'), may hold values from 1.5668244e-09 to 6.267298e-09
- bias_moment: float32 [304], replicated, may hold values from 1.5668244e-09 to 6.267298e-09
Outputs:
- conv_new: float32 [256, 48], P('dp')
- conv_grad: float32 [256, 48], P('dp')
- conv_moment_new: float32 [256, 48], P('dp')
- lin_new: float32 [2592, 128], P(None, 'dp')
- lin_grad: float32 [2592, 128], P(None, 'dp')
- lin_rows_new: float32 [2592], replicated
- lin_cols_new: float32 [128], P('dp')
- mats_new: float32 [3, 128, 128], P(None, None, 'dp')
- mats_grad: float32 [3, 128, 128], P(None, None, 'dp')
- mats_rows_new: float32 [3, 128], replicated
- mats_cols_new: float32 [3, 128], P(None, 'dp')
- emb_new: float32 [18, 128], P(None, 'dp')
- emb_grad: float32 [18, 128], P(None, 'dp')
- emb_moment_new: float32 [18, 128], P(None, 'dp')
- heads_new: float32 [3, 8, 128], P(None, None, 'dp')
- heads_grad: float32 [3, 8, 128], P(None, None, 'dp')
- head_moment_new: float32 [3, 8, 128], P(None, None, 'dp')
- bias_new: float32 [304], replicated
- bias_grad: float32 [304], replicated
- bias_moment_new: float32 [304], replicated
- grad_norm: float32 [], replicated
- loss: float32 [], replicated
- conv_low: bfloat16 [256, 48], P('dp')
- lin_low: bfloat16 [2592, 128], P(None, 'dp')
Inputs may be any that keep to these rules, and one draw needn't show every extreme that they name: Option 0 is legal in every row. In every row the first step is valid and the valid steps come first.
All inputs are finite; a program needn't handle non-finite values.
Results may differ from a plain program's by a relative error of at most 0.0075.
Values may be sent and summed in bfloat16 or wider, within the bound.
A program may use at most 320 MiB of HBM per device.

v0:
```python
import jax
import jax.numpy as jnp
from jax import lax
from jax.sharding import PartitionSpec as P

D = 128
C1 = 16
C2 = 32
OPTS = 18
KERN = 256
GAMES = 8
FEAT = 2592
BIAS = 304


CLIP_LIMIT = 0.05
DECAY_RATE = 0.8
STEP_RATE = 0.5
FLOOR_ONE = 1e-30
FLOOR_TWO = 0.001


def shifted(value, axis, steps):
    count = lax.axis_size(axis)
    first, last = (max(0, -steps), min(count, count - steps))
    return lax.ppermute(value, axis, [(source, source + steps) for source in range(first, last)])


def rounded(value):
    return lax.optimization_barrier(value.astype(jnp.bfloat16)).astype(jnp.float32)


def passing(value):
    return value


def value_keep(value):
    return (rounded(value), None)


def value_pass(kept, grad):
    return (grad,)


def grad_keep(value):
    return (value, None)


def grad_round(kept, grad):
    return (rounded(grad),)


def rounders():
    value_low = jax.custom_vjp(rounded)
    value_low.defvjp(value_keep, value_pass)
    grad_low = jax.custom_vjp(passing)
    grad_low.defvjp(grad_keep, grad_round)
    return (value_low, grad_low)


def matmul_plain(operand, matrix):
    return jnp.dot(operand, matrix, preferred_element_type=jnp.float32)


def silu_slope(value):
    sigma = jax.nn.sigmoid(value)
    return sigma * (1.0 + value * (1.0 - sigma))


def plan_loss(
    states,
    matrices,
    option_table,
    head_table,
    value_bias,
    options,
    legal,
    games,
    valid,
    rewards,
    returns,
):
    value_low, grad_low = rounders()
    row_count = states.shape[0]
    feature_count = states.shape[1]
    option_count = option_table.shape[0]
    trans_in = matrices[0]
    trans_out = matrices[1]
    value_in = matrices[2]
    game_pick = jax.nn.one_hot(games, head_table.shape[1], dtype=jnp.float32)
    head_rows = jnp.einsum("bg,kgd->kbd", game_pick, head_table, precision=lax.Precision.HIGHEST)
    reward_head = head_rows[0]
    discount_head = head_rows[1]
    value_head = head_rows[2]
    valid_float = valid.astype(jnp.float32)
    pre_all = grad_low(matmul_plain(states, trans_in)[:, None, :] + option_table[None, :, :])
    hidden_all = jax.nn.silu(pre_all)
    change_all = grad_low(
        matmul_plain(
            value_low(hidden_all).reshape(row_count * option_count, feature_count), trans_out
        )
    )
    after_all = states[:, None, :] + change_all.reshape(row_count, option_count, feature_count)
    after_low = value_low(after_all)
    judged_all = jax.nn.silu(
        grad_low(
            matmul_plain(after_low.reshape(row_count * option_count, feature_count), value_in)
            + value_bias
        )
    )
    judged_all = judged_all.reshape(row_count, option_count, feature_count)
    value_all = jnp.sum(judged_all * value_head[:, None, :], axis=2)
    reward_all = jnp.sum(hidden_all * reward_head[:, None, :], axis=2)
    discount_all = jax.nn.sigmoid(jnp.sum(hidden_all * discount_head[:, None, :], axis=2))
    backed_up = reward_all + discount_all * value_all
    allowed = legal > 0
    highest = jnp.max(jnp.where(allowed, backed_up, -1e30), axis=1, keepdims=True)
    shares = jnp.where(allowed, jnp.exp(jnp.where(allowed, backed_up - highest, -60.0)), 0.0)
    planned = jnp.sum(shares * backed_up, axis=1) / jnp.sum(shares, axis=1)
    choose = jax.nn.one_hot(options[:, 0], option_count, dtype=jnp.float32)
    rollout = jnp.sum(choose[:, :, None] * after_all, axis=1)
    rollout_low = jnp.sum(choose[:, :, None] * after_low, axis=1)
    plan_miss = planned - returns[:, 0]
    reward_miss = jnp.sum(choose * reward_all, axis=1) - rewards[:, 0]
    value_miss = jnp.sum(choose * value_all, axis=1) - returns[:, 1]
    errors = valid_float[:, 0] * (
        plan_miss * plan_miss + reward_miss * reward_miss + value_miss * value_miss
    )
    for depth_k in range(1, options.shape[1]):
        option_bias = matmul_plain(
            jax.nn.one_hot(options[:, depth_k], option_count, dtype=jnp.float32), option_table
        )
        hidden_k = jax.nn.silu(grad_low(matmul_plain(rollout_low, trans_in) + option_bias))
        rollout = rollout + grad_low(matmul_plain(value_low(hidden_k), trans_out))
        rollout_low = value_low(rollout)
        judged_k = jax.nn.silu(grad_low(matmul_plain(rollout_low, value_in) + value_bias))
        reward_miss = jnp.sum(hidden_k * reward_head, axis=1) - rewards[:, depth_k]
        value_miss = jnp.sum(judged_k * value_head, axis=1) - returns[:, depth_k + 1]
        errors = errors + valid_float[:, depth_k] * (
            reward_miss * reward_miss + value_miss * value_miss
        )
    return jnp.sum(errors)


def patches(grid, stride, outputs):
    frame_count = grid.shape[0]
    blocks = grid.shape[1] // stride
    columns = grid.shape[2] // blocks
    blocked = grid.reshape(frame_count, blocks, stride, blocks, columns)
    tall = jnp.stack(
        [blocked[:, block_row : block_row + outputs] for block_row in range(2)], axis=2
    )
    wide = jnp.stack(
        [tall[:, :, :, :, block_col : block_col + outputs] for block_col in range(2)], axis=5
    )
    return wide.transpose(0, 1, 4, 2, 3, 5, 6).reshape(
        frame_count * outputs * outputs, 4 * stride * columns
    )


def unpatch(pieces, frame_count, stride, outputs, columns):
    blocks = outputs + 1
    parted = pieces.reshape(frame_count, outputs, outputs, 2, stride, 2, columns).transpose(
        0, 1, 3, 4, 2, 5, 6
    )
    gathered = jnp.zeros((frame_count, blocks, stride, blocks, columns), pieces.dtype)
    for block_row in range(2):
        for block_col in range(2):
            gathered = gathered + jnp.pad(
                parted[:, :, block_row, :, :, block_col, :],
                ((0, 0), (block_row, 1 - block_row), (0, 0), (block_col, 1 - block_col), (0, 0)),
            )
    return gathered.reshape(frame_count, blocks * stride, blocks * columns)


def encode(frame_block, kernels, linear, bias_enc):
    frame_count = frame_block.shape[0]
    out_one = frame_block.shape[1] // 4 - 1
    out_two = out_one // 2 - 1
    patch_one = patches(frame_block, 4, out_one)
    z_one = jnp.dot(patch_one, kernels[:, :C1], preferred_element_type=jnp.float32) + bias_enc[:C1]
    a_one = jax.nn.silu(z_one).astype(jnp.bfloat16).reshape(frame_count, out_one, out_one * C1)
    patch_two = patches(a_one, 2, out_two)
    z_two = (
        jnp.dot(patch_two, kernels[:, C1:], preferred_element_type=jnp.float32)
        + bias_enc[C1 : C1 + C2]
    )
    a_two = jax.nn.silu(z_two).astype(jnp.bfloat16).reshape(frame_count, out_two * out_two * C2)
    states = (
        jnp.dot(a_two, linear, preferred_element_type=jnp.float32) + bias_enc[C1 + C2 :]
    ).astype(jnp.bfloat16)
    return (states, z_one, a_one, z_two, a_two)


def encoder_blank(frame_count, frame_side):
    out_one = frame_side // 4 - 1
    out_two = out_one // 2 - 1
    return (
        jnp.zeros((frame_count, D), jnp.bfloat16),
        jnp.zeros((frame_count * out_one * out_one, C1), jnp.float32),
        jnp.zeros((frame_count, out_one, out_one * C1), jnp.bfloat16),
        jnp.zeros((frame_count * out_two * out_two, C2), jnp.float32),
        jnp.zeros((frame_count, out_two * out_two * C2), jnp.bfloat16),
    )


def contract_rows(first_arg, second_arg):
    return lax.dot_general(
        first_arg, second_arg, (((0,), (0,)), ((), ())), preferred_element_type=jnp.float32
    )


def encode_back(frame_block, kernels, linear, saved, returned):
    z_one, a_one, z_two, a_two = saved
    frame_count = frame_block.shape[0]
    out_one = frame_block.shape[1] // 4 - 1
    out_two = out_one // 2 - 1
    grad_linear = contract_rows(a_two, returned)
    da_two = jnp.dot(returned, linear.T, preferred_element_type=jnp.float32).reshape(
        frame_count * out_two * out_two, C2
    )
    dz_two = (da_two * silu_slope(z_two)).astype(jnp.bfloat16)
    grad_two = contract_rows(patches(a_one, 2, out_two), dz_two)
    dpatch = jnp.dot(dz_two, kernels[:, C1:].T, preferred_element_type=jnp.float32)
    da_one = unpatch(dpatch, frame_count, 2, out_two, 2 * C1).reshape(
        frame_count * out_one * out_one, C1
    )
    dz_one = (da_one * silu_slope(z_one)).astype(jnp.bfloat16)
    grad_one = contract_rows(patches(frame_block, 4, out_one), dz_one)
    bias_part = jnp.concatenate(
        [
            jnp.sum(dz_one.astype(jnp.float32), axis=0),
            jnp.sum(dz_two.astype(jnp.float32), axis=0),
            jnp.sum(returned.astype(jnp.float32), axis=0),
        ]
    )
    return (jnp.concatenate([grad_one, grad_two], axis=1), grad_linear, bias_part)


def collect(shards):
    return (
        lax.all_gather(shards[0], "dp", axis=0, tiled=True),
        lax.all_gather(shards[1], "dp", axis=1, tiled=True),
        lax.all_gather(shards[2], "dp", axis=2, tiled=True),
        lax.all_gather(shards[3], "dp", axis=1, tiled=True),
        lax.all_gather(shards[4], "dp", axis=2, tiled=True),
    )


def spread(gradients):
    return (
        lax.psum_scatter(gradients[0], "dp", scatter_dimension=0, tiled=True),
        lax.psum_scatter(gradients[1], "dp", scatter_dimension=1, tiled=True),
        lax.psum_scatter(gradients[2], "dp", scatter_dimension=2, tiled=True),
        lax.psum_scatter(gradients[3], "dp", scatter_dimension=1, tiled=True),
        lax.psum_scatter(gradients[4], "dp", scatter_dimension=2, tiled=True),
    )


def relative(square_total, entries):
    return jnp.maximum(FLOOR_TWO, jnp.sqrt(square_total / entries))


def unfactored(weight, grad, moment, scale):
    moment_new = DECAY_RATE * moment + (1.0 - DECAY_RATE) * (grad * grad + FLOOR_ONE)
    return (weight - STEP_RATE * scale * grad * lax.rsqrt(moment_new), moment_new)


def per_device(
    frames,
    options,
    legal,
    games,
    valid,
    rewards,
    returns,
    conv_kernels,
    enc_linear,
    plan_mats,
    option_emb,
    heads,
    biases,
    conv_moment,
    lin_rows,
    lin_cols,
    mats_rows,
    mats_cols,
    emb_moment,
    head_moment,
    bias_moment,
):
    totals = lax.psum(
        (
            jnp.sum(valid.astype(jnp.float32)),
            jnp.sum(conv_kernels * conv_kernels),
            jnp.sum(enc_linear * enc_linear),
            jnp.sum(plan_mats * plan_mats),
            jnp.sum(option_emb * option_emb),
            jnp.sum(heads * heads),
        ),
        "dp",
    )
    inverse_count = 1.0 / totals[0]
    section_id = lax.axis_index("section")
    low_shards = (
        conv_kernels.astype(jnp.bfloat16),
        enc_linear.astype(jnp.bfloat16),
        plan_mats.astype(jnp.bfloat16),
        option_emb.astype(jnp.bfloat16),
        heads.astype(jnp.bfloat16),
    )
    bias_enc = biases[: C1 + C2 + D]
    value_bias = biases[C1 + C2 + D :]
    grad_total = None
    bias_total = jnp.zeros(biases.shape, jnp.float32)
    loss_total = jnp.zeros((), jnp.float32)
    for which_batch in range(frames.shape[0]):
        gathered = collect(low_shards)
        kernels, linear, matrices, option_table, head_table = gathered
        frame_block = frames[which_batch]
        frame_count = frame_block.shape[0]

        def run_encoder():
            return encode(frame_block, kernels, linear, bias_enc)

        def skip_encoder():
            return encoder_blank(frame_count, frame_block.shape[1])

        encoded = lax.cond(section_id == 0, run_encoder, skip_encoder)
        arrived = shifted(encoded[0], "section", 1)

        def run_planner():

            def local_loss(states, matrix_all, table_all, head_all, bias_value):
                return (
                    plan_loss(
                        states,
                        matrix_all,
                        table_all,
                        head_all,
                        bias_value,
                        options[which_batch],
                        legal[which_batch],
                        games[which_batch],
                        valid[which_batch],
                        rewards[which_batch],
                        returns[which_batch],
                    )
                    * inverse_count
                )

            loss_part, pullback = jax.vjp(
                local_loss,
                arrived.astype(jnp.float32),
                matrices.astype(jnp.float32),
                option_table.astype(jnp.float32),
                head_table.astype(jnp.float32),
                value_bias,
            )
            pulled = pullback(jnp.ones((), jnp.float32))
            return (
                loss_part,
                pulled[1],
                pulled[2],
                pulled[3],
                pulled[4],
                pulled[0].astype(jnp.bfloat16),
            )

        def skip_planner():
            return (
                jnp.zeros((), jnp.float32),
                jnp.zeros(matrices.shape, jnp.float32),
                jnp.zeros(option_table.shape, jnp.float32),
                jnp.zeros(head_table.shape, jnp.float32),
                jnp.zeros(value_bias.shape, jnp.float32),
                jnp.zeros((frame_count, D), jnp.bfloat16),
            )

        planned = lax.cond(section_id == 1, run_planner, skip_planner)
        returned = shifted(planned[5], "section", -1)

        def run_back():
            return encode_back(frame_block, kernels, linear, encoded[1:], returned)

        def skip_back():
            return (
                jnp.zeros(kernels.shape, jnp.float32),
                jnp.zeros(linear.shape, jnp.float32),
                jnp.zeros(bias_enc.shape, jnp.float32),
            )

        backed = lax.cond(section_id == 0, run_back, skip_back)
        gradients = (backed[0], backed[1], planned[1], planned[2], planned[3])
        term = spread(gradients)
        grad_total = (
            term
            if grad_total is None
            else tuple((left_part + right_part for left_part, right_part in zip(grad_total, term)))
        )
        bias_total = bias_total + jnp.concatenate([backed[2], planned[4]])
        loss_total = loss_total + planned[0]
    summed = lax.psum(
        (grad_total[0], grad_total[1], grad_total[2], grad_total[3], grad_total[4]), "section"
    )
    bias_raw, loss_value = lax.psum((bias_total, loss_total), ("section", "dp"))
    g_conv, g_lin, g_mats, g_emb, g_heads = summed
    partial_squares = (
        jnp.sum(g_conv * g_conv)
        + jnp.sum(g_lin * g_lin)
        + jnp.sum(g_mats * g_mats)
        + jnp.sum(g_emb * g_emb)
        + jnp.sum(g_heads * g_heads)
    )
    reduced = lax.psum(
        (partial_squares, jnp.sum(g_lin * g_lin, axis=1), jnp.sum(g_mats * g_mats, axis=2)), "dp"
    )
    grad_norm = jnp.sqrt(reduced[0] + jnp.sum(bias_raw * bias_raw))
    factor = jnp.minimum(1.0, CLIP_LIMIT / grad_norm)
    conv_grad = factor * g_conv
    lin_grad = factor * g_lin
    mats_grad = factor * g_mats
    emb_grad = factor * g_emb
    heads_grad = factor * g_heads
    bias_grad = factor * bias_raw
    conv_new, conv_moment_new = unfactored(
        conv_kernels, conv_grad, conv_moment, relative(totals[1], KERN * (C1 + C2))
    )
    emb_new, emb_moment_new = unfactored(
        option_emb, emb_grad, emb_moment, relative(totals[4], OPTS * D)
    )
    heads_new, head_moment_new = unfactored(
        heads, heads_grad, head_moment, relative(totals[5], 3 * GAMES * D)
    )
    bias_new, bias_moment_new = unfactored(
        biases, bias_grad, bias_moment, relative(jnp.sum(biases * biases), BIAS)
    )
    lin_rows_new = DECAY_RATE * lin_rows + (1.0 - DECAY_RATE) * (
        factor * factor * reduced[1] / D + FLOOR_ONE
    )
    lin_cols_new = DECAY_RATE * lin_cols + (1.0 - DECAY_RATE) * jnp.mean(
        lin_grad * lin_grad + FLOOR_ONE, axis=0
    )
    lin_second = lin_rows_new[:, None] * lin_cols_new[None, :] / jnp.mean(lin_rows_new)
    lin_new = enc_linear - STEP_RATE * relative(totals[2], FEAT * D) * lin_grad * lax.rsqrt(
        lin_second
    )
    mats_rows_new = DECAY_RATE * mats_rows + (1.0 - DECAY_RATE) * (
        factor * factor * reduced[2] / D + FLOOR_ONE
    )
    mats_cols_new = DECAY_RATE * mats_cols + (1.0 - DECAY_RATE) * jnp.mean(
        mats_grad * mats_grad + FLOOR_ONE, axis=1
    )
    mats_second = (
        mats_rows_new[:, :, None]
        * mats_cols_new[:, None, :]
        / jnp.mean(mats_rows_new, axis=1)[:, None, None]
    )
    mats_new = plan_mats - STEP_RATE * relative(totals[3], 3 * D * D) * mats_grad * lax.rsqrt(
        mats_second
    )
    return (
        conv_new,
        conv_grad,
        conv_moment_new,
        lin_new,
        lin_grad,
        lin_rows_new,
        lin_cols_new,
        mats_new,
        mats_grad,
        mats_rows_new,
        mats_cols_new,
        emb_new,
        emb_grad,
        emb_moment_new,
        heads_new,
        heads_grad,
        head_moment_new,
        bias_new,
        bias_grad,
        bias_moment_new,
        grad_norm,
        loss_value,
        conv_new.astype(jnp.bfloat16),
        lin_new.astype(jnp.bfloat16),
    )


def solution(mesh):
    return jax.shard_map(
        per_device,
        mesh=mesh,
        in_specs=(
            P(None, "dp", None, None),
            P(None, "dp", None),
            P(None, "dp", None),
            P(None, "dp"),
            P(None, "dp", None),
            P(None, "dp", None),
            P(None, "dp", None),
            P("dp", None),
            P(None, "dp"),
            P(None, None, "dp"),
            P(None, "dp"),
            P(None, None, "dp"),
            P(),
            P("dp", None),
            P(),
            P("dp"),
            P(),
            P(None, "dp"),
            P(None, "dp"),
            P(None, None, "dp"),
            P(),
        ),
        out_specs=(
            P("dp", None),
            P("dp", None),
            P("dp", None),
            P(None, "dp"),
            P(None, "dp"),
            P(),
            P("dp"),
            P(None, None, "dp"),
            P(None, None, "dp"),
            P(),
            P(None, "dp"),
            P(None, "dp"),
            P(None, "dp"),
            P(None, "dp"),
            P(None, None, "dp"),
            P(None, None, "dp"),
            P(None, None, "dp"),
            P(),
            P(),
            P(),
            P(),
            P(),
            P("dp", None),
            P(None, "dp"),
        ),
        check_vma=False,
    )
```

profile of v0, /device:TPU:0, one launch (start us, length us, event | category | flops | bytes accessed | tf_op | source)
XLA Modules:
  0.0 2170.1 jit_solution(4522365950694477139)
XLA Ops:
  21.8 45.0 %all_gather.21 = bf16[256,48]{1,0:T(8,128)(2,1)} all-gather(bf16[16,48]{1,0:T(8,128)(2,1)S(1)} %get-tuple-element.751), channel_id=1, replica_groups=mesh['section'=2,'dp'=16] {'dp'}, dimensions={0}, use_global_device_ids=true | all-gather | bytes 26112 | tf_op jit(solution)/shard_map/all_gather | solution.py:242
  68.0 39.5 %all_gather.22 = bf16[2592,128]{0,1:T(8,128)(2,1)S(1)} all-gather(bf16[2592,8]{0,1:T(8,128)(2,1)S(1)} %get-tuple-element.745), channel_id=1, replica_groups=mesh['section'=2,'dp'=16] {'dp'}, dimensions={1}, use_global_device_ids=true | all-gather | bytes 705024 | tf_op jit(solution)/shard_map/all_gather | solution.py:243
  107.5 343.3 %conditional.6 = (bf16[64,128]{1,0:T(8,128)(2,1)}, f32[25600,16]{0,1:T(8,128)S(1)}, bf16[64,20,320]{2,1,0:T(8,128)(2,1)S(1)}, f32[5184,32]{0,1:T(8,128)}, bf16[64,2592]{1,0:T(8,128)(2,1)}) conditional(s32[]{:T(128)} %convert_element_type.302, () %tuple.73, (bf16[1,64,84,336]{1,3,2,0:T(8,128)(2,1)}, bf16[256,48]{1,0:T(8,128)(2,1)}, f32[176]{0:T(256)}, ...), branch_computations={%region_2.0_spmd, %region_3.0_spmd} | conditional | flops 356347904 | bytes 164964480 | solution.py:329
  144.7 93.6 %copy.351 = bf16[64,20,20,2,4,2,16]{2,1,0,6,5,4,3:T(8,128)(2,1)} copy(bf16[64,20,20,2,4,2,16]{0,6,2,4,1,3,5:T(8,128)(2,1)} %maximum_bitcast_fusion) | data formatting | bytes 26214400 | tf_op jit(solution)/shard_map/cond/branch_1_fun/transpose | solution.py:156
  238.3 92.7 %reshape.327 = bf16[25600,256]{0,1:T(8,128)(2,1)} reshape(bf16[64,20,20,2,4,2,16]{2,1,0,6,5,4,3:T(8,128)(2,1)} %copy.351) | data formatting | bytes 26214400 | tf_op jit(solution)/shard_map/cond/branch_1_fun/reshape | solution.py:156
  381.6 23.6 %copy.357 = bf16[64,9,9,2,2,2,32]{6,5,4,3,2,1,0:T(2,128)(2,1)} copy(bf16[64,9,9,2,2,2,32]{0,6,5,2,4,3,1:T(8,128)(2,1)} %maximum_bitcast_fusion.1) | data formatting | bytes 5308416 | tf_op jit(solution)/shard_map/cond/branch_1_fun/transpose | solution.py:156
  405.2 27.0 %reshape.329 = bf16[5184,256]{1,0:T(8,128)(2,1)} reshape(bf16[64,9,9,2,2,2,32]{6,5,4,3,2,1,0:T(2,128)(2,1)} %copy.357) | data formatting | bytes 5308416 | tf_op jit(solution)/shard_map/cond/branch_1_fun/reshape | solution.py:156
  460.2 343.1 %conditional.9 = (bf16[64,128]{1,0:T(8,128)(2,1)}, f32[25600,16]{0,1:T(8,128)S(1)}, bf16[64,20,320]{2,1,0:T(8,128)(2,1)S(1)}, f32[5184,32]{0,1:T(8,128)}, bf16[64,2592]{1,0:T(8,128)(2,1)}) conditional(s32[]{:T(128)} %convert_element_type.302, () %tuple.79, (bf16[1,64,84,336]{1,3,2,0:T(8,128)(2,1)}, bf16[256,48]{1,0:T(8,128)(2,1)}, f32[176]{0:T(256)}, ...), branch_computations={%region_40.41_spmd, %region_41.42_spmd} | conditional | flops 356347904 | bytes 164964480 | solution.py:329
  497.5 93.6 %copy.384 = bf16[64,20,20,2,4,2,16]{2,1,0,6,5,4,3:T(8,128)(2,1)} copy(bf16[64,20,20,2,4,2,16]{0,6,2,4,1,3,5:T(8,128)(2,1)} %maximum_bitcast_fusion.4) | data formatting | bytes 26214400 | tf_op jit(solution)/shard_map/cond/branch_1_fun/transpose | solution.py:156
  591.0 92.7 %reshape.341 = bf16[25600,256]{0,1:T(8,128)(2,1)} reshape(bf16[64,20,20,2,4,2,16]{2,1,0,6,5,4,3:T(8,128)(2,1)} %copy.384) | data formatting | bytes 26214400 | tf_op jit(solution)/shard_map/cond/branch_1_fun/reshape | solution.py:156
  734.2 23.6 %copy.390 = bf16[64,9,9,2,2,2,32]{6,5,4,3,2,1,0:T(2,128)(2,1)} copy(bf16[64,9,9,2,2,2,32]{0,6,5,2,4,3,1:T(8,128)(2,1)} %maximum_bitcast_fusion.5) | data formatting | bytes 5308416 | tf_op jit(solution)/shard_map/cond/branch_1_fun/transpose | solution.py:156
  757.8 27.0 %reshape.343 = bf16[5184,256]{1,0:T(8,128)(2,1)} reshape(bf16[64,9,9,2,2,2,32]{6,5,4,3,2,1,0:T(2,128)(2,1)} %copy.390) | data formatting | bytes 5308416 | tf_op jit(solution)/shard_map/cond/branch_1_fun/reshape | solution.py:156
  808.2 40.2 %all_gather.20 = bf16[3,128,128]{1,2,0:T(8,128)(2,1)} all-gather(bf16[3,128,8]{1,2,0:T(8,128)(2,1)S(1)} %get-tuple-element.749), channel_id=1, replica_groups=mesh['section'=2,'dp'=16] {'dp'}, dimensions={2}, use_global_device_ids=true | all-gather | bytes 104448 | tf_op jit(solution)/shard_map/all_gather | solution.py:244
  848.4 37.2 %psum.113 = f32[]{:T(128)} all-reduce(f32[]{:T(128)} %convert_reduce_fusion.18), channel_id=1, replica_groups=mesh['section'=2,'dp'=16] {'dp'}, use_global_device_ids=true, to_apply=%region_5.0 | all-reduce | flops 1 | bytes 8 | tf_op jit(solution)/shard_map/psum | solution.py:292
  888.3 37.8 %all_gather.23 = bf16[18,128]{0,1:T(8,128)(2,1)S(1)} all-gather(bf16[18,8]{0,1:T(8,128)(2,1)} %get-tuple-element.753), channel_id=1, replica_groups=mesh['section'=2,'dp'=16] {'dp'}, dimensions={1}, use_global_device_ids=true | all-gather | bytes 4896 | tf_op jit(solution)/shard_map/all_gather | solution.py:245
  926.1 38.8 %all_gather.24 = bf16[3,8,128]{1,0,2:T(4,128)(2,1)} all-gather(bf16[3,8,8]{1,0,2:T(4,128)(2,1)} %copy.419), channel_id=1, replica_groups=mesh['section'=2,'dp'=16] {'dp'}, dimensions={2}, use_global_device_ids=true | all-gather | bytes 6528 | tf_op jit(solution)/shard_map/all_gather | solution.py:246
  973.8 403.8 %conditional.8 = (f32[256,48]{0,1:T(8,128)S(1)}, f32[2592,128]{1,0:T(8,128)S(1)}, f32[176]{0:T(256)S(1)}) conditional(s32[]{:T(128)} %convert_element_type.302, () %tuple.71, (bf16[1,64,84,336]{1,3,2,0:T(8,128)(2,1)}, bf16[64,128]{1,0:T(8,128)(2,1)S(1)}, bf16[2592,128]{0,1:T(8,128)(2,1)S(1)}, f32[5184,32]{0,1:T(8,128)}, ...), branch_computations={%region_34.35_spmd, %region_35.39_spmd} | conditional | flops 487868576 | bytes 240462720 | solution.py:393
  988.0 23.6 %copy.383 = bf16[64,9,9,2,2,2,32]{6,5,4,3,2,1,0:T(2,128)(2,1)} copy(bf16[64,9,9,2,2,2,32]{0,6,2,4,1,3,5:T(8,128)(2,1)} %maximum_bitcast_fusion.3) | data formatting | bytes 5308416 | tf_op jit(solution)/shard_map/cond/branch_1_fun/transpose | solution.py:156
  1011.6 27.0 %reshape.340 = bf16[5184,256]{1,0:T(8,128)(2,1)} reshape(bf16[64,9,9,2,2,2,32]{6,5,4,3,2,1,0:T(2,128)(2,1)} %copy.383) | data formatting | bytes 5308416 | tf_op jit(solution)/shard_map/cond/branch_1_fun/reshape | solution.py:156
  1084.1 93.7 %copy.378 = bf16[64,20,20,2,4,2,16]{2,1,0,6,5,4,3:T(8,128)(2,1)} copy(bf16[64,20,20,2,4,2,16]{0,6,2,4,1,3,5:T(8,128)(2,1)} %maximum_bitcast_fusion.2) | data formatting | bytes 26214400 | tf_op jit(solution)/shard_map/cond/branch_1_fun/transpose | solution.py:156
  1177.9 92.7 %reshape.335 = bf16[25600,256]{0,1:T(8,128)(2,1)} reshape(bf16[64,20,20,2,4,2,16]{2,1,0,6,5,4,3:T(8,128)(2,1)} %copy.378) | data formatting | bytes 26214400 | tf_op jit(solution)/shard_map/cond/branch_1_fun/reshape | solution.py:156
  1295.9 23.6 %fusion.261 = (f32[64,9,1,2,9,1,32]{6,5,3,2,4,1,0:T(1,128)S(1)}, f32[64,9,1,2,9,1,32]{6,5,3,2,4,1,0:T(1,128)S(1)}, f32[64,9,1,2,9,1,32]{6,5,3,2,4,1,0:T(1,128)S(1)}, f32[64,9,1,2,9,1,32]{6,5,3,2,4,1,0:T(1,128)S(1)}) fusion(f32[64,9,2,2,9,2,32]{6,5,3,2,4,1,0:T(2,128)} %bitcast.670), kind=kLoop, calls=%fused_computation.585 | loop fusion | bytes 10616832 | tf_op jit(solution)/shard_map/cond/branch_1_fun/slice | solution.py:170
  1378.7 401.1 %conditional.11 = (f32[256,48]{0,1:T(8,128)S(1)}, f32[2592,128]{1,0:T(8,128)}, f32[176]{0:T(256)}) conditional(s32[]{:T(128)} %convert_element_type.302, () %tuple.77, (bf16[1,64,84,336]{1,3,2,0:T(8,128)(2,1)}, bf16[64,128]{1,0:T(8,128)(2,1)}, bf16[2592,128]{0,1:T(8,128)(2,1)}, f32[5184,32]{0,1:T(8,128)}, bf16[256,48]{1,0:T(8,128)(2,1)}, ...), branch_computations={%region_70.71_spmd, %region_71.75_spmd} | conditional | flops 487868576 | bytes 242985824 | solution.py:393
  1387.1 23.6 %copy.416 = bf16[64,9,9,2,2,2,32]{6,5,4,3,2,1,0:T(2,128)(2,1)} copy(bf16[64,9,9,2,2,2,32]{0,6,2,4,1,3,5:T(8,128)(2,1)} %maximum_bitcast_fusion.7) | data formatting | bytes 5308416 | tf_op jit(solution)/shard_map/cond/branch_1_fun/transpose | solution.py:156
  1410.7 27.1 %reshape.354 = bf16[5184,256]{1,0:T(8,128)(2,1)} reshape(bf16[64,9,9,2,2,2,32]{6,5,4,3,2,1,0:T(2,128)(2,1)} %copy.416) | data formatting | bytes 5308416 | tf_op jit(solution)/shard_map/cond/branch_1_fun/reshape | solution.py:156
  1484.0 93.7 %copy.411 = bf16[64,20,20,2,4,2,16]{2,1,0,6,5,4,3:T(8,128)(2,1)} copy(bf16[64,20,20,2,4,2,16]{0,6,2,4,1,3,5:T(8,128)(2,1)} %maximum_bitcast_fusion.6) | data formatting | bytes 26214400 | tf_op jit(solution)/shard_map/cond/branch_1_fun/transpose | solution.py:156
  1577.8 92.7 %reshape.349 = bf16[25600,256]{0,1:T(8,128)(2,1)} reshape(bf16[64,20,20,2,4,2,16]{2,1,0,6,5,4,3:T(8,128)(2,1)} %copy.411) | data formatting | bytes 26214400 | tf_op jit(solution)/shard_map/cond/branch_1_fun/reshape | solution.py:156
  1791.2 74.4 %all-reduce.25 = (f32[18,128]{0,1:T(8,128)S(1)}, f32[3,8,128]{2,1,0:T(8,128)S(1)}) all-reduce(f32[18,128]{0,1:T(8,128)S(1)} %copy.447, f32[3,8,128]{2,1,0:T(8,128)S(1)} %add.565), channel_id=10, replica_groups=mesh['section'=2,'dp'=16] {'dp'}, use_global_device_ids=true, to_apply=%region_86.87.clone | all-reduce | flops 5376 | bytes 43008
  1866.5 37.0 %all-reduce.23 = (f32[304]{0:T(512)S(1)}, f32[]{:T(128)}) all-reduce(f32[304]{0:T(512)S(1)} %maximum_add_fusion, f32[]{:T(128)S(6)} %add.546), channel_id=1, replica_groups=mesh['section'=2,'dp'=16] {'section','dp'}, use_global_device_ids=true, to_apply=%region_95.96 | all-reduce | flops 305 | bytes 2440 | tf_op jit(solution)/shard_map/psum | solution.py:406
  1904.8 25.4 %reduce-scatter.6.cloned.1.call-done = f32[3,128,8]{1,2,0:T(8,128)} async-done(((f32[3,128,128]{1,2,0:T(8,128)}), f32[3,128,8]{1,2,0:T(8,128)}) %reduce-scatter.6.cloned.1.call-update) | async-done | bytes 12304 | tf_op jit(solution)/shard_map/reduce_scatter | solution.py:254
  1936.2 111.1 %all-reduce.32.cloned.1.call-done = f32[2592,128]{0,1:T(8,128)} async-done(((f32[2592,128]{0,1:T(8,128)}), f32[2592,128]{0,1:T(8,128)}) %all-reduce.32.cloned.1.call-update) | async-done | bytes 1327120
  2071.6 77.1 %all-reduce.24 = (f32[]{:T(128)}, f32[]{:T(128)}, f32[2592]{0:T(1024)S(1)}, f32[]{:T(128)}, f32[3,128]{1,0:T(4,128)S(1)}, /*index=5*/f32[]{:T(128)}, f32[]{:T(128)}, f32[]{:T(128)}) all-reduce(f32[]{:T(128)S(6)} %add.519, f32[]{:T(128)} %get-tuple-element.750, ...), channel_id=1, replica_groups=mesh['section'=2,'dp'=16] {'dp'}, use_global_device_ids=true, to_apply=%region_94.95 | all-reduce | flops 2982 | bytes 23856 | tf_op jit(solution)/shard_map/psum | solution.py:415
  (291 shorter events, 605.9 us)
Async XLA Ops:
  7.2 1896.8 %reduce-scatter.8.cloned.1.call-start = ((), (), s32[]{:S(2)}) async-start(), calls=%async_computation.4 | async-start | bytes 139264
  107.5 866.3 %copy-start.4 = (bf16[2592,128]{0,1:T(8,128)(2,1)}, bf16[2592,128]{0,1:T(8,128)(2,1)S(1)}, u32[]{:S(2)}) copy-start(bf16[2592,128]{0,1:T(8,128)(2,1)S(1)} %all_gather.22) | copy-start | bytes 1990660
  238.3 92.7 %copy-start.21 = (bf16[256,48]{1,0:T(8,128)(2,1)S(1)}, bf16[256,48]{1,0:T(8,128)(2,1)}, u32[]{:S(2)}) copy-start(bf16[256,48]{1,0:T(8,128)(2,1)} %get-tuple-element.97) | copy-start | bytes 73732 | tf_op jit(solution)/shard_map/cond
  450.8 514.0 %collective-permute-start = (bf16[64,128]{1,0:T(8,128)(2,1)}, bf16[64,128]{1,0:T(8,128)(2,1)S(1)}, u32[]{:S(2)}, u32[]{:S(2)}) collective-permute-start(bf16[64,128]{1,0:T(8,128)(2,1)} %get-tuple-element.196), channel_id=1, source_target_pairs={{0,16},{1,17},{2,18},{3,19},{4,20},{5,21},{6,22},{7,23},{8,24},{9,... | collective-permute-start | bytes 49160 | tf_op jit(solution)/shard_map/ppermute | solution.py:26
  460.2 345.0 %copy-start.68 = (f32[3,128,8]{1,2,0:T(8,128)S(1)}, f32[3,128,8]{1,2,0:T(8,128)}, u32[]{:S(2)}) copy-start(f32[3,128,8]{1,2,0:T(8,128)} %param.42) | copy-start | bytes 36868
  460.2 345.6 %copy-start.89 = (f32[18,8]{0,1:T(8,128)S(1)}, f32[18,8]{0,1:T(8,128)}, u32[]{:S(2)}) copy-start(f32[18,8]{0,1:T(8,128)} %param.43) | copy-start | bytes 1732
  460.2 346.8 %copy-start.66 = (f32[3,8,8]{2,1,0:T(8,128)S(1)}, f32[3,8,8]{2,1,0:T(8,128)}, u32[]{:S(2)}) copy-start(f32[3,8,8]{2,1,0:T(8,128)} %param.44) | copy-start | bytes 2308
  460.2 347.4 %copy-start.88 = (s32[2,64,3]{1,0,2:T(2,128)S(1)}, s32[2,64,3]{1,0,2:T(2,128)}, u32[]{:S(2)}) copy-start(s32[2,64,3]{1,0,2:T(2,128)} %param.37) | copy-start | bytes 4612
  591.0 92.7 %copy-start.22 = (bf16[256,48]{1,0:T(8,128)(2,1)S(1)}, bf16[256,48]{1,0:T(8,128)(2,1)}, u32[]{:S(2)}) copy-start(bf16[256,48]{1,0:T(8,128)(2,1)} %get-tuple-element.121) | copy-start | bytes 73732 | tf_op jit(solution)/shard_map/cond
  803.3 161.6 %copy-start.8 = (f32[25600,16]{0,1:T(8,128)}, f32[25600,16]{0,1:T(8,128)S(1)}, u32[]{:S(2)}) copy-start(f32[25600,16]{0,1:T(8,128)S(1)} %get-tuple-element.206) | copy-start | bytes 4915204
  803.3 161.6 %copy-start.13 = (bf16[64,20,320]{2,1,0:T(8,128)(2,1)}, bf16[64,20,320]{2,1,0:T(8,128)(2,1)S(1)}, u32[]{:S(2)}) copy-start(bf16[64,20,320]{2,1,0:T(8,128)(2,1)S(1)} %get-tuple-element.207) | copy-start | bytes 2457604
  803.3 165.9 %collective-permute-start.2 = (bf16[64,128]{1,0:T(8,128)(2,1)}, bf16[64,128]{1,0:T(8,128)(2,1)}, u32[]{:S(2)}, u32[]{:S(2)}) collective-permute-start(bf16[64,128]{1,0:T(8,128)(2,1)} %get-tuple-element.203), channel_id=1, source_target_pairs={{0,16},{1,17},{2,18},{3,19},{4,20},{5,21},{6,22},{7,23},{8,24},{9,... | collective-permute-start | bytes 49160 | tf_op jit(solution)/shard_map/ppermute | solution.py:26
  967.9 5.9 collective-permute-start.1
  972.5 405.1 %collective-permute-start.3 = (bf16[64,128]{1,0:T(8,128)(2,1)}, bf16[64,128]{1,0:T(8,128)(2,1)}, u32[]{:S(2)}, u32[]{:S(2)}) collective-permute-start(bf16[64,128]{1,0:T(8,128)(2,1)} %get-tuple-element.204), channel_id=1, source_target_pairs={{16,0},{17,1},{18,2},{19,3},{20,4},{21,5},{22,6},{23,7},{24,8},{25... | collective-permute-start | bytes 49160 | tf_op jit(solution)/shard_map/ppermute | solution.py:26
  1177.9 92.8 %copy-start.1 = (bf16[5184,32]{1,0:T(8,128)(2,1)S(1)}, bf16[5184,32]{1,0:T(8,128)(2,1)}, u32[]{:S(2)}) copy-start(bf16[5184,32]{1,0:T(8,128)(2,1)} %copy-done) | copy-start | bytes 995332 | tf_op jit(solution)/shard_map/cond
  1177.9 92.8 %copy-start.23 = (bf16[256,48]{1,0:T(8,128)(2,1)S(1)}, bf16[256,48]{1,0:T(8,128)(2,1)}, u32[]{:S(2)}) copy-start(bf16[256,48]{1,0:T(8,128)(2,1)} %get-tuple-element.116) | copy-start | bytes 73732 | tf_op jit(solution)/shard_map/cond
  1577.7 92.8 %copy-start.3 = (bf16[5184,32]{1,0:T(8,128)(2,1)S(1)}, bf16[5184,32]{1,0:T(8,128)(2,1)}, u32[]{:S(2)}) copy-start(bf16[5184,32]{1,0:T(8,128)(2,1)} %copy-done.2) | copy-start | bytes 995332 | tf_op jit(solution)/shard_map/cond
  1577.7 92.8 %copy-start.24 = (bf16[256,48]{1,0:T(8,128)(2,1)S(1)}, bf16[256,48]{1,0:T(8,128)(2,1)}, u32[]{:S(2)}) copy-start(bf16[256,48]{1,0:T(8,128)(2,1)} %get-tuple-element.140) | copy-start | bytes 73732 | tf_op jit(solution)/shard_map/cond
  1779.8 373.8 %copy-start.101 = (f32[3,128]{1,0:T(4,128)S(1)}, f32[3,128]{1,0:T(4,128)}, u32[]{:S(2)}) copy-start(f32[3,128]{1,0:T(4,128)} %param.49) | copy-start | bytes 4612
  1780.7 375.9 %copy-start.94 = (f32[2592]{0:T(1024)S(1)}, f32[2592]{0:T(1024)}, u32[]{:S(2)}) copy-start(f32[2592]{0:T(1024)} %param.47) | copy-start | bytes 31108
  1781.4 377.4 %copy-start.118 = (f32[8]{0:T(128)S(1)}, f32[8]{0:T(128)}, u32[]{:S(2)}) copy-start(f32[8]{0:T(128)} %param.48) | copy-start | bytes 100
  1781.4 377.4 %copy-start.102 = (f32[3,8]{1,0:T(4,128)S(1)}, f32[3,8]{1,0:T(4,128)}, u32[]{:S(2)}) copy-start(f32[3,8]{1,0:T(4,128)} %param.50) | copy-start | bytes 292
  1781.4 377.5 %copy-start.90 = (f32[18,8]{0,1:T(8,128)S(1)}, f32[18,8]{0,1:T(8,128)}, u32[]{:S(2)}) copy-start(f32[18,8]{0,1:T(8,128)} %param.43) | copy-start | bytes 1732
  1781.4 377.5 %copy-start.100 = (f32[18,8]{0,1:T(8,128)S(1)}, f32[18,8]{0,1:T(8,128)}, u32[]{:S(2)}) copy-start(f32[18,8]{0,1:T(8,128)} %param.51) | copy-start | bytes 1732
  1781.4 378.1 %copy-start.67 = (f32[3,8,8]{2,1,0:T(8,128)S(1)}, f32[3,8,8]{2,1,0:T(8,128)}, u32[]{:S(2)}) copy-start(f32[3,8,8]{2,1,0:T(8,128)} %param.44) | copy-start | bytes 2308
  1781.4 378.1 %copy-start.93 = (f32[3,8,8]{2,1,0:T(8,128)S(1)}, f32[3,8,8]{2,1,0:T(8,128)}, u32[]{:S(2)}) copy-start(f32[3,8,8]{2,1,0:T(8,128)} %param.52) | copy-start | bytes 2308
  1781.5 378.7 %copy-start.103 = (f32[304]{0:T(512)S(1)}, f32[304]{0:T(512)}, u32[]{:S(2)}) copy-start(f32[304]{0:T(512)} %param.53) | copy-start | bytes 3652
  1781.5 379.2 %copy-start.28 = (f32[2592,8]{0,1:T(8,128)S(1)}, f32[2592,8]{0,1:T(8,128)}, u32[]{:S(2)}) copy-start(f32[2592,8]{0,1:T(8,128)} %param.41) | copy-start | bytes 248836
  1781.5 148.7 %reduce-scatter.6.cloned.1.call-start = ((), (), s32[]{:S(2)}) async-start(), calls=%async_computation.3 | async-start | bytes 208896 | tf_op jit(solution)/shard_map/reduce_scatter | solution.py:254
  1783.3 378.2 %copy-start.69 = (f32[3,128,8]{1,2,0:T(8,128)S(1)}, f32[3,128,8]{1,2,0:T(8,128)}, u32[]{:S(2)}) copy-start(f32[3,128,8]{1,2,0:T(8,128)} %param.42) | copy-start | bytes 36868
  1783.3 264.0 %all-reduce.32.cloned.1.call-start = ((), (), s32[]{:S(2)}) async-start(), calls=%async_computation.5 | async-start | bytes 2752512
  1786.8 280.0 %all-reduce.30.cloned.1.call-start = ((), (), s32[]{:S(2)}) async-start(), calls=%async_computation.2 | async-start | bytes 172032 | tf_op jit(solution)/shard_map/psum | solution.py:403
  (35 other events, 503.8 us)
Sparse Core Ops, SparseCore 0:
  1781.6 73.4 reduce-scatter.7
  1857.4 72.7 reduce-scatter.5
  1935.7 111.5 all-reduce.31
  2050.1 16.6 all-reduce.29
where the time goes:
time: 2190 us; the launch traced here: 2170 us
  local copies, waits for them, and re-layouts  1270 us (58%)
  blocking collectives  431 us (20%)
  other arithmetic  212 us (10%)
  waiting for transfers between devices  154 us (7%)
  matrix products  62.7 us (3%)
  between operations  26.5 us (1%)
    reshape x8, local copies, waits for them, and re-layouts, patches(): wide.transpose(0, 1, 4, 2, 3, 5, 6)  479 us
    transpose x8, local copies, waits for them, and re-layouts, patches(): wide.transpose(0, 1, 4, 2, 3, 5, 6)  469 us
    unnamed x6, waiting for transfers between devices  111 us
    transpose x8, other arithmetic, patches(): wide.transpose(0, 1, 4, 2, 3, 5, 6)  85.8 us
    psum x1, blocking collectives, per_device(): lax.psum((partial_squares, jnp.sum(g_lin * g_lin, axis=1), jnp.sum(g_mats...  77.1 us
    unnamed x1, blocking collectives  74.4 us
    another operation x12, local copies, waits for them, and re-layouts, patches(): jnp.stack([blocked[:, block_row:block_row + outputs] for block_row in ran...  63.9 us
    another operation x8, other arithmetic, patches(): jnp.stack([tall[:, :, :, :, block_col:block_col + outputs] for block_col...  54 us
  transfers between devices with their start and end apart: 8, of which 3 were waited for; matrix products, arithmetic and copies ran while one was open for 36% of the time, Pallas kernels for 0%

commit v1 on v0

v1 whole, which is shorter than its diff:
```python
import functools

import jax
import jax.numpy as jnp
from jax import lax
from jax.experimental import pallas as pl
from jax.experimental.pallas import tpu as pltpu
from jax.sharding import PartitionSpec as P

D = 128
C1 = 16
C2 = 32
OPTS = 18
KERN = 256
GAMES = 8
FEAT = 2592
BIAS = 304

OUT1 = 20
OUT2 = 9
WIDE = 384
FEATS_ROW = OUT2 * C2

CLIP_LIMIT = 0.05
DECAY_RATE = 0.8
STEP_RATE = 0.5
FLOOR_ONE = 1e-30
FLOOR_TWO = 0.001

HIGH = lax.Precision.HIGHEST
BF = jnp.bfloat16
F32 = jnp.float32


def dot(left, right, over_left=1, over_right=0, precision=None):
    return lax.dot_general(
        left,
        right,
        (((over_left,), (over_right,)), ((), ())),
        precision=precision,
        preferred_element_type=F32,
    )


def sigmoid(value):
    return 0.5 * jnp.tanh(0.5 * value) + 0.5


def slope(value, sigma):
    return sigma * (1.0 + value * (1.0 - sigma))


def iota(shape, axis):
    return lax.broadcasted_iota(jnp.int32, shape, axis)


def turn(value, steps):
    return pltpu.roll(value, steps, 1)


def fold(value, width):
    step = 64
    while step >= width:
        value = value + turn(value, step)
        step //= 2
    return value


def row_of(column):
    square = jnp.broadcast_to(column, (128, 128))
    return jnp.sum(jnp.where(iota((128, 128), 0) == iota((128, 128), 1), square, 0.0), axis=0, keepdims=True)


def load_frames(frames_hbm, section, frame_buf, sems, chunk):
    copies = []
    for which in range(frame_buf.shape[0] // chunk):
        rows = pl.ds(which * chunk, chunk)
        copies.append(
            pltpu.make_async_copy(
                frames_hbm.at[section, rows], frame_buf.at[rows], sems.at[which]
            )
        )
    return copies


def place_frames(frame_buf, pixels, first, chunk, frames):
    for row in range(first, first + chunk):
        block, part = row // 4, row % 4
        pixels[block * frames : (block + 1) * frames, part * WIDE : part * WIDE + 336] = frame_buf[row]


def build_bands(kernels, band_one, band_two):
    rows48 = iota((48, WIDE), 0)
    lanes48 = iota((48, WIDE), 1)
    pick_one = jnp.where((lanes48 % C1 == rows48) & (lanes48 < OUT1 * C1), 1.0, 0.0).astype(BF)
    pick_two = jnp.where(
        (lanes48 % C2 + C1 == rows48) & (lanes48 < OUT2 * C2), 1.0, 0.0
    ).astype(BF)
    wide_one = dot(kernels, pick_one)
    wide_two = dot(kernels, pick_two)
    group = iota((16, WIDE), 1) // C1
    for tap in range(8):
        left = wide_one[tap * 32 : tap * 32 + 16]
        right = wide_one[tap * 32 + 16 : tap * 32 + 32]
        for block in range(24):
            rows = tap * WIDE + block * 16
            if block > OUT1:
                band_one[rows : rows + 16] = jnp.zeros((16, WIDE), BF)
            else:
                band_one[rows : rows + 16] = jnp.where(
                    group == block, left, jnp.where(group == block - 1, right, 0.0)
                ).astype(BF)
    group = iota((32, WIDE), 1) // C2
    for tap in range(4):
        left = wide_two[tap * 64 : tap * 64 + 32]
        right = wide_two[tap * 64 + 32 : tap * 64 + 64]
        for block in range(12):
            rows = tap * WIDE + block * 32
            if block > OUT2:
                band_two[rows : rows + 32] = jnp.zeros((32, WIDE), BF)
            else:
                band_two[rows : rows + 32] = jnp.where(
                    group == block, left, jnp.where(group == block - 1, right, 0.0)
                ).astype(BF)


def wide_biases(bias_row):
    bias8 = jnp.broadcast_to(bias_row, (8, BIAS))
    rows = iota((BIAS, WIDE), 0)
    lanes = iota((BIAS, WIDE), 1)
    one = jnp.where((lanes % C1 == rows) & (lanes < OUT1 * C1), 1.0, 0.0)
    two = jnp.where((lanes % C2 + C1 == rows) & (lanes < OUT2 * C2), 1.0, 0.0)
    rows = iota((D, BIAS), 0)
    lanes = iota((D, BIAS), 1)
    three = jnp.where(lanes == rows + C1 + C2, 1.0, 0.0)
    four = jnp.where(lanes == rows + C1 + C2 + D, 1.0, 0.0)
    return (
        dot(bias8, one, precision=HIGH)[0:1],
        dot(bias8, two, precision=HIGH)[0:1],
        dot(three, bias8, 1, 1, precision=HIGH)[:, 0:1],
        dot(four, bias8, 1, 1, precision=HIGH)[:, 0:1],
    )


def encode_one(pixels, band_one, bias, z_one, act_one, frames, chunk):
    half = 4 * WIDE
    rows = chunk * frames
    for first in range(0, OUT1, chunk):
        low = first * frames
        z = dot(pixels[low : low + rows, :], band_one[0:half, :]) + dot(
            pixels[low + frames : low + frames + rows, :], band_one[half : 2 * half, :]
        )
        z = z + bias
        act = (z * sigmoid(z)).astype(BF)
        for step in range(chunk):
            at, part = divmod(first + step, 2)
            spot = (slice(at * frames, (at + 1) * frames), slice(part * WIDE, (part + 1) * WIDE))
            z_one[spot] = z[step * frames : (step + 1) * frames]
            act_one[spot] = act[step * frames : (step + 1) * frames]


def encode_two(act_one, band_two, bias, z_two, act_two, frames, chunk):
    half = 2 * WIDE
    rows = chunk * frames
    for first in range(0, OUT2, chunk):
        low = first * frames
        z = dot(act_one[low : low + rows, :], band_two[0:half, :]) + dot(
            act_one[low + frames : low + frames + rows, :], band_two[half : 2 * half, :]
        )
        z = z + bias
        z_two[low : low + rows] = z
        act = (z * sigmoid(z)).astype(BF)
        for step in range(chunk):
            at = (first + step) * FEATS_ROW
            act_two[:, at : at + FEATS_ROW] = act[step * frames : (step + 1) * frames, :FEATS_ROW]


def back_two(dstate_t, linear_t, act_two, z_two, dz_two, grad_linear, frames):
    grad_linear(dot(dstate_t, act_two[...]))
    dact = dot(dstate_t, linear_t, 0, 0)
    dz_two[0:frames] = jnp.zeros((frames, WIDE), BF)
    dz_two[(OUT2 + 1) * frames : (OUT2 + 2) * frames] = jnp.zeros((frames, WIDE), BF)
    blank = jnp.zeros((frames, WIDE - FEATS_ROW), F32)
    for at in range(OUT2):
        z = z_two[at * frames : (at + 1) * frames]
        part = jnp.concatenate([dact[:, at * FEATS_ROW : (at + 1) * FEATS_ROW], blank], axis=1)
        dz_two[(at + 1) * frames : (at + 2) * frames] = (part * slope(z, sigmoid(z))).astype(BF)


def back_one(dz_two, band_two, z_one, dz_one, frames, chunk):
    half = 2 * WIDE
    rows = chunk * frames
    for first in range(0, OUT1 // 2, chunk):
        low = first * frames
        dact = dot(dz_two[low + frames : low + frames + rows], band_two[0:half], 1, 1) + dot(
            dz_two[low : low + rows], band_two[half : 2 * half], 1, 1
        )
        z = z_one[low : low + rows]
        dz = (dact * slope(z, sigmoid(z))).astype(BF)
        for step in range(chunk):
            for part in range(2):
                at = (2 * (first + step) + part) * frames
                dz_one[at : at + frames] = dz[
                    step * frames : (step + 1) * frames, part * WIDE : (part + 1) * WIDE
                ]


def band_sums(full, base, outputs, width):
    per_tile = 128 // width
    lane = iota((width, 128), 1) // width
    sums = []
    for shift in range(2):
        total = None
        for spot in range(per_tile):
            part = None
            for position in range(outputs):
                tile, inside = divmod(position + shift, per_tile)
                if inside != spot:
                    continue
                term = full[
                    position * width : (position + 1) * width,
                    base + tile * 128 : base + (tile + 1) * 128,
                ]
                part = term if part is None else part + term
            if part is None:
                continue
            part = jnp.where(lane == spot, part, 0.0)
            total = part if total is None else total + part
        sums.append(fold(total, width))
    return sums


def kernel_grad(full_pairs, outputs, width, taps_per):
    tiles = []
    lane = iota((width, 128), 1) // width
    pieces = []
    for full in full_pairs:
        for tap in range(taps_per):
            pieces.extend(band_sums(full, tap * WIDE, outputs, width))
    per_tile = 128 // width
    for tile in range(2):
        total = jnp.zeros((width, 128), F32)
        for spot in range(per_tile):
            total = jnp.where(lane == spot, pieces[tile * per_tile + spot], total)
        tiles.append(total)
    return jnp.concatenate(tiles, axis=1)


def tiled(tile, count):
    return jnp.concatenate([tile] * count, axis=1)


def twice(row):
    return jnp.concatenate([row, row], axis=1)


def plan(states, mats_t, emb_t, heads_t, bias_col, options, legal, games, valid, rewards, returns):
    frames = states.shape[1]
    pairs = OPTS // 2
    lanes = OPTS * frames
    trans_in, trans_out, value_in = mats_t
    low_half = iota((1, 128), 1) < frames
    upper = iota((1, 128), 1) // frames

    valid_f = [twice(v.astype(F32)) for v in valid]
    rewards = [twice(r) for r in rewards]
    returns = [twice(r) for r in returns]
    chosen = [twice(o) for o in options]
    game = twice(games)

    game_rows = iota((24, WIDE), 0)
    game_pick = jnp.where(
        game_rows == tiled(game, 3) + GAMES * (iota((24, WIDE), 1) // 128), 1.0, 0.0
    ).astype(BF)
    head_rows = dot(heads_t, game_pick)
    hr, hd, hv = (head_rows[:, k * 128 : (k + 1) * 128] for k in range(3))

    option_rows = jnp.where(
        iota((32, lanes), 0) == iota((32, lanes), 1) // frames, 1.0, 0.0
    ).astype(BF)
    s_low = twice(states)
    s_f = s_low.astype(F32)
    base = dot(trans_in, s_low)
    pre = tiled(base, pairs) + dot(emb_t, option_rows)
    sig_h = sigmoid(pre)
    hid = pre * sig_h
    hid_low = hid.astype(BF)
    after = tiled(s_f, pairs) + dot(trans_out, hid_low)
    after_low = after.astype(BF)
    judge_pre = dot(value_in, after_low) + bias_col
    sig_j = sigmoid(judge_pre)
    judged = judge_pre * sig_j

    def tile_of(value, k):
        return value[:, k * 128 : (k + 1) * 128]

    def over(value):
        return jnp.sum(value, axis=0, keepdims=True)

    reward = [over(tile_of(hid, k) * hr) for k in range(pairs)]
    gamma = [sigmoid(over(tile_of(hid, k) * hd)) for k in range(pairs)]
    value = [over(tile_of(judged, k) * hv) for k in range(pairs)]
    backed = [reward[k] + gamma[k] * value[k] for k in range(pairs)]
    allowed = [
        jnp.concatenate([legal[2 * k], legal[2 * k + 1]], axis=1) > 0 for k in range(pairs)
    ]
    highest = functools.reduce(
        jnp.maximum, [jnp.where(allowed[k], backed[k], -1e30) for k in range(pairs)]
    )
    highest = jnp.maximum(highest, turn(highest, frames))
    shares = [
        jnp.where(allowed[k], jnp.exp(jnp.where(allowed[k], backed[k] - highest, -60.0)), 0.0)
        for k in range(pairs)
    ]

    def halves(total):
        return total + turn(total, frames)

    share_sum = halves(sum(shares))
    planned = halves(sum(shares[k] * backed[k] for k in range(pairs))) / share_sum
    choose = [chosen[0] == 2 * k + upper for k in range(pairs)]

    def chosen_of(parts):
        return halves(sum(jnp.where(choose[k], parts[k], 0.0) for k in range(pairs)))

    roll_f = [chosen_of([tile_of(after, k) for k in range(pairs)])]
    roll_low = [roll_f[0].astype(BF)]
    plan_miss = planned - returns[0]
    reward_miss = [chosen_of(reward) - rewards[0]]
    value_miss = [chosen_of(value) - returns[1]]
    steps = len(options)
    picks, pre_k, sig_k, hid_k, hid_k_low, judge_k, sig_jk, judged_k = ([None] for _ in range(8))
    for k in range(1, steps):
        picks.append(jnp.where(iota((32, 128), 0) == chosen[k], 1.0, 0.0).astype(BF))
        pre_k.append(dot(trans_in, roll_low[k - 1]) + dot(emb_t, picks[k]))
        sig_k.append(sigmoid(pre_k[k]))
        hid_k.append(pre_k[k] * sig_k[k])
        hid_k_low.append(hid_k[k].astype(BF))
        roll_f.append(roll_f[k - 1] + dot(trans_out, hid_k_low[k]))
        roll_low.append(roll_f[k].astype(BF))
        judge_k.append(dot(value_in, roll_low[k]) + bias_col)
        sig_jk.append(sigmoid(judge_k[k]))
        judged_k.append(judge_k[k] * sig_jk[k])
        reward_miss.append(over(hid_k[k] * hr) - rewards[k])
        value_miss.append(over(judged_k[k] * hv) - returns[k + 1])
    errors = valid_f[0] * plan_miss * plan_miss
    for k in range(steps):
        errors = errors + valid_f[k] * (
            reward_miss[k] * reward_miss[k] + value_miss[k] * value_miss[k]
        )
    errors = jnp.where(low_half, errors, 0.0)

    half = jnp.where(low_half, 1.0, 0.0)
    d_plan = 2.0 * valid_f[0] * plan_miss / share_sum
    d_reward_k = [2.0 * valid_f[k] * reward_miss[k] for k in range(steps)]
    d_value_k = [2.0 * valid_f[k] * value_miss[k] for k in range(steps)]

    def through(matrix_t, grad):
        return dot(matrix_t, grad, 0, 0)

    d_roll = None
    d_judge_low, d_step_low, d_pre_low = ([None] * steps for _ in range(3))
    d_hr = jnp.zeros((D, 128), F32)
    d_hd = jnp.zeros((D, 128), F32)
    d_hv = jnp.zeros((D, 128), F32)
    for k in range(steps - 1, 0, -1):
        d_judge_low[k] = (d_value_k[k] * hv * slope(judge_k[k], sig_jk[k])).astype(BF)
        term = through(value_in, d_judge_low[k])
        d_roll = term if d_roll is None else d_roll + term
        d_step_low[k] = d_roll.astype(BF)
        d_hid = through(trans_out, d_step_low[k]) + d_reward_k[k] * hr
        d_pre_low[k] = (d_hid * slope(pre_k[k], sig_k[k])).astype(BF)
        d_roll = d_roll + through(trans_in, d_pre_low[k])
        d_hr = d_hr + (half * d_reward_k[k]) * hid_k[k]
        d_hv = d_hv + (half * d_value_k[k]) * judged_k[k]

    d_backed = [d_plan * shares[k] * (1.0 + backed[k] - planned) for k in range(pairs)]
    d_reward = [
        d_backed[k] + jnp.where(choose[k], d_reward_k[0], 0.0) for k in range(pairs)
    ]
    d_value = [
        d_backed[k] * gamma[k] + jnp.where(choose[k], d_value_k[0], 0.0) for k in range(pairs)
    ]
    d_gamma = [d_backed[k] * value[k] * gamma[k] * (1.0 - gamma[k]) for k in range(pairs)]
    d_judge = [
        (d_value[k] * hv * slope(tile_of(judge_pre, k), tile_of(sig_j, k))).astype(BF)
        for k in range(pairs)
    ]
    d_judge_all = jnp.concatenate(d_judge, axis=1)
    d_after = through(value_in, d_judge_all)
    d_after = [
        tile_of(d_after, k) + jnp.where(choose[k], d_roll, 0.0) for k in range(pairs)
    ]
    d_after_low = jnp.concatenate([d.astype(BF) for d in d_after], axis=1)
    d_hid_all = through(trans_out, d_after_low)
    d_pre = [
        (
            (tile_of(d_hid_all, k) + d_reward[k] * hr + d_gamma[k] * hd)
            * slope(tile_of(pre, k), tile_of(sig_h, k))
        ).astype(BF)
        for k in range(pairs)
    ]
    d_pre_all = jnp.concatenate(d_pre, axis=1)
    d_base = through(trans_in, d_pre_all)
    d_state = halves(sum(d_after[k] + tile_of(d_base, k) for k in range(pairs)))
    for k in range(pairs):
        d_hr = d_hr + d_reward[k] * tile_of(hid, k)
        d_hd = d_hd + d_gamma[k] * tile_of(hid, k)
        d_hv = d_hv + d_value[k] * tile_of(judged, k)

    def both(parts):
        joined = [jnp.where(low_half, parts[k].astype(F32), parts[k + 1].astype(F32)) for k in range(1, steps, 2)]
        return [part.astype(BF) for part in joined]

    def with_steps(wide, parts):
        return jnp.concatenate([wide] + both(parts), axis=1)

    before_low = [None] + roll_low[:-1]
    d_pre_cat = with_steps(d_pre_all, d_pre_low)
    d_judge_cat = with_steps(d_judge_all, d_judge_low)
    grad_in = dot(d_pre_cat, with_steps(tiled(s_low, pairs), before_low), 1, 1)
    grad_out = dot(
        with_steps(d_after_low, d_step_low), with_steps(hid_low, hid_k_low), 1, 1
    )
    grad_value = dot(d_judge_cat, with_steps(after_low, roll_low), 1, 1)
    grad_emb = dot(d_pre_cat, with_steps(option_rows, picks), 1, 1)
    grad_heads = dot(
        jnp.concatenate([d_hr, d_hd, d_hv], axis=1), game_pick.astype(F32), 1, 1, precision=HIGH
    )
    grad_bias = jnp.sum(d_judge_cat.astype(F32), axis=1, keepdims=True)
    return (
        d_state[:, :frames],
        (grad_in, grad_out, grad_value),
        grad_emb,
        grad_heads,
        grad_bias,
        errors,
    )


def local_kernel(
    frames_hbm,
    kernels_ref,
    linear_ref,
    mats_ref,
    emb_ref,
    heads_ref,
    bias_ref,
    options_ref,
    legal_ref,
    games_ref,
    valid_ref,
    rewards_ref,
    returns_ref,
    lin_out,
    mats_out,
    emb_out,
    heads_out,
    conv_out,
    small_out,
    frame_buf,
    pixels,
    band_one,
    band_two,
    z_one,
    act_one,
    z_two,
    act_two,
    dz_two,
    dz_one,
    sems,
):
    section = lax.axis_index("section")
    frames = frame_buf.shape[1]
    side = frame_buf.shape[0]
    chunk = 12
    copies = load_frames(frames_hbm, section, frame_buf, sems, chunk)
    for copy in copies:
        copy.start()
    build_bands(kernels_ref[...], band_one, band_two)
    bias_one, bias_two, bias_three, bias_four = wide_biases(bias_ref[...])
    tail = jnp.zeros((pixels.shape[0], WIDE - 336), BF)
    for part in range(4):
        pixels[:, part * WIDE + 336 : (part + 1) * WIDE] = tail
    for which, copy in enumerate(copies):
        copy.wait()
        place_frames(frame_buf, pixels, which * chunk, chunk, frames)
    encode_one(pixels, band_one, bias_one, z_one, act_one, frames, 4)
    encode_two(act_one, band_two, bias_two, z_two, act_two, frames, 3)
    linear_t = linear_ref[...]
    states = (dot(linear_t, act_two[...], 1, 1) + bias_three).astype(BF)

    def row(ref, k):
        return ref[k, pl.ds(section, 1), :]

    depth = options_ref.shape[0]
    d_state, grad_mats, grad_emb, grad_heads, grad_bias, errors = plan(
        states,
        tuple(mats_ref[k] for k in range(3)),
        emb_ref[:, 0:32],
        heads_ref[:, 0:24],
        bias_four,
        [row(options_ref, k) for k in range(depth)],
        [row(legal_ref, k) for k in range(OPTS)],
        games_ref[pl.ds(section, 1), :],
        [row(valid_ref, k) for k in range(depth)],
        [row(rewards_ref, k) for k in range(depth)],
        [returns_ref[section, k : k + 1, :] for k in range(depth + 1)],
    )
    for k in range(3):
        mats_out[k] = grad_mats[k]
    emb_out[...] = jnp.concatenate([grad_emb, jnp.zeros((D, 96), F32)], axis=1)
    heads_out[...] = jnp.concatenate([grad_heads, jnp.zeros((D, 104), F32)], axis=1)
    d_state_low = d_state.astype(BF)
    grad_three = jnp.sum(d_state_low.astype(F32), axis=1, keepdims=True)

    def keep_linear(grad):
        lin_out[...] = grad

    back_two(d_state_low, linear_t, act_two, z_two, dz_two, keep_linear, frames)
    d_two = dz_two[frames : (OUT2 + 1) * frames]
    rows_two = OUT2 * frames
    grad_two = kernel_grad(
        [
            dot(d_two, act_one[0:rows_two], 0, 0),
            dot(d_two, act_one[frames : frames + rows_two], 0, 0),
        ],
        OUT2,
        C2,
        2,
    )
    bias_two_grad = fold(tiles_sum(dot(jnp.ones((8, rows_two), BF), d_two)), C2)
    back_one(dz_two, band_two, z_one, dz_one, frames, 5)
    d_one = dz_one[...]
    rows_one = OUT1 * frames
    grad_one = kernel_grad(
        [
            dot(d_one, pixels[0:rows_one], 0, 0),
            dot(d_one, pixels[frames : frames + rows_one], 0, 0),
        ],
        OUT1,
        C1,
        4,
    )
    bias_one_grad = fold(tiles_sum(dot(jnp.ones((8, rows_one), BF), d_one)), C1)
    conv_t = jnp.concatenate(
        [grad_one, grad_two, jnp.zeros((128 - C1 - C2, KERN), F32)], axis=0
    )
    conv_out[...] = conv_t.T
    lane = iota((8, 128), 1)
    line = iota((8, 128), 0)
    row_zero = jnp.where(
        lane < C1, bias_one_grad, jnp.where(lane < C1 + C2, turn(bias_two_grad, C1), 0.0)
    )
    count = sum(row(valid_ref, k).astype(F32) for k in range(depth))
    count = jnp.where(iota((1, 128), 1) < frames, twice(count), 0.0)
    small = jnp.where(line == 0, row_zero, 0.0)
    small = jnp.where(line == 1, row_of(grad_three), small)
    small = jnp.where(line == 2, row_of(grad_bias), small)
    small = jnp.where(line == 3, errors, small)
    small = jnp.where(line == 4, count, small)
    small_out[...] = small


def tiles_sum(value):
    return sum(value[:, k * 128 : (k + 1) * 128] for k in range(value.shape[1] // 128))


VMEM_SPEC = pl.BlockSpec(memory_space=pltpu.VMEM)
ANY_SPEC = pl.BlockSpec(memory_space=pl.ANY)


def local_scratch(frames, side):
    return [
        pltpu.VMEM((side, frames, 336), BF),
        pltpu.VMEM(((OUT1 + 1) * frames, 4 * WIDE), BF),
        pltpu.VMEM((8 * WIDE, WIDE), BF),
        pltpu.VMEM((4 * WIDE, WIDE), BF),
        pltpu.VMEM((OUT1 // 2 * frames, 2 * WIDE), F32),
        pltpu.VMEM((OUT1 // 2 * frames, 2 * WIDE), BF),
        pltpu.VMEM((OUT2 * frames, WIDE), F32),
        pltpu.VMEM((frames, FEAT), BF),
        pltpu.VMEM(((OUT2 + 2) * frames, WIDE), BF),
        pltpu.VMEM((OUT1 * frames, WIDE), BF),
        pltpu.SemaphoreType.DMA((side // 12,)),
    ]


def local_step(frames, kernels, linear_t, mats_t, emb_t, heads_t, biases, options, legal, games, valid, rewards, returns):
    count = frames.shape[1]
    side = frames.shape[2]
    shapes = [(D, FEAT), (3, D, D), (D, 128), (D, 128), (KERN, 128), (8, 128)]
    return pl.pallas_call(
        local_kernel,
        out_shape=[jax.ShapeDtypeStruct(shape, F32) for shape in shapes],
        in_specs=[ANY_SPEC] + [VMEM_SPEC] * 12,
        out_specs=[VMEM_SPEC] * len(shapes),
        scratch_shapes=local_scratch(count, side),
        compiler_params=pltpu.CompilerParams(vmem_limit_bytes=56 * 1024 * 1024),
    )(
        frames.transpose(0, 2, 1, 3),
        kernels,
        linear_t,
        mats_t,
        emb_t,
        heads_t,
        biases.reshape(1, BIAS),
        options.transpose(2, 0, 1),
        legal.transpose(2, 0, 1),
        games,
        valid.transpose(2, 0, 1),
        rewards.transpose(2, 0, 1),
        returns.transpose(0, 2, 1),
    )


def gather_rows(shard):
    return lax.all_gather(shard, "dp", axis=0, tiled=True)


def relative(square_total, entries):
    return jnp.maximum(FLOOR_TWO, jnp.sqrt(square_total / entries))


def unfactored(weight, grad, moment, scale):
    moment_new = DECAY_RATE * moment + (1.0 - DECAY_RATE) * (grad * grad + FLOOR_ONE)
    return (weight - STEP_RATE * scale * grad * lax.rsqrt(moment_new), moment_new)


def per_device(
    frames,
    options,
    legal,
    games,
    valid,
    rewards,
    returns,
    conv_kernels,
    enc_linear,
    plan_mats,
    option_emb,
    heads,
    biases,
    conv_moment,
    lin_rows,
    lin_cols,
    mats_rows,
    mats_cols,
    emb_moment,
    head_moment,
    bias_moment,
):
    weight_squares = lax.psum(
        (
            jnp.sum(conv_kernels * conv_kernels),
            jnp.sum(enc_linear * enc_linear),
            jnp.sum(plan_mats * plan_mats),
            jnp.sum(option_emb * option_emb),
            jnp.sum(heads * heads),
        ),
        "dp",
    )
    width = enc_linear.shape[1]
    kernels = gather_rows(conv_kernels.astype(BF))
    linear_t = gather_rows(enc_linear.astype(BF).T)
    mats_t = gather_rows(plan_mats.astype(BF).transpose(2, 0, 1)).transpose(1, 0, 2)
    emb_t = gather_rows(option_emb.astype(BF).T)
    heads_t = gather_rows(heads.astype(BF).reshape(3 * GAMES, width).T)
    emb_t = jnp.pad(emb_t, ((0, 0), (0, 128 - OPTS)))
    heads_t = jnp.pad(heads_t, ((0, 0), (0, 128 - 3 * GAMES)))
    lin, mats, emb, hds, conv, small = local_step(
        frames,
        kernels,
        linear_t,
        mats_t,
        emb_t,
        heads_t,
        biases,
        options,
        legal,
        games,
        valid,
        rewards,
        returns,
    )
    rows = jnp.concatenate(
        [lin, mats[0], mats[1], mats[2], emb[:, :OPTS], hds[:, : 3 * GAMES]], axis=1
    )
    rows = lax.psum(lax.psum_scatter(rows, "dp", scatter_dimension=0, tiled=True), "section")
    conv = lax.psum(
        lax.psum_scatter(conv[:, : C1 + C2], "dp", scatter_dimension=0, tiled=True), "section"
    )
    small = lax.psum(small, ("section", "dp"))
    inverse_count = 1.0 / jnp.sum(small[4])
    loss_value = jnp.sum(small[3]) * inverse_count
    bias_raw = (
        jnp.concatenate([small[0, : C1 + C2], small[1], small[2]]) * inverse_count
    )
    rows = rows * inverse_count
    g_conv = conv * inverse_count
    g_lin = rows[:, :FEAT].T
    g_mats = rows[:, FEAT : FEAT + 3 * D].reshape(width, 3, D).transpose(1, 2, 0)
    g_emb = rows[:, FEAT + 3 * D : FEAT + 3 * D + OPTS].T
    g_heads = rows[:, FEAT + 3 * D + OPTS :].T.reshape(3, GAMES, width)
    partial_squares = (
        jnp.sum(g_conv * g_conv)
        + jnp.sum(g_lin * g_lin)
        + jnp.sum(g_mats * g_mats)
        + jnp.sum(g_emb * g_emb)
        + jnp.sum(g_heads * g_heads)
    )
    reduced = lax.psum(
        (partial_squares, jnp.sum(g_lin * g_lin, axis=1), jnp.sum(g_mats * g_mats, axis=2)), "dp"
    )
    grad_norm = jnp.sqrt(reduced[0] + jnp.sum(bias_raw * bias_raw))
    factor = jnp.minimum(1.0, CLIP_LIMIT / grad_norm)
    conv_grad = factor * g_conv
    lin_grad = factor * g_lin
    mats_grad = factor * g_mats
    emb_grad = factor * g_emb
    heads_grad = factor * g_heads
    bias_grad = factor * bias_raw
    conv_new, conv_moment_new = unfactored(
        conv_kernels, conv_grad, conv_moment, relative(weight_squares[0], KERN * (C1 + C2))
    )
    emb_new, emb_moment_new = unfactored(
        option_emb, emb_grad, emb_moment, relative(weight_squares[3], OPTS * D)
    )
    heads_new, head_moment_new = unfactored(
        heads, heads_grad, head_moment, relative(weight_squares[4], 3 * GAMES * D)
    )
    bias_new, bias_moment_new = unfactored(
        biases, bias_grad, bias_moment, relative(jnp.sum(biases * biases), BIAS)
    )
    lin_rows_new = DECAY_RATE * lin_rows + (1.0 - DECAY_RATE) * (
        factor * factor * reduced[1] / D + FLOOR_ONE
    )
    lin_cols_new = DECAY_RATE * lin_cols + (1.0 - DECAY_RATE) * jnp.mean(
        lin_grad * lin_grad + FLOOR_ONE, axis=0
    )
    lin_second = lin_rows_new[:, None] * lin_cols_new[None, :] / jnp.mean(lin_rows_new)
    lin_new = enc_linear - STEP_RATE * relative(weight_squares[1], FEAT * D) * lin_grad * lax.rsqrt(
        lin_second
    )
    mats_rows_new = DECAY_RATE * mats_rows + (1.0 - DECAY_RATE) * (
        factor * factor * reduced[2] / D + FLOOR_ONE
    )
    mats_cols_new = DECAY_RATE * mats_cols + (1.0 - DECAY_RATE) * jnp.mean(
        mats_grad * mats_grad + FLOOR_ONE, axis=1
    )
    mats_second = (
        mats_rows_new[:, :, None]
        * mats_cols_new[:, None, :]
        / jnp.mean(mats_rows_new, axis=1)[:, None, None]
    )
    mats_new = plan_mats - STEP_RATE * relative(weight_squares[2], 3 * D * D) * mats_grad * lax.rsqrt(
        mats_second
    )
    return (
        conv_new,
        conv_grad,
        conv_moment_new,
        lin_new,
        lin_grad,
        lin_rows_new,
        lin_cols_new,
        mats_new,
        mats_grad,
        mats_rows_new,
        mats_cols_new,
        emb_new,
        emb_grad,
        emb_moment_new,
        heads_new,
        heads_grad,
        head_moment_new,
        bias_new,
        bias_grad,
        bias_moment_new,
        grad_norm,
        loss_value,
        conv_new.astype(BF),
        lin_new.astype(BF),
    )


def solution(mesh):
    return jax.shard_map(
        per_device,
        mesh=mesh,
        in_specs=(
            P(None, "dp", None, None),
            P(None, "dp", None),
            P(None, "dp", None),
            P(None, "dp"),
            P(None, "dp", None),
            P(None, "dp", None),
            P(None, "dp", None),
            P("dp", None),
            P(None, "dp"),
            P(None, None, "dp"),
            P(None, "dp"),
            P(None, None, "dp"),
            P(),
            P("dp", None),
            P(),
            P("dp"),
            P(),
            P(None, "dp"),
            P(None, "dp"),
            P(None, None, "dp"),
            P(),
        ),
        out_specs=(
            P("dp", None),
            P("dp", None),
            P("dp", None),
            P(None, "dp"),
            P(None, "dp"),
            P(),
            P("dp"),
            P(None, None, "dp"),
            P(None, None, "dp"),
            P(),
            P(None, "dp"),
            P(None, "dp"),
            P(None, "dp"),
            P(None, "dp"),
            P(None, None, "dp"),
            P(None, None, "dp"),
            P(None, None, "dp"),
            P(),
            P(),
            P(),
            P(),
            P(),
            P("dp", None),
            P(None, "dp"),
        ),
        check_vma=False,
    )
```

time: 2190 us -> 561 us (0.26)
  local copies, waits for them, and re-layouts: 1270 us -> 8.73 us
  other arithmetic: 212 us -> 17.7 us
  blocking collectives: 431 us -> 317 us
  matrix products: 62.7 us -> 0 us
    reshape x20 -> x2, local copies, waits for them, and re-layouts: 597 us -> 1.32 us  [the longest x1 1.24 us: local_step(): biases.reshape(1, BIAS)]
    transpose x8 -> x0, local copies, waits for them, and re-layouts: 469 us -> none  [patches(): wide.transpose(0, 1, 4, 2, 3, 5, 6)]
    reduce_scatter x1 -> x2, waiting for transfers between devices: 25.4 us -> 151 us  [the longest x1 124 us: per_device(): lax.psum_scatter(rows, 'dp', scatter_dimension=0, tiled=True)]
    unnamed x6 -> x3, waiting for transfers between devices: 111 us -> 0.05 us
    another operation x28 -> x0, local copies, waits for them, and re-layouts: 94.2 us -> none  [the longest x12 63.9 us: patches(): jnp.stack([blocked[:, block_row:block_row + outputs] for block_row in ran...]
    transpose x8 -> x0, other arithmetic: 85.8 us -> none  [patches(): wide.transpose(0, 1, 4, 2, 3, 5, 6)]
    unnamed x1 -> x0, blocking collectives: 74.4 us -> none
    dot_general x16 -> x0, matrix products: 62.7 us -> none  [the longest x6 30.9 us: contract_rows(): lax.dot_general(first_arg, second_arg, (((0,), (0,)), ((), ())), preferre...]
  transfers between devices with their start and end apart: 8 -> 3, of which waited for: 3 -> 3; matrix products, arithmetic and copies ran while one was open for 36% -> 1% of each run, Pallas kernels for 0% -> 0%
where the time goes in v1:
time: 561 us; the launch traced here: 560 us
  blocking collectives  317 us (57%)
  waiting for transfers between devices  169 us (30%)
  between operations  27.1 us (5%)
  Pallas kernels  19.5 us (3%)
  other arithmetic  17.7 us (3%)
  local copies, waits for them, and re-layouts  8.73 us (2%)
    all_gather x5, blocking collectives, gather_rows(): return lax.all_gather(shard, 'dp', axis=0, tiled=True)  201 us
    reduce_scatter x1, waiting for transfers between devices, per_device(): lax.psum_scatter(rows, 'dp', scatter_dimension=0, tiled=True)  124 us
    psum x1, blocking collectives, per_device(): lax.psum((partial_squares, jnp.sum(g_lin * g_lin, axis=1), jnp.sum(g_mats...  77 us
    psum x1, blocking collectives, per_device(): small = lax.psum(small, ('section', 'dp'))  37 us
    reduce_scatter x1, waiting for transfers between devices, per_device(): lax.psum_scatter(conv[:, :C1 + C2], 'dp', scatter_dimension=0, tiled=True)  26.7 us
    pallas_call x1, Pallas kernels, local_step(): pl.pallas_call(local_kernel, out_shape=[jax.ShapeDtypeStruct(shape, F32)...  19.5 us
    psum x1, waiting for transfers between devices, per_device(): lax.psum(lax.psum_scatter(rows, 'dp', scatter_dimension=0, tiled=True), '...  18.5 us
  transfers between devices with their start and end apart: 3, of which 3 were waited for; matrix products, arithmetic and copies ran while one was open for 1% of the time, Pallas kernels for 0%

profile of v1, /device:TPU:0, one launch (start us, length us, event | category | flops | bytes accessed | tf_op | source)
XLA Modules:
  0.0 559.6 jit_solution(8044312830308663349)
XLA Ops:
  7.2 1.4 multiply_reduce_fusion.4
  8.6 45.0 %all_gather.15.kernels_ref = bf16[256,48]{1,0:T(8,128)(2,1)} all-gather(bf16[16,48]{1,0:T(8,128)(2,1)S(1)} %get-tuple-element.130), channel_id=1, replica_groups=mesh['section'=2,'dp'=16] {'dp'}, dimensions={0}, use_global_device_ids=true | all-gather | bytes 26112 | tf_op jit(solution)/shard_map/all_gather | solution.py:618
  53.6 1.6 multiply_reduce_fusion
  55.2 41.8 %all_gather.16.linear_ref = bf16[128,2592]{1,0:T(8,128)(2,1)} all-gather(bf16[8,2592]{1,0:T(8,128)(2,1)S(1)} %get-tuple-element.122), channel_id=1, replica_groups=mesh['section'=2,'dp'=16] {'dp'}, dimensions={0}, use_global_device_ids=true | all-gather | bytes 705024 | tf_op jit(solution)/shard_map/all_gather | solution.py:618
  97.0 1.4 multiply_reduce_fusion.2
  98.4 40.6 %all_gather.17 = bf16[128,3,128]{2,0,1:T(8,128)(2,1)} all-gather(bf16[8,3,128]{2,0,1:T(8,128)(2,1)S(1)} %get-tuple-element.128), channel_id=1, replica_groups=mesh['section'=2,'dp'=16] {'dp'}, dimensions={0}, use_global_device_ids=true | all-gather | bytes 104448 | tf_op jit(solution)/shard_map/all_gather | solution.py:618
  139.0 1.4 multiply_reduce_fusion.5
  140.3 35.6 %all_gather.18 = bf16[128,18]{1,0:T(8,128)(2,1)S(1)} all-gather(bf16[8,18]{1,0:T(8,128)(2,1)S(1)} %get-tuple-element.136), channel_id=1, replica_groups=mesh['section'=2,'dp'=16] {'dp'}, dimensions={0}, use_global_device_ids=true | all-gather | bytes 4896 | tf_op jit(solution)/shard_map/all_gather | solution.py:618
  176.0 1.4 multiply_reduce_fusion.1
  177.4 37.6 %all_gather.19 = bf16[128,24]{1,0:T(8,128)(2,1)S(1)} all-gather(bf16[8,24]{1,0:T(8,128)(2,1)S(1)} %bitcast.53), channel_id=1, replica_groups=mesh['section'=2,'dp'=16] {'dp'}, dimensions={0}, use_global_device_ids=true | all-gather | bytes 6528 | tf_op jit(solution)/shard_map/all_gather | solution.py:618
  216.3 1.2 reshape.70.bias_ref
  217.5 19.5 %shard_map.388 = (f32[128,2592]{1,0:T(8,128)}, f32[3,128,128]{2,1,0:T(8,128)}, f32[128,128]{1,0:T(8,128)}, f32[128,128]{1,0:T(8,128)}, f32[256,128]{1,0:T(8,128)}, /*index=5*/f32[8,128]{1,0:T(8,128)}) custom-call(bf16[2,84,64,336]{3,2,1,0:T(8,128)(2,1)} %bitcast.47, bf16[256,48]{1,0:T(8,128)(2,1)} %all_gather.15.kernels_ref, ...), custom_call_target="tpu_custom_call" | custom-call | tf_op jit(solution)/shard_map/pallas_call | solution.py:593
  237.1 0.9 slice_bitcast_fusion
  238.1 2.4 concatenate.6
  242.6 37.0 %psum.79 = f32[8,128]{1,0:T(8,128)S(1)} all-reduce(f32[8,128]{1,0:T(8,128)S(1)} %copy-done.15), channel_id=1, replica_groups=mesh['section'=2,'dp'=16] {'section','dp'}, use_global_device_ids=true, to_apply=%region_4.0 | all-reduce | flops 1024 | bytes 8192 | tf_op jit(solution)/shard_map/psum | solution.py:693
  281.6 0.7 multiply_reduce_fusion.9
  282.3 26.7 %reduce-scatter.3.cloned.1.call-done = f32[16,48]{1,0:T(8,128)} async-done(((f32[256,48]{1,0:T(8,128)}), f32[16,48]{1,0:T(8,128)}) %reduce-scatter.3.cloned.1.call-update) | async-done | bytes 3088 | tf_op jit(solution)/shard_map/reduce_scatter | solution.py:691
  309.0 2.6 psum.78
  311.6 123.9 %reduce-scatter.5.cloned.1.call-done = f32[8,3018]{1,0:T(8,128)} async-done(((f32[128,3018]{1,0:T(8,128)}), f32[8,3018]{1,0:T(8,128)}) %reduce-scatter.5.cloned.1.call-update) | async-done | bytes 96592 | tf_op jit(solution)/shard_map/reduce_scatter | solution.py:689
  436.1 18.5 %all-reduce.5.cloned.1.call-done = f32[8,3018]{1,0:T(8,128)} async-done(((f32[8,3018]{1,0:T(8,128)}), f32[8,3018]{1,0:T(8,128)}) %all-reduce.5.cloned.1.call-update) | async-done | bytes 96592 | tf_op jit(solution)/shard_map/psum | solution.py:689
  454.7 0.9 broadcast_multiply_fusion
  456.2 0.7 fusion.2
  456.9 0.7 multiply_reduce_fusion.7
  457.5 0.7 multiply_reduce_fusion.6
  461.5 77.0 %all-reduce.2 = (f32[]{:T(128)}, f32[]{:T(128)}, f32[2592]{0:T(1024)S(1)}, f32[]{:T(128)}, f32[3,128]{1,0:T(4,128)S(1)}, /*index=5*/f32[]{:T(128)}, f32[]{:T(128)}, f32[]{:T(128)}) all-reduce(f32[]{:T(128)S(6)} %add.120, f32[]{:T(128)} %get-tuple-element.129, ...), channel_id=1, replica_groups=mesh['section'=2,'dp'=16] {'dp'}, use_global_device_ids=true, to_apply=%region_13.14 | all-reduce | flops 2982 | bytes 23856 | tf_op jit(solution)/shard_map/psum | solution.py:712
  543.9 0.7 copy.54
  544.6 0.7 copy.53
  545.3 0.7 copy.55
  548.0 0.7 multiply_subtract_fusion.4
  548.6 0.7 multiply_subtract_fusion.5
  549.3 0.7 fusion.4
  550.0 0.7 multiply_subtract_fusion.2
  (69 shorter events, 6.5 us)
Async XLA Ops:
  7.2 301.8 %reduce-scatter.3.cloned.1.call-start = ((), (), s32[]{:S(2)}) async-start(), calls=%async_computation.2 | async-start | bytes 139264 | tf_op jit(solution)/shard_map/reduce_scatter | solution.py:691
  237.1 198.4 %reduce-scatter.5.cloned.1.call-start = ((), (), s32[]{:S(2)}) async-start(), calls=%async_computation.3 | async-start | bytes 1671168 | tf_op jit(solution)/shard_map/reduce_scatter | solution.py:689
  240.5 0.7 copy-start.3
  240.5 0.8 copy-start.9
  240.5 0.9 copy-start.7
  240.5 2.2 copy-start.15
  240.5 301.1 %copy-start.16 = (f32[3,128]{1,0:T(4,128)S(1)}, f32[3,128]{1,0:T(4,128)}, u32[]{:S(2)}) copy-start(f32[3,128]{1,0:T(4,128)} %param.37) | copy-start | bytes 4612
  240.5 305.5 %copy-start.6 = (f32[16,48]{1,0:T(8,128)S(1)}, f32[16,48]{1,0:T(8,128)}, u32[]{:S(2)}) copy-start(f32[16,48]{1,0:T(8,128)} %param.28) | copy-start | bytes 9220
  240.5 305.5 %copy-start.11 = (f32[16,48]{1,0:T(8,128)S(1)}, f32[16,48]{1,0:T(8,128)}, u32[]{:S(2)}) copy-start(f32[16,48]{1,0:T(8,128)} %param.34) | copy-start | bytes 9220
  240.5 306.1 %copy-start.10 = (f32[2592]{0:T(1024)S(1)}, f32[2592]{0:T(1024)}, u32[]{:S(2)}) copy-start(f32[2592]{0:T(1024)} %param.35) | copy-start | bytes 31108
  240.5 307.3 %copy-start.20 = (f32[8]{0:T(128)S(1)}, f32[8]{0:T(128)}, u32[]{:S(2)}) copy-start(f32[8]{0:T(128)} %param.36) | copy-start | bytes 100
  240.6 307.3 %copy-start.17 = (f32[3,8]{1,0:T(4,128)S(1)}, f32[3,8]{1,0:T(4,128)}, u32[]{:S(2)}) copy-start(f32[3,8]{1,0:T(4,128)} %param.38) | copy-start | bytes 292
  240.6 307.4 %copy-start.8 = (f32[18,8]{0,1:T(8,128)S(1)}, f32[18,8]{0,1:T(8,128)}, u32[]{:S(2)}) copy-start(f32[18,8]{0,1:T(8,128)} %param.31) | copy-start | bytes 1732
  240.6 307.4 %copy-start.14 = (f32[18,8]{0,1:T(8,128)S(1)}, f32[18,8]{0,1:T(8,128)}, u32[]{:S(2)}) copy-start(f32[18,8]{0,1:T(8,128)} %param.39) | copy-start | bytes 1732
  240.6 308.0 %copy-start.18 = (f32[304]{0:T(512)S(1)}, f32[304]{0:T(512)}, u32[]{:S(2)}) copy-start(f32[304]{0:T(512)} %param.41) | copy-start | bytes 3652
  240.6 308.7 %copy-start = (f32[2592,8]{0,1:T(8,128)S(1)}, f32[2592,8]{0,1:T(8,128)}, u32[]{:S(2)}) copy-start(f32[2592,8]{0,1:T(8,128)} %param.29) | copy-start | bytes 248836
  240.6 309.4 %copy-start.4 = (f32[3,128,8]{1,2,0:T(8,128)S(1)}, f32[3,128,8]{1,2,0:T(8,128)}, u32[]{:S(2)}) copy-start(f32[3,128,8]{1,2,0:T(8,128)} %param.30) | copy-start | bytes 36868
  240.7 214.0 %all-reduce.5.cloned.1.call-start = ((), (), s32[]{:S(2)}) async-start(), calls=%async_computation.4 | async-start | bytes 196608 | tf_op jit(solution)/shard_map/psum | solution.py:689
  540.0 10.8 %copy-start.1 = (f32[2592,8]{0,1:T(8,128)}, f32[2592,8]{0,1:T(8,128)S(1)}, u32[]{:S(2)}) copy-start(f32[2592,8]{0,1:T(8,128)S(1)} %get-tuple-element.115) | copy-start | bytes 248836
  540.1 10.6 %copy-start.5 = (f32[3,128,8]{1,2,0:T(8,128)}, f32[3,128,8]{1,2,0:T(8,128)S(1)}, u32[]{:S(2)}) copy-start(f32[3,128,8]{1,2,0:T(8,128)S(1)} %get-tuple-element.111) | copy-start | bytes 36868
  541.7 9.0 %copy-start.12 = (f32[3,128]{1,0:T(4,128)}, f32[3,128]{1,0:T(4,128)S(1)}, u32[]{:S(2)}) copy-start(f32[3,128]{1,0:T(4,128)S(1)} %get-tuple-element.113) | copy-start | bytes 4612
  547.2 3.5 copy-start.2
  547.9 2.9 copy-start.19
  547.9 2.8 copy-start.13
Sparse Core Ops, SparseCore 0:
  237.2 71.7 reduce-scatter.2
  314.5 120.9 reduce-scatter.4
  437.9 16.7 all-reduce.4

commit v2 on v1

--- a/solution.py
+++ b/solution.py
@@ -19,6 +19,7 @@
 OUT1 = 20
 OUT2 = 9
 WIDE = 384
+CHUNK = 12
 FEATS_ROW = OUT2 * C2
 
 CLIP_LIMIT = 0.05
@@ -90,8 +91,9 @@
 
 
 def build_bands(kernels, band_one, band_two):
-    rows48 = iota((48, WIDE), 0)
-    lanes48 = iota((48, WIDE), 1)
+    held = kernels.shape[1]
+    rows48 = iota((held, WIDE), 0)
+    lanes48 = iota((held, WIDE), 1)
     pick_one = jnp.where((lanes48 % C1 == rows48) & (lanes48 < OUT1 * C1), 1.0, 0.0).astype(BF)
     pick_two = jnp.where(
         (lanes48 % C2 + C1 == rows48) & (lanes48 < OUT2 * C2), 1.0, 0.0
@@ -175,8 +177,7 @@
             act_two[:, at : at + FEATS_ROW] = act[step * frames : (step + 1) * frames, :FEATS_ROW]
 
 
-def back_two(dstate_t, linear_t, act_two, z_two, dz_two, grad_linear, frames):
-    grad_linear(dot(dstate_t, act_two[...]))
+def back_two(dstate_t, linear_t, z_two, dz_two, frames):
     dact = dot(dstate_t, linear_t, 0, 0)
     dz_two[0:frames] = jnp.zeros((frames, WIDE), BF)
     dz_two[(OUT2 + 1) * frames : (OUT2 + 2) * frames] = jnp.zeros((frames, WIDE), BF)
@@ -254,7 +255,7 @@
     return jnp.concatenate([row, row], axis=1)
 
 
-def plan(states, mats_t, emb_t, heads_t, bias_col, options, legal, games, valid, rewards, returns):
+def plan(states, mats_t, emb_t, heads_t, bias_col, options, legal, games, valid, rewards, returns, scale):
     frames = states.shape[1]
     pairs = OPTS // 2
     lanes = OPTS * frames
@@ -348,12 +349,13 @@
         errors = errors + valid_f[k] * (
             reward_miss[k] * reward_miss[k] + value_miss[k] * value_miss[k]
         )
-    errors = jnp.where(low_half, errors, 0.0)
+    errors = jnp.where(low_half, errors * scale, 0.0)
 
     half = jnp.where(low_half, 1.0, 0.0)
-    d_plan = 2.0 * valid_f[0] * plan_miss / share_sum
-    d_reward_k = [2.0 * valid_f[k] * reward_miss[k] for k in range(steps)]
-    d_value_k = [2.0 * valid_f[k] * value_miss[k] for k in range(steps)]
+    double = 2.0 * scale
+    d_plan = double * valid_f[0] * plan_miss / share_sum
+    d_reward_k = [double * valid_f[k] * reward_miss[k] for k in range(steps)]
+    d_value_k = [double * valid_f[k] * value_miss[k] for k in range(steps)]
 
     def through(matrix_t, grad):
         return dot(matrix_t, grad, 0, 0)
@@ -436,6 +438,53 @@
         grad_bias,
         errors,
     )
+
+
+def frame_rows(section, refs):
+    options_ref, legal_ref, games_ref, valid_ref, rewards_ref, returns_ref = refs
+
+    def row(ref, k):
+        return ref[k, pl.ds(section, 1), :]
+
+    depth = options_ref.shape[0]
+    return (
+        [row(options_ref, k) for k in range(depth)],
+        [row(legal_ref, k) for k in range(OPTS)],
+        games_ref[pl.ds(section, 1), :],
+        [row(valid_ref, k) for k in range(depth)],
+        [row(rewards_ref, k) for k in range(depth)],
+        [returns_ref[section, k : k + 1, :] for k in range(depth + 1)],
+    )
+
+
+def clear_tails(pixels):
+    tail = jnp.zeros((pixels.shape[0], WIDE - 336), BF)
+    for part in range(4):
+        pixels[:, part * WIDE + 336 : (part + 1) * WIDE] = tail
+
+
+def grad_kernel_two(act_one, dz_two, frames):
+    rows = OUT2 * frames
+    d_two = dz_two[frames : frames + rows]
+    grad = kernel_grad(
+        [dot(d_two, act_one[0:rows], 0, 0), dot(d_two, act_one[frames : frames + rows], 0, 0)],
+        OUT2,
+        C2,
+        2,
+    )
+    return grad, fold(tiles_sum(dot(jnp.ones((8, rows), BF), d_two)), C2)
+
+
+def grad_kernel_one(pixels, dz_one, frames):
+    rows = OUT1 * frames
+    d_one = dz_one[...]
+    grad = kernel_grad(
+        [dot(d_one, pixels[0:rows], 0, 0), dot(d_one, pixels[frames : frames + rows], 0, 0)],
+        OUT1,
+        C1,
+        4,
+    )
+    return grad, fold(tiles_sum(dot(jnp.ones((8, rows), BF), d_one)), C1)
 
 
 def local_kernel(
@@ -472,94 +521,65 @@
 ):
     section = lax.axis_index("section")
     frames = frame_buf.shape[1]
-    side = frame_buf.shape[0]
-    chunk = 12
-    copies = load_frames(frames_hbm, section, frame_buf, sems, chunk)
+    copies = load_frames(frames_hbm, section, frame_buf, sems, CHUNK)
     for copy in copies:
         copy.start()
     build_bands(kernels_ref[...], band_one, band_two)
     bias_one, bias_two, bias_three, bias_four = wide_biases(bias_ref[...])
-    tail = jnp.zeros((pixels.shape[0], WIDE - 336), BF)
-    for part in range(4):
-        pixels[:, part * WIDE + 336 : (part + 1) * WIDE] = tail
+    clear_tails(pixels)
     for which, copy in enumerate(copies):
         copy.wait()
-        place_frames(frame_buf, pixels, which * chunk, chunk, frames)
+        place_frames(frame_buf, pixels, which * CHUNK, CHUNK, frames)
     encode_one(pixels, band_one, bias_one, z_one, act_one, frames, 4)
     encode_two(act_one, band_two, bias_two, z_two, act_two, frames, 3)
     linear_t = linear_ref[...]
     states = (dot(linear_t, act_two[...], 1, 1) + bias_three).astype(BF)
-
-    def row(ref, k):
-        return ref[k, pl.ds(section, 1), :]
-
-    depth = options_ref.shape[0]
     d_state, grad_mats, grad_emb, grad_heads, grad_bias, errors = plan(
         states,
         tuple(mats_ref[k] for k in range(3)),
         emb_ref[:, 0:32],
         heads_ref[:, 0:24],
         bias_four,
-        [row(options_ref, k) for k in range(depth)],
-        [row(legal_ref, k) for k in range(OPTS)],
-        games_ref[pl.ds(section, 1), :],
-        [row(valid_ref, k) for k in range(depth)],
-        [row(rewards_ref, k) for k in range(depth)],
-        [returns_ref[section, k : k + 1, :] for k in range(depth + 1)],
+        *frame_rows(
+            section, (options_ref, legal_ref, games_ref, valid_ref, rewards_ref, returns_ref)
+        ),
+        1.0,
     )
     for k in range(3):
         mats_out[k] = grad_mats[k]
     emb_out[...] = jnp.concatenate([grad_emb, jnp.zeros((D, 96), F32)], axis=1)
     heads_out[...] = jnp.concatenate([grad_heads, jnp.zeros((D, 104), F32)], axis=1)
     d_state_low = d_state.astype(BF)
-    grad_three = jnp.sum(d_state_low.astype(F32), axis=1, keepdims=True)
-
-    def keep_linear(grad):
-        lin_out[...] = grad
-
-    back_two(d_state_low, linear_t, act_two, z_two, dz_two, keep_linear, frames)
-    d_two = dz_two[frames : (OUT2 + 1) * frames]
-    rows_two = OUT2 * frames
-    grad_two = kernel_grad(
-        [
-            dot(d_two, act_one[0:rows_two], 0, 0),
-            dot(d_two, act_one[frames : frames + rows_two], 0, 0),
-        ],
-        OUT2,
-        C2,
-        2,
-    )
-    bias_two_grad = fold(tiles_sum(dot(jnp.ones((8, rows_two), BF), d_two)), C2)
+    lin_out[...] = dot(d_state_low, act_two[...])
+    back_two(d_state_low, linear_t, z_two, dz_two, frames)
+    grad_two, bias_two_grad = grad_kernel_two(act_one, dz_two, frames)
     back_one(dz_two, band_two, z_one, dz_one, frames, 5)
-    d_one = dz_one[...]
-    rows_one = OUT1 * frames
-    grad_one = kernel_grad(
-        [
-            dot(d_one, pixels[0:rows_one], 0, 0),
-            dot(d_one, pixels[frames : frames + rows_one], 0, 0),
-        ],
-        OUT1,
-        C1,
-        4,
-    )
-    bias_one_grad = fold(tiles_sum(dot(jnp.ones((8, rows_one), BF), d_one)), C1)
-    conv_t = jnp.concatenate(
-        [grad_one, grad_two, jnp.zeros((128 - C1 - C2, KERN), F32)], axis=0
-    )
-    conv_out[...] = conv_t.T
+    grad_one, bias_one_grad = grad_kernel_one(pixels, dz_one, frames)
+    conv_out[...] = stack_kernels(grad_one, grad_two)
     lane = iota((8, 128), 1)
     line = iota((8, 128), 0)
     row_zero = jnp.where(
         lane < C1, bias_one_grad, jnp.where(lane < C1 + C2, turn(bias_two_grad, C1), 0.0)
     )
-    count = sum(row(valid_ref, k).astype(F32) for k in range(depth))
+    count = sum(
+        valid_ref[k, pl.ds(section, 1), :].astype(F32) for k in range(valid_ref.shape[0])
+    )
     count = jnp.where(iota((1, 128), 1) < frames, twice(count), 0.0)
     small = jnp.where(line == 0, row_zero, 0.0)
-    small = jnp.where(line == 1, row_of(grad_three), small)
+    small = jnp.where(line == 1, row_of(lane_sum(d_state_low)), small)
     small = jnp.where(line == 2, row_of(grad_bias), small)
     small = jnp.where(line == 3, errors, small)
     small = jnp.where(line == 4, count, small)
     small_out[...] = small
+
+
+def lane_sum(value):
+    return jnp.sum(value.astype(F32), axis=1, keepdims=True)
+
+
+def stack_kernels(grad_one, grad_two):
+    rows = jnp.concatenate([grad_one, grad_two, jnp.zeros((128 - C1 - C2, KERN), F32)], axis=0)
+    return rows.T
 
 
 def tiles_sum(value):
@@ -582,7 +602,7 @@
         pltpu.VMEM((frames, FEAT), BF),
         pltpu.VMEM(((OUT2 + 2) * frames, WIDE), BF),
         pltpu.VMEM((OUT1 * frames, WIDE), BF),
-        pltpu.SemaphoreType.DMA((side // 12,)),
+        pltpu.SemaphoreType.DMA((side // CHUNK,)),
     ]
 
 
@@ -611,6 +631,631 @@
         valid.transpose(2, 0, 1),
         rewards.transpose(2, 0, 1),
         returns.transpose(0, 2, 1),
+    )
+
+
+MESH = pl.DeviceIdType.MESH
+LIN_PAD = 2688
+QUARTER = 896
+HALF = 2 * QUARTER
+AT_MATS = LIN_PAD
+AT_EMB = AT_MATS + 3 * D
+AT_HEADS = AT_EMB + 128
+AT_END = AT_HEADS + 128
+
+
+def fused_kernel(
+    peers,
+    frames_hbm,
+    conv_ref,
+    lin_ref,
+    mats_ref,
+    emb_ref,
+    heads_ref,
+    bias_ref,
+    options_ref,
+    legal_ref,
+    games_ref,
+    valid_ref,
+    rewards_ref,
+    returns_ref,
+    main_out,
+    conv_out,
+    tile_out,
+    stats_out,
+    frame_buf,
+    pixels,
+    band_one,
+    band_two,
+    z_one,
+    act_one,
+    z_two,
+    act_two,
+    dz_two,
+    dz_one,
+    frame_sems,
+    stage,
+    kernel_msg,
+    weight_msg,
+    weights,
+    grad_own,
+    grad_mate,
+    grad_msg,
+    grad_in,
+    tile_msg,
+    tile_in,
+    stats_in,
+    half_in,
+    conv_half_in,
+    send_sems,
+    recv_sems,
+    all_send,
+    all_recv,
+    mate_send,
+    mate_recv,
+):
+    section = lax.axis_index("section")
+    place = lax.axis_index("dp")
+    mate = 1 - section
+    frames = frame_buf.shape[1]
+    everyone = 2 * peers
+
+    barrier = pltpu.get_barrier_semaphore()
+
+    def other(step):
+        flat = lax.rem(section * peers + place + step, everyone)
+        return flat // peers, lax.rem(flat, peers)
+
+    def greet(step, carry):
+        to_section, to_place = other(step)
+        pl.semaphore_signal(barrier, inc=1, device_id=(to_section, to_place), device_id_type=MESH)
+        return carry
+
+    lax.fori_loop(1, everyone, greet, 0)
+    copies = load_frames(frames_hbm, section, frame_buf, frame_sems, CHUNK)
+    for copy in copies:
+        copy.start()
+
+    def to_peer(phase, step, source, target):
+        peer = lax.rem(place + step, peers)
+        return pltpu.make_async_remote_copy(
+            src_ref=source(peer),
+            dst_ref=target.at[place],
+            send_sem=send_sems.at[phase, step],
+            recv_sem=recv_sems.at[phase, place],
+            device_id=(section, peer),
+            device_id_type=MESH,
+        )
+
+    def from_peer(phase, step, target):
+        peer = lax.rem(place + step, peers)
+        return pltpu.make_async_remote_copy(
+            src_ref=target.at[peer],
+            dst_ref=target.at[peer],
+            send_sem=send_sems.at[phase, step],
+            recv_sem=recv_sems.at[phase, peer],
+            device_id=(section, peer),
+            device_id_type=MESH,
+        )
+
+    def each_peer(act):
+        def body(step, carry):
+            act(step)
+            return carry
+
+        lax.fori_loop(1, peers, body, 0)
+
+    def to_other(phase, step, source, target):
+        to_section, to_place = other(step)
+        return pltpu.make_async_remote_copy(
+            src_ref=source(to_section, to_place),
+            dst_ref=target.at[section, place],
+            send_sem=all_send.at[phase, step],
+            recv_sem=all_recv.at[phase, section, place],
+            device_id=(to_section, to_place),
+            device_id_type=MESH,
+        )
+
+    def from_other(phase, step, target):
+        its_section, its_place = other(step)
+        return pltpu.make_async_remote_copy(
+            src_ref=target.at[its_section, its_place],
+            dst_ref=target.at[its_section, its_place],
+            send_sem=all_send.at[phase, step],
+            recv_sem=all_recv.at[phase, its_section, its_place],
+            device_id=(its_section, its_place),
+            device_id_type=MESH,
+        )
+
+    def each_other(act):
+        def body(step, carry):
+            act(step)
+            return carry
+
+        lax.fori_loop(1, everyone, body, 0)
+
+    def to_mate(which, source, target):
+        return pltpu.make_async_remote_copy(
+            src_ref=source,
+            dst_ref=target,
+            send_sem=mate_send.at[which],
+            recv_sem=mate_recv.at[which],
+            device_id=(mate, place),
+            device_id_type=MESH,
+        )
+
+    upper_lanes = iota((16, 128), 1) >= 64
+    counts = sum(
+        valid_ref[k, m : m + 1, :].astype(F32)
+        for k in range(valid_ref.shape[0])
+        for m in range(valid_ref.shape[1])
+    )
+    conv_pad = jnp.concatenate([conv_ref[...], jnp.zeros((16, 80), F32)], axis=1)
+    kernel_msg[place] = jnp.where(
+        upper_lanes & (iota((16, 128), 0) == 0), jnp.broadcast_to(twice(counts), (16, 128)), conv_pad
+    ).astype(BF)
+    heads_pad = jnp.concatenate([heads_ref[...], jnp.zeros((24, 120), F32)], axis=1)
+    heads_pad = jnp.concatenate([heads_pad, jnp.zeros((104, 128), F32)], axis=0).T
+    stage[:, 0:FEAT] = lin_ref[...]
+    stage[:, FEAT:LIN_PAD] = jnp.zeros((8, LIN_PAD - FEAT), F32)
+    for k in range(3):
+        stage[:, AT_MATS + k * D : AT_MATS + (k + 1) * D] = mats_ref[k]
+    stage[:, AT_EMB:AT_HEADS] = jnp.concatenate(
+        [emb_ref[...], jnp.zeros((8, 128 - OPTS), F32)], axis=1
+    )
+    stage[:, AT_HEADS:AT_END] = heads_pad[0:8]
+    stage[:, AT_END : 2 * HALF] = jnp.zeros((8, 2 * HALF - AT_END), F32)
+    first = stage[:, pl.ds(pl.multiple_of(section * HALF, 128), QUARTER)]
+    second = stage[:, pl.ds(pl.multiple_of(section * HALF + QUARTER, 128), QUARTER)]
+    weight_msg[section, place] = jnp.concatenate([first, second], axis=0).astype(BF)
+
+    pl.semaphore_wait(barrier, everyone - 1)
+    own_kernel = lambda peer: kernel_msg.at[place]
+    own_weight = lambda peer: weight_msg.at[section, place]
+    each_peer(lambda step: to_peer(0, step, own_kernel, kernel_msg).start())
+    each_peer(lambda step: to_peer(1, step, own_weight, weight_msg.at[section]).start())
+
+    bias_one, bias_two, bias_three, bias_four = wide_biases(bias_ref[...])
+    clear_tails(pixels)
+    act_two[:, FEAT:LIN_PAD] = jnp.zeros((frames, LIN_PAD - FEAT), BF)
+    for which, copy in enumerate(copies):
+        copy.wait()
+        place_frames(frame_buf, pixels, which * CHUNK, CHUNK, frames)
+    each_peer(lambda step: from_peer(0, step, kernel_msg).wait_recv())
+    kernels = kernel_msg[...].reshape(KERN, 128)
+    counted = jnp.where(iota((KERN, 128), 1) >= 64, kernels.astype(F32), 0.0)
+    count = jnp.sum(jnp.sum(counted, axis=0, keepdims=True), axis=1, keepdims=True)
+    scale = 1.0 / count
+    build_bands(kernels, band_one, band_two)
+    encode_one(pixels, band_one, bias_one, z_one, act_one, frames, 4)
+    each_peer(lambda step: from_peer(1, step, weight_msg.at[section]).wait_recv())
+    pass_weights = to_mate(0, weight_msg.at[section], weight_msg.at[section])
+    pass_weights.start()
+    encode_two(act_one, band_two, bias_two, z_two, act_two, frames, 3)
+    to_mate(0, weight_msg.at[section], weight_msg.at[mate]).wait_recv()
+    for half in range(2):
+        block = weight_msg[half].astype(F32)
+        for part in range(2):
+            lane = (2 * half + part) * QUARTER
+            weights[:, lane : lane + QUARTER] = (
+                block[:, part * 8 : (part + 1) * 8].reshape(D, QUARTER).astype(BF)
+            )
+    linear_t = weights[:, 0:LIN_PAD]
+    states = (dot(linear_t, act_two[...], 1, 1) + bias_three).astype(BF)
+    d_state, grad_mats, grad_emb, grad_heads, grad_bias, errors = plan(
+        states,
+        tuple(weights[:, AT_MATS + k * D : AT_MATS + (k + 1) * D] for k in range(3)),
+        weights[:, AT_EMB : AT_EMB + 32],
+        weights[:, AT_HEADS : AT_HEADS + 24],
+        bias_four,
+        *frame_rows(
+            section, (options_ref, legal_ref, games_ref, valid_ref, rewards_ref, returns_ref)
+        ),
+        scale,
+    )
+
+    d_state_low = d_state.astype(BF)
+    grad_linear = dot(d_state_low, act_two[...])
+    grad_own[0] = grad_linear[:, 0:HALF].reshape(peers, 8, HALF)
+    grad_own[1, :, :, 0 : LIN_PAD - HALF] = grad_linear[:, HALF:LIN_PAD].reshape(
+        peers, 8, LIN_PAD - HALF
+    )
+    for k in range(3):
+        lane = AT_MATS - HALF + k * D
+        grad_own[1, :, :, lane : lane + D] = grad_mats[k].reshape(peers, 8, D)
+    lane = AT_EMB - HALF
+    grad_own[1, :, :, lane : lane + 128] = jnp.concatenate(
+        [grad_emb, jnp.zeros((D, 96), F32)], axis=1
+    ).reshape(peers, 8, 128)
+    grad_own[1, :, :, lane + 128 : lane + 256] = jnp.concatenate(
+        [grad_heads, jnp.zeros((D, 104), F32)], axis=1
+    ).reshape(peers, 8, 128)
+    grad_own[1, :, :, lane + 256 : HALF] = jnp.zeros((peers, 8, 2 * HALF - AT_END), F32)
+    pass_grads = to_mate(1, grad_own.at[mate], grad_mate)
+    pass_grads.start()
+    back_two(d_state_low, linear_t, z_two, dz_two, frames)
+    grad_two, bias_two_grad = grad_kernel_two(act_one, dz_two, frames)
+    pass_grads.wait_recv()
+    paired = grad_own[section] + grad_mate[...]
+    grad_msg[...] = jnp.concatenate(
+        [paired[:, :, 0:QUARTER], paired[:, :, QUARTER:HALF]], axis=1
+    ).astype(BF)
+    each_peer(lambda step: to_peer(2, step, lambda peer: grad_msg.at[peer], grad_in).start())
+    grad_in[place] = grad_msg[place]
+    back_one(dz_two, band_two, z_one, dz_one, frames, 5)
+    grad_one, bias_one_grad = grad_kernel_one(pixels, dz_one, frames)
+
+    conv_rows = stack_kernels(grad_one, grad_two).reshape(everyone, 8, 128)
+    lane = iota((8, 128), 1)
+    line = iota((8, 128), 0)
+    row_three = row_of(lane_sum(d_state_low))
+    row_four = row_of(grad_bias)
+    row_first = jnp.where(
+        lane < C1, bias_one_grad, jnp.where(lane < C1 + C2, turn(bias_two_grad, C1), 0.0)
+    )
+    rows = [turn(row_three, 64), row_three, turn(row_four, 64), row_four, turn(row_first, 64)[0:1], turn(errors, 64)]
+    extra = jnp.zeros((8, 128), F32)
+    for which, row in enumerate(rows):
+        extra = jnp.where(line == which, row, extra)
+    tiles = jnp.where(iota((everyone, 8, 128), 2) >= 64, extra[None], conv_rows)
+    tile_msg[...] = tiles.reshape(peers, 2, 8, 128)
+    each_other(
+        lambda step: to_other(0, step, lambda s, d: tile_msg.at[d, s], tile_in).start()
+    )
+    tile_in[section, place] = tile_msg[place, section]
+    each_peer(lambda step: from_peer(2, step, grad_in).wait_recv())
+    total = jnp.sum(grad_in[...].astype(F32), axis=0)
+    squares = total * total
+    stat = jnp.zeros((16, 128), F32)
+    stat_line = iota((16, 128), 0)
+    for part in range(2):
+        sums = jnp.sum(squares[part * 8 : (part + 1) * 8], axis=0, keepdims=True)
+        for tile in range(7):
+            stat = jnp.where(
+                stat_line == part * 7 + tile, sums[:, tile * 128 : (tile + 1) * 128], stat
+            )
+    each_other(lambda step: from_other(0, step, tile_in).wait_recv())
+    tile_total = jnp.sum(tile_in[...].reshape(everyone, 8, 128), axis=0)
+    conv_squares = jnp.where(lane < C1 + C2, tile_total * tile_total, 0.0)
+    stat = jnp.where(stat_line == 14, jnp.sum(conv_squares, axis=0, keepdims=True), stat)
+
+    def square_sum(value):
+        return jnp.sum(jnp.sum(value * value, axis=0, keepdims=True), axis=1, keepdims=True)
+
+    weight_squares = [
+        square_sum(conv_pad),
+        square_sum(lin_ref[...]),
+        sum(square_sum(mats_ref[k]) for k in range(3)),
+        square_sum(emb_ref[...]),
+        square_sum(heads_ref[...]),
+    ]
+    for which, value in enumerate(weight_squares):
+        stat = jnp.where((stat_line == 15) & (iota((16, 128), 1) == which), value, stat)
+    stats_in[section, place] = stat
+    own_half = jnp.concatenate([total[0:8], total[8:16]], axis=1)
+    half_in[section] = own_half
+    conv_half_in[section] = tile_total
+    each_other(
+        lambda step: to_other(
+            1, step, lambda s, d: stats_in.at[section, place], stats_in
+        ).start()
+    )
+    pass_half = to_mate(2, half_in.at[section], half_in.at[section])
+    pass_half.start()
+    pass_conv = to_mate(3, conv_half_in.at[section], conv_half_in.at[section])
+    pass_conv.start()
+    tile_out[...] = tile_total
+    to_mate(2, half_in.at[section], half_in.at[mate]).wait_recv()
+    to_mate(3, conv_half_in.at[section], conv_half_in.at[mate]).wait_recv()
+    for half in range(2):
+        main_out[:, half * HALF : (half + 1) * HALF] = half_in[half]
+        conv_out[half * 8 : (half + 1) * 8] = conv_half_in[half]
+    each_other(lambda step: from_other(1, step, stats_in).wait_recv())
+    stats_out[...] = jnp.sum(stats_in[...], axis=1)
+
+    each_peer(lambda step: to_peer(0, step, own_kernel, kernel_msg).wait_send())
+    each_peer(lambda step: to_peer(1, step, own_weight, weight_msg.at[section]).wait_send())
+    each_peer(lambda step: to_peer(2, step, lambda peer: grad_msg.at[peer], grad_in).wait_send())
+    each_other(
+        lambda step: to_other(0, step, lambda s, d: tile_msg.at[d, s], tile_in).wait_send()
+    )
+    each_other(
+        lambda step: to_other(
+            1, step, lambda s, d: stats_in.at[section, place], stats_in
+        ).wait_send()
+    )
+    for copy in (pass_weights, pass_grads, pass_half, pass_conv):
+        copy.wait_send()
+
+
+def fused_step(peers, frames, shards, biases, rows):
+    count = frames.shape[1]
+    side = frames.shape[2]
+    scratch = local_scratch(count, side)
+    scratch[7] = pltpu.VMEM((count, LIN_PAD), BF)
+    scratch += [
+        pltpu.VMEM((8, 2 * HALF), F32),
+        pltpu.VMEM((peers, 16, 128), BF),
+        pltpu.VMEM((2, peers, 16, QUARTER), BF),
+        pltpu.VMEM((D, 2 * HALF), BF),
+        pltpu.VMEM((2, peers, 8, HALF), F32),
+        pltpu.VMEM((peers, 8, HALF), F32),
+        pltpu.VMEM((peers, 16, QUARTER), BF),
+        pltpu.VMEM((peers, 16, QUARTER), BF),
+        pltpu.VMEM((peers, 2, 8, 128), F32),
+        pltpu.VMEM((2, peers, 8, 128), F32),
+        pltpu.VMEM((2, peers, 16, 128), F32),
+        pltpu.VMEM((2, 8, HALF), F32),
+        pltpu.VMEM((2, 8, 128), F32),
+        pltpu.SemaphoreType.DMA((3, peers)),
+        pltpu.SemaphoreType.DMA((3, peers)),
+        pltpu.SemaphoreType.DMA((2, 2 * peers)),
+        pltpu.SemaphoreType.DMA((2, 2, peers)),
+        pltpu.SemaphoreType.DMA((4,)),
+        pltpu.SemaphoreType.DMA((4,)),
+    ]
+    shapes = [(8, 2 * HALF), (16, 128), (8, 128), (2, 16, 128)]
+    operands = [frames.transpose(0, 2, 1, 3), *shards, biases.reshape(1, BIAS), *rows]
+    return pl.pallas_call(
+        functools.partial(fused_kernel, peers),
+        out_shape=[jax.ShapeDtypeStruct(shape, F32) for shape in shapes],
+        in_specs=[ANY_SPEC] + [VMEM_SPEC] * (len(operands) - 1),
+        out_specs=[VMEM_SPEC] * len(shapes),
+        scratch_shapes=scratch,
+        compiler_params=pltpu.CompilerParams(
+            vmem_limit_bytes=56 * 1024 * 1024, collective_id=0, has_side_effects=True
+        ),
+    )(*operands)
+
+
+def column_of(row):
+    square = jnp.broadcast_to(row, (8, 8))
+    return jnp.sum(jnp.where(iota((8, 8), 0) == iota((8, 8), 1), square, 0.0), axis=1, keepdims=True)
+
+
+def row_back(column):
+    square = jnp.broadcast_to(column, (8, 8))
+    return jnp.sum(jnp.where(iota((8, 8), 0) == iota((8, 8), 1), square, 0.0), axis=0, keepdims=True)
+
+
+def total_of(value):
+    return jnp.sum(jnp.sum(value, axis=0, keepdims=True), axis=1, keepdims=True)
+
+
+def update_kernel(
+    main_ref,
+    convg_ref,
+    tile_ref,
+    stats_ref,
+    conv_ref,
+    lin_ref,
+    mats_ref,
+    emb_ref,
+    heads_ref,
+    bias_ref,
+    conv_moment,
+    lin_rows,
+    lin_cols,
+    mats_rows,
+    mats_cols,
+    emb_moment,
+    head_moment,
+    bias_moment,
+    conv_new,
+    conv_grad,
+    conv_moment_new,
+    lin_new,
+    lin_grad,
+    lin_rows_new,
+    lin_cols_new,
+    mats_new,
+    mats_grad,
+    mats_rows_new,
+    mats_cols_new,
+    emb_new,
+    emb_grad,
+    emb_moment_new,
+    heads_new,
+    heads_grad,
+    head_moment_new,
+    bias_new,
+    bias_grad,
+    bias_moment_new,
+    norm_out,
+    loss_out,
+    conv_low,
+    lin_low,
+):
+    stats = stats_ref[...]
+    tile = tile_ref[...]
+    squares = jnp.where(iota((2, 16, 128), 1) < 15, stats, 0.0)
+    squares = total_of(squares[0] + squares[1])
+    scales = 0.5 * (stats[0] + stats[1])[15:16]
+    bias_raw = jnp.concatenate(
+        [tile[4:5, 64 : 64 + C1 + C2]] + [tile[k : k + 1, 64:128] for k in range(4)], axis=1
+    )
+    norm = jnp.sqrt(squares + total_of(bias_raw * bias_raw))
+    factor = jnp.minimum(1.0, CLIP_LIMIT / norm)
+    norm_out[...] = norm
+    loss_out[...] = total_of(tile[5:6, 64:128])
+
+    def simple(weight, grad, moment, square_total, outs):
+        new, moment_new = unfactored(
+            weight, grad, moment, relative(square_total, weight.size * outs[3])
+        )
+        outs[0][...] = new
+        outs[1][...] = grad
+        outs[2][...] = moment_new
+        return new
+
+    peers = D // lin_ref.shape[0]
+    conv = simple(
+        conv_ref[...],
+        factor * convg_ref[:, 0 : C1 + C2],
+        conv_moment[...],
+        scales[:, 0:1],
+        (conv_new, conv_grad, conv_moment_new, peers),
+    )
+    conv_low[...] = conv.astype(BF)
+    simple(
+        emb_ref[...],
+        factor * main_ref[:, AT_EMB : AT_EMB + OPTS],
+        emb_moment[...],
+        scales[:, 3:4],
+        (emb_new, emb_grad, emb_moment_new, peers),
+    )
+    heads_t = jnp.concatenate([main_ref[:, AT_HEADS:AT_END], jnp.zeros((120, 128), F32)], axis=0).T
+    simple(
+        heads_ref[...],
+        factor * heads_t[0 : 3 * GAMES, 0:8],
+        head_moment[...],
+        scales[:, 4:5],
+        (heads_new, heads_grad, head_moment_new, peers),
+    )
+    bias = bias_ref[...]
+    simple(
+        bias,
+        factor * bias_raw,
+        bias_moment[...],
+        total_of(bias * bias),
+        (bias_new, bias_grad, bias_moment_new, 1),
+    )
+    row_sums = [stats[t // 14, t % 14 : t % 14 + 1] for t in range(24)]
+
+    def factored(weight, grad, rows_old, cols_old, row_sum, square_total, entries):
+        rows = DECAY_RATE * rows_old + (1.0 - DECAY_RATE) * (
+            factor * factor * row_sum / D + FLOOR_ONE
+        )
+        wide = grad.shape[1]
+        cols = DECAY_RATE * cols_old + (1.0 - DECAY_RATE) * (
+            jnp.sum(grad * grad + FLOOR_ONE, axis=1, keepdims=True) / wide
+        )
+        mean = jnp.sum(rows, axis=1, keepdims=True) / wide
+        second = rows * cols / mean
+        new = weight - STEP_RATE * relative(square_total, entries) * grad * lax.rsqrt(second)
+        return new, rows, cols
+
+    grad = factor * main_ref[:, 0:FEAT]
+    new, rows, cols = factored(
+        lin_ref[...],
+        grad,
+        lin_rows[...],
+        column_of(lin_cols[...]),
+        jnp.concatenate(row_sums[:21], axis=1)[:, 0:FEAT],
+        scales[:, 1:2],
+        FEAT * D,
+    )
+    lin_new[...] = new
+    lin_grad[...] = grad
+    lin_rows_new[...] = rows
+    lin_cols_new[...] = row_back(cols)
+    lin_low[...] = new.astype(BF)
+    for k in range(3):
+        grad = factor * main_ref[:, AT_MATS + k * D : AT_MATS + (k + 1) * D]
+        new, rows, cols = factored(
+            mats_ref[k],
+            grad,
+            mats_rows[k : k + 1],
+            column_of(mats_cols[k : k + 1]),
+            row_sums[21 + k],
+            scales[:, 2:3],
+            3 * D * D,
+        )
+        mats_new[k] = new
+        mats_grad[k] = grad
+        mats_rows_new[k : k + 1] = rows
+        mats_cols_new[k : k + 1] = row_back(cols)
+
+
+def fused_device(
+    frames,
+    options,
+    legal,
+    games,
+    valid,
+    rewards,
+    returns,
+    conv_kernels,
+    enc_linear,
+    plan_mats,
+    option_emb,
+    heads,
+    biases,
+    conv_moment,
+    lin_rows,
+    lin_cols,
+    mats_rows,
+    mats_cols,
+    emb_moment,
+    head_moment,
+    bias_moment,
+):
+    width = enc_linear.shape[1]
+    peers = D // width
+    shards = (
+        conv_kernels,
+        enc_linear.T,
+        plan_mats.transpose(0, 2, 1),
+        option_emb.T,
+        heads.reshape(3 * GAMES, width),
+    )
+    summed = fused_step(
+        peers,
+        frames,
+        shards,
+        biases,
+        (
+            options.transpose(2, 0, 1),
+            legal.transpose(2, 0, 1),
+            games,
+            valid.transpose(2, 0, 1),
+            rewards.transpose(2, 0, 1),
+            returns.transpose(0, 2, 1),
+        ),
+    )
+    shapes = [(16, 48)] * 3 + [(8, FEAT)] * 2 + [(1, FEAT), (1, 8)] + [(3, 8, D)] * 2 + [(3, D), (3, 8)]
+    shapes += [(8, OPTS)] * 3 + [(24, 8)] * 3 + [(1, BIAS)] * 3 + [(1, 1)] * 2
+    outs = [jax.ShapeDtypeStruct(shape, F32) for shape in shapes]
+    outs += [jax.ShapeDtypeStruct((16, 48), BF), jax.ShapeDtypeStruct((8, FEAT), BF)]
+    operands = [
+        *summed,
+        *shards,
+        biases.reshape(1, BIAS),
+        conv_moment,
+        lin_rows.reshape(1, FEAT),
+        lin_cols.reshape(1, width),
+        mats_rows,
+        mats_cols,
+        emb_moment.T,
+        head_moment.reshape(3 * GAMES, width),
+        bias_moment.reshape(1, BIAS),
+    ]
+    o = pl.pallas_call(
+        update_kernel,
+        out_shape=outs,
+        in_specs=[VMEM_SPEC] * len(operands),
+        out_specs=[VMEM_SPEC] * len(outs),
+    )(*operands)
+    flat_heads = [h.reshape(3, GAMES, width) for h in o[14:17]]
+    return (
+        *o[0:3],
+        o[3].T,
+        o[4].T,
+        o[5].reshape(FEAT),
+        o[6].reshape(width),
+        o[7].transpose(0, 2, 1),
+        o[8].transpose(0, 2, 1),
+        o[9],
+        o[10],
+        o[11].T,
+        o[12].T,
+        o[13].T,
+        *flat_heads,
+        *[b.reshape(BIAS) for b in o[17:20]],
+        o[20].reshape(()),
+        o[21].reshape(()),
+        o[22],
+        o[23].T,
     )
 
 
@@ -786,7 +1431,7 @@
 
 def solution(mesh):
     return jax.shard_map(
-        per_device,
+        fused_device if mesh.shape["dp"] * 8 == D else per_device,
         mesh=mesh,
         in_specs=(
             P(None, "dp", None, None),

time: 561 us -> 66.9 us (0.12)
  blocking collectives: 317 us -> 0 us
  waiting for transfers between devices: 169 us -> 0 us
  Pallas kernels: 19.5 us -> 56.9 us
  between operations: 27.1 us -> 0.68 us
  other arithmetic: 17.7 us -> 5.1 us
    all_gather x5 -> x0, blocking collectives: 201 us -> none  [gather_rows(): return lax.all_gather(shard, 'dp', axis=0, tiled=True)]
    reduce_scatter x2 -> x0, waiting for transfers between devices: 151 us -> none  [the longest x1 124 us: per_device(): lax.psum_scatter(rows, 'dp', scatter_dimension=0, tiled=True)]
    psum x3 -> x0, blocking collectives: 117 us -> none  [the longest x1 77 us: per_device(): lax.psum((partial_squares, jnp.sum(g_lin * g_lin, axis=1), jnp.sum(g_mats...]
    pallas_call x1 -> x2, Pallas kernels: 19.5 us -> 56.9 us  [the longest x1 54.7 us: fused_step(): pl.pallas_call(functools.partial(fused_kernel, peers), out_shape=[jax.Sha...]
    psum x1 -> x0, waiting for transfers between devices: 18.5 us -> none  [per_device(): lax.psum(lax.psum_scatter(rows, 'dp', scatter_dimension=0, tiled=True), '...]
    reduce_sum x16 -> x0, other arithmetic: 12.7 us -> none  [the longest x1 1.59 us: per_device(): jnp.sum(enc_linear * enc_linear)]
  transfers between devices with their start and end apart: 3 -> 0, of which waited for: 3 -> 0; matrix products, arithmetic and copies ran while one was open for 1% -> 0% of each run, Pallas kernels for 0% -> 0%
where the time goes in v2:
time: 66.9 us; the launch traced here: 66.5 us
  Pallas kernels  56.9 us (85%)
  other arithmetic  5.1 us (8%)
  local copies, waits for them, and re-layouts  3.8 us (6%)
  between operations  0.68 us (1%)
    pallas_call x1, Pallas kernels, fused_step(): pl.pallas_call(functools.partial(fused_kernel, peers), out_shape=[jax.Sha...  54.7 us
    pallas_call x4, other arithmetic, fused_device(): pl.pallas_call(update_kernel, out_shape=outs, in_specs=[VMEM_SPEC] * len(...  5.1 us
    pallas_call x1, Pallas kernels, fused_device(): pl.pallas_call(update_kernel, out_shape=outs, in_specs=[VMEM_SPEC] * len(...  2.19 us

profile of v2, /device:TPU:0, one launch (start us, length us, event | category | flops | bytes accessed | tf_op | source)
XLA Modules:
  0.0 66.5 jit_solution(6222209389207648848)
XLA Ops:
  0.7 1.2 %reshape.98.bias_ref = f32[1,304]{1,0:T(1,128)} reshape(f32[304]{0:T(512)} %param.33) | data formatting | bytes 2432 | tf_op jit(solution)/shard_map/reshape | solution.py:998
  1.9 1.2 %reshape.102.bias_moment = f32[1,304]{1,0:T(1,128)} reshape(f32[304]{0:T(512)} %param.41) | data formatting | bytes 2432 | tf_op jit(solution)/shard_map/reshape | solution.py:1231
  3.1 1.3 %reshape.99.lin_rows = f32[1,2592]{1,0:T(1,128)} reshape(f32[2592]{0:T(1024)} %param.35) | data formatting | bytes 20736 | tf_op jit(solution)/shard_map/reshape | solution.py:1225
  4.5 54.7 %shard_map.388 = (f32[8,3584]{1,0:T(8,128)}, f32[16,128]{1,0:T(8,128)}, f32[8,128]{1,0:T(8,128)}, f32[2,16,128]{2,1,0:T(8,128)}) custom-call(bf16[2,84,64,336]{3,2,1,0:T(8,128)(2,1)} %bitcast.27, f32[16,48]{1,0:T(8,128)} %conv_ref.3, f32[8,2592]{1,0:T(8,128)} %bitcast.28, f32[3,8,128]{2,1,0:T(8,128)} %bitcast.30, f32[8,18]{1,0:T(8,128)} %bitcast.35, ...), custom_call_target="tpu_custom_call" | custom-call | tf_op jit(solution)/shard_map/pallas_call | solution.py:999
  59.2 2.2 %shard_map.389 = (f32[16,48]{1,0:T(8,128)}, f32[16,48]{1,0:T(8,128)}, f32[16,48]{1,0:T(8,128)}, f32[8,2592]{1,0:T(8,128)}, f32[8,2592]{1,0:T(8,128)}, /*index=5*...) custom-call(f32[8,3584]{1,0:T(8,128)} %get-tuple-element.52.main_ref, ...), custom_call_target="tpu_custom_call" | custom-call | tf_op jit(solution)/shard_map/pallas_call | solution.py:1233
  61.4 1.3 %reduce.1 = f32[304]{0:T(512)} reduce(f32[1,304]{1,0:T(1,128)} %get-tuple-element.73, f32[]{:T(128)} %constant.8), dimensions={0}, to_apply=%get-tuple-element.73.reduce_sub_computation | reduce | bytes 2436 | tf_op jit(solution)/shard_map/pallas_call | solution.py:1233
  62.6 1.3 %reduce.2 = f32[304]{0:T(512)} reduce(f32[1,304]{1,0:T(1,128)} %get-tuple-element.74, f32[]{:T(128)} %constant.8), dimensions={0}, to_apply=%get-tuple-element.74.reduce_sub_computation | reduce | bytes 2436 | tf_op jit(solution)/shard_map/pallas_call | solution.py:1233
  63.9 1.2 %reduce.3 = f32[304]{0:T(512)} reduce(f32[1,304]{1,0:T(1,128)} %get-tuple-element.75, f32[]{:T(128)} %constant.8), dimensions={0}, to_apply=%get-tuple-element.75.reduce_sub_computation | reduce | bytes 2436 | tf_op jit(solution)/shard_map/pallas_call | solution.py:1233
  65.1 1.3 %reduce = f32[2592]{0:T(1024)} reduce(f32[1,2592]{1,0:T(1,128)} %get-tuple-element.61, f32[]{:T(128)} %constant.8), dimensions={0}, to_apply=%get-tuple-element.61.reduce_sub_computation | reduce | bytes 20740 | tf_op jit(solution)/shard_map/pallas_call | solution.py:1233

commit v3 on v2

--- a/solution.py
+++ b/solution.py
@@ -19,6 +19,9 @@
 OUT1 = 20
 OUT2 = 9
 WIDE = 384
+LIN_PAD = 2688
+EMB_LANE = FEAT % 128
+HEAD_LANE = EMB_LANE + OPTS
 CHUNK = 12
 FEATS_ROW = OUT2 * C2
 
@@ -100,30 +103,33 @@
     ).astype(BF)
     wide_one = dot(kernels, pick_one)
     wide_two = dot(kernels, pick_two)
-    group = iota((16, WIDE), 1) // C1
-    for tap in range(8):
-        left = wide_one[tap * 32 : tap * 32 + 16]
-        right = wide_one[tap * 32 + 16 : tap * 32 + 32]
-        for block in range(24):
-            rows = tap * WIDE + block * 16
-            if block > OUT1:
-                band_one[rows : rows + 16] = jnp.zeros((16, WIDE), BF)
-            else:
-                band_one[rows : rows + 16] = jnp.where(
-                    group == block, left, jnp.where(group == block - 1, right, 0.0)
-                ).astype(BF)
-    group = iota((32, WIDE), 1) // C2
-    for tap in range(4):
-        left = wide_two[tap * 64 : tap * 64 + 32]
-        right = wide_two[tap * 64 + 32 : tap * 64 + 64]
-        for block in range(12):
-            rows = tap * WIDE + block * 32
-            if block > OUT2:
-                band_two[rows : rows + 32] = jnp.zeros((32, WIDE), BF)
-            else:
-                band_two[rows : rows + 32] = jnp.where(
-                    group == block, left, jnp.where(group == block - 1, right, 0.0)
-                ).astype(BF)
+    for wide, band, width, taps, blocks in (
+        (wide_one, band_one, C1, 8, OUT1),
+        (wide_two, band_two, C2, 4, OUT2),
+    ):
+        per_tile = 128 // width
+        group = iota((width, 128), 1) // width
+        for tap in range(taps):
+            base = 2 * tap * width
+            for block in range(blocks + 1):
+                rows = tap * WIDE + block * width
+                tile, spot = divmod(block, per_tile)
+                lanes = slice(tile * 128, (tile + 1) * 128)
+                left = jnp.where(group == spot, wide[base : base + width, lanes], 0.0)
+                right = wide[base + width : base + 2 * width]
+                if spot > 0:
+                    left = jnp.where(group == spot - 1, right[:, lanes], left)
+                elif block > 0:
+                    before = slice((tile - 1) * 128, tile * 128)
+                    band[rows : rows + width, before] = jnp.where(
+                        group == per_tile - 1, right[:, before], 0.0
+                    ).astype(BF)
+                band[rows : rows + width, lanes] = left.astype(BF)
+
+
+def clear_bands(band_one, band_two):
+    band_one[...] = jnp.zeros(band_one.shape, BF)
+    band_two[...] = jnp.zeros(band_two.shape, BF)
 
 
 def wide_biases(bias_row):
@@ -206,7 +212,7 @@
                 ]
 
 
-def band_sums(full, base, outputs, width):
+def band_sums(term, outputs, width):
     per_tile = 128 // width
     lane = iota((width, 128), 1) // width
     sums = []
@@ -218,11 +224,8 @@
                 tile, inside = divmod(position + shift, per_tile)
                 if inside != spot:
                     continue
-                term = full[
-                    position * width : (position + 1) * width,
-                    base + tile * 128 : base + (tile + 1) * 128,
-                ]
-                part = term if part is None else part + term
+                one = term(position, tile)
+                part = one if part is None else part + one
             if part is None:
                 continue
             part = jnp.where(lane == spot, part, 0.0)
@@ -231,13 +234,12 @@
     return sums
 
 
-def kernel_grad(full_pairs, outputs, width, taps_per):
+def kernel_grad(terms, outputs, width):
     tiles = []
     lane = iota((width, 128), 1) // width
     pieces = []
-    for full in full_pairs:
-        for tap in range(taps_per):
-            pieces.extend(band_sums(full, tap * WIDE, outputs, width))
+    for term in terms:
+        pieces.extend(band_sums(term, outputs, width))
     per_tile = 128 // width
     for tile in range(2):
         total = jnp.zeros((width, 128), F32)
@@ -255,7 +257,7 @@
     return jnp.concatenate([row, row], axis=1)
 
 
-def plan(states, mats_t, emb_t, heads_t, bias_col, options, legal, games, valid, rewards, returns, scale):
+def plan(states, mats_t, table, bias_col, options, legal, games, valid, rewards, returns, scale):
     frames = states.shape[1]
     pairs = OPTS // 2
     lanes = OPTS * frames
@@ -269,20 +271,20 @@
     chosen = [twice(o) for o in options]
     game = twice(games)
 
-    game_rows = iota((24, WIDE), 0)
+    game_rows = iota((128, WIDE), 0) - HEAD_LANE
     game_pick = jnp.where(
-        game_rows == tiled(game, 3) + GAMES * (iota((24, WIDE), 1) // 128), 1.0, 0.0
-    ).astype(BF)
-    head_rows = dot(heads_t, game_pick)
+        game_rows == tiled(game, 3) + GAMES * (iota((128, WIDE), 1) // 128), 1.0, 0.0
+    )
+    head_rows = dot(table, game_pick.astype(BF))
     hr, hd, hv = (head_rows[:, k * 128 : (k + 1) * 128] for k in range(3))
 
     option_rows = jnp.where(
-        iota((32, lanes), 0) == iota((32, lanes), 1) // frames, 1.0, 0.0
+        iota((128, lanes), 0) - EMB_LANE == iota((128, lanes), 1) // frames, 1.0, 0.0
     ).astype(BF)
     s_low = twice(states)
     s_f = s_low.astype(F32)
     base = dot(trans_in, s_low)
-    pre = tiled(base, pairs) + dot(emb_t, option_rows)
+    pre = tiled(base, pairs) + dot(table, option_rows)
     sig_h = sigmoid(pre)
     hid = pre * sig_h
     hid_low = hid.astype(BF)
@@ -332,8 +334,8 @@
     steps = len(options)
     picks, pre_k, sig_k, hid_k, hid_k_low, judge_k, sig_jk, judged_k = ([None] for _ in range(8))
     for k in range(1, steps):
-        picks.append(jnp.where(iota((32, 128), 0) == chosen[k], 1.0, 0.0).astype(BF))
-        pre_k.append(dot(trans_in, roll_low[k - 1]) + dot(emb_t, picks[k]))
+        picks.append(jnp.where(iota((128, 128), 0) - EMB_LANE == chosen[k], 1.0, 0.0).astype(BF))
+        pre_k.append(dot(trans_in, roll_low[k - 1]) + dot(table, picks[k]))
         sig_k.append(sigmoid(pre_k[k]))
         hid_k.append(pre_k[k] * sig_k[k])
         hid_k_low.append(hid_k[k].astype(BF))
@@ -425,16 +427,14 @@
         with_steps(d_after_low, d_step_low), with_steps(hid_low, hid_k_low), 1, 1
     )
     grad_value = dot(d_judge_cat, with_steps(after_low, roll_low), 1, 1)
-    grad_emb = dot(d_pre_cat, with_steps(option_rows, picks), 1, 1)
-    grad_heads = dot(
-        jnp.concatenate([d_hr, d_hd, d_hv], axis=1), game_pick.astype(F32), 1, 1, precision=HIGH
+    grad_table = dot(d_pre_cat, with_steps(option_rows, picks), 1, 1) + dot(
+        jnp.concatenate([d_hr, d_hd, d_hv], axis=1), game_pick, 1, 1, precision=HIGH
     )
     grad_bias = jnp.sum(d_judge_cat.astype(F32), axis=1, keepdims=True)
     return (
         d_state[:, :frames],
         (grad_in, grad_out, grad_value),
-        grad_emb,
-        grad_heads,
+        grad_table,
         grad_bias,
         errors,
     )
@@ -466,24 +466,40 @@
 def grad_kernel_two(act_one, dz_two, frames):
     rows = OUT2 * frames
     d_two = dz_two[frames : frames + rows]
-    grad = kernel_grad(
-        [dot(d_two, act_one[0:rows], 0, 0), dot(d_two, act_one[frames : frames + rows], 0, 0)],
-        OUT2,
-        C2,
-        2,
-    )
+    full = [dot(d_two, act_one[0:rows], 0, 0), dot(d_two, act_one[frames : frames + rows], 0, 0)]
+
+    def term_of(tap):
+        def term(position, tile):
+            lane = (tap % 2) * WIDE + tile * 128
+            return full[tap // 2][position * C2 : (position + 1) * C2, lane : lane + 128]
+
+        return term
+
+    grad = kernel_grad([term_of(tap) for tap in range(4)], OUT2, C2)
     return grad, fold(tiles_sum(dot(jnp.ones((8, rows), BF), d_two)), C2)
 
 
 def grad_kernel_one(pixels, dz_one, frames):
     rows = OUT1 * frames
     d_one = dz_one[...]
-    grad = kernel_grad(
-        [dot(d_one, pixels[0:rows], 0, 0), dot(d_one, pixels[frames : frames + rows], 0, 0)],
-        OUT1,
-        C1,
-        4,
-    )
+    turned = d_one.T
+
+    def term_of(tap):
+        first = (tap // 4) * frames
+        base = (tap % 4) * WIDE
+        blocks = []
+        for group, (low, high) in enumerate(((0, 256), (128, 384), (256, 384))):
+            left = turned[group * 128 : min((group + 1) * 128, OUT1 * C1)]
+            blocks.append(dot(left, pixels[first : first + rows, base + low : base + high]))
+
+        def term(position, tile):
+            group, inside = divmod(position, 8)
+            lane = (tile - group) * 128
+            return blocks[group][inside * C1 : (inside + 1) * C1, lane : lane + 128]
+
+        return term
+
+    grad = kernel_grad([term_of(tap) for tap in range(8)], OUT1, C1)
     return grad, fold(tiles_sum(dot(jnp.ones((8, rows), BF), d_one)), C1)
 
 
@@ -492,8 +508,7 @@
     kernels_ref,
     linear_ref,
     mats_ref,
-    emb_ref,
-    heads_ref,
+    table_ref,
     bias_ref,
     options_ref,
     legal_ref,
@@ -503,8 +518,7 @@
     returns_ref,
     lin_out,
     mats_out,
-    emb_out,
-    heads_out,
+    table_out,
     conv_out,
     small_out,
     frame_buf,
@@ -524,6 +538,7 @@
     copies = load_frames(frames_hbm, section, frame_buf, sems, CHUNK)
     for copy in copies:
         copy.start()
+    clear_bands(band_one, band_two)
     build_bands(kernels_ref[...], band_one, band_two)
     bias_one, bias_two, bias_three, bias_four = wide_biases(bias_ref[...])
     clear_tails(pixels)
@@ -534,11 +549,10 @@
     encode_two(act_one, band_two, bias_two, z_two, act_two, frames, 3)
     linear_t = linear_ref[...]
     states = (dot(linear_t, act_two[...], 1, 1) + bias_three).astype(BF)
-    d_state, grad_mats, grad_emb, grad_heads, grad_bias, errors = plan(
+    d_state, grad_mats, grad_table, grad_bias, errors = plan(
         states,
         tuple(mats_ref[k] for k in range(3)),
-        emb_ref[:, 0:32],
-        heads_ref[:, 0:24],
+        table_ref[...],
         bias_four,
         *frame_rows(
             section, (options_ref, legal_ref, games_ref, valid_ref, rewards_ref, returns_ref)
@@ -547,8 +561,7 @@
     )
     for k in range(3):
         mats_out[k] = grad_mats[k]
-    emb_out[...] = jnp.concatenate([grad_emb, jnp.zeros((D, 96), F32)], axis=1)
-    heads_out[...] = jnp.concatenate([grad_heads, jnp.zeros((D, 104), F32)], axis=1)
+    table_out[...] = grad_table
     d_state_low = d_state.astype(BF)
     lin_out[...] = dot(d_state_low, act_two[...])
     back_two(d_state_low, linear_t, z_two, dz_two, frames)
@@ -606,14 +619,14 @@
     ]
 
 
-def local_step(frames, kernels, linear_t, mats_t, emb_t, heads_t, biases, options, legal, games, valid, rewards, returns):
+def local_step(frames, kernels, linear_t, mats_t, table, biases, options, legal, games, valid, rewards, returns):
     count = frames.shape[1]
     side = frames.shape[2]
-    shapes = [(D, FEAT), (3, D, D), (D, 128), (D, 128), (KERN, 128), (8, 128)]
+    shapes = [(D, FEAT), (3, D, D), (D, 128), (KERN, 128), (8, 128)]
     return pl.pallas_call(
         local_kernel,
         out_shape=[jax.ShapeDtypeStruct(shape, F32) for shape in shapes],
-        in_specs=[ANY_SPEC] + [VMEM_SPEC] * 12,
+        in_specs=[ANY_SPEC] + [VMEM_SPEC] * 11,
         out_specs=[VMEM_SPEC] * len(shapes),
         scratch_shapes=local_scratch(count, side),
         compiler_params=pltpu.CompilerParams(vmem_limit_bytes=56 * 1024 * 1024),
@@ -622,8 +635,7 @@
         kernels,
         linear_t,
         mats_t,
-        emb_t,
-        heads_t,
+        table,
         biases.reshape(1, BIAS),
         options.transpose(2, 0, 1),
         legal.transpose(2, 0, 1),
@@ -635,13 +647,21 @@
 
 
 MESH = pl.DeviceIdType.MESH
-LIN_PAD = 2688
-QUARTER = 896
+
+
+def packed(value):
+    axis = value.ndim - 2
+    return jnp.concatenate([value[..., 0:QUARTER], value[..., QUARTER:HALF]], axis=axis)
+
+
+QUARTER = 768
 HALF = 2 * QUARTER
+AT_EMB = FEAT
+AT_HEADS = AT_EMB + OPTS
 AT_MATS = LIN_PAD
-AT_EMB = AT_MATS + 3 * D
-AT_HEADS = AT_EMB + 128
-AT_END = AT_HEADS + 128
+TILES = HALF // 128
+NEAR = 8
+FOUR = 4
 
 
 def fused_kernel(
@@ -679,18 +699,23 @@
     weight_msg,
     weights,
     grad_own,
-    grad_mate,
+    mate_msg,
+    mate_in,
     grad_msg,
-    grad_in,
+    near_in,
+    cross_in,
+    cross_msg,
+    far_in,
+    tile_own,
+    tile_mate,
     tile_msg,
     tile_in,
     stats_in,
+    stats_both,
+    stats_base,
     half_in,
-    conv_half_in,
     send_sems,
     recv_sems,
-    all_send,
-    all_recv,
     mate_send,
     mate_recv,
 ):
@@ -698,91 +723,86 @@
     place = lax.axis_index("dp")
     mate = 1 - section
     frames = frame_buf.shape[1]
-    everyone = 2 * peers
 
     barrier = pltpu.get_barrier_semaphore()
 
-    def other(step):
-        flat = lax.rem(section * peers + place + step, everyone)
-        return flat // peers, lax.rem(flat, peers)
-
     def greet(step, carry):
-        to_section, to_place = other(step)
-        pl.semaphore_signal(barrier, inc=1, device_id=(to_section, to_place), device_id_type=MESH)
+        peer = lax.rem(place + step, peers)
+        pl.semaphore_signal(barrier, inc=1, device_id=(section, peer), device_id_type=MESH)
         return carry
 
-    lax.fori_loop(1, everyone, greet, 0)
+    pl.semaphore_signal(barrier, inc=1, device_id=(mate, place), device_id_type=MESH)
+    lax.fori_loop(1, peers, greet, 0)
     copies = load_frames(frames_hbm, section, frame_buf, frame_sems, CHUNK)
+    wait_frames = lambda: [copy.wait() for copy in copies]
     for copy in copies:
         copy.start()
 
-    def to_peer(phase, step, source, target):
-        peer = lax.rem(place + step, peers)
-        return pltpu.make_async_remote_copy(
-            src_ref=source(peer),
-            dst_ref=target.at[place],
-            send_sem=send_sems.at[phase, step],
-            recv_sem=recv_sems.at[phase, place],
+    sends = []
+
+    side, spot = place // NEAR, lax.rem(place, NEAR)
+    row, column = spot // FOUR, lax.rem(spot, FOUR)
+
+    def near(step):
+        return side * NEAR + lax.rem(spot + step, NEAR)
+
+    def beyond(step):
+        return (1 - side) * NEAR + lax.rem(spot + step, NEAR)
+
+    def beside(step):
+        return place - column + lax.rem(column + step, FOUR)
+
+    def across(step, where):
+        return (1 - side) * NEAR + lax.rem(row + step, 2) * FOUR + where
+
+    def send(sems, peer, source, target):
+        pltpu.make_async_remote_copy(
+            src_ref=source,
+            dst_ref=target,
+            send_sem=send_sems.at[sems],
+            recv_sem=recv_sems.at[sems],
             device_id=(section, peer),
             device_id_type=MESH,
-        )
-
-    def from_peer(phase, step, target):
-        peer = lax.rem(place + step, peers)
-        return pltpu.make_async_remote_copy(
-            src_ref=target.at[peer],
-            dst_ref=target.at[peer],
-            send_sem=send_sems.at[phase, step],
-            recv_sem=recv_sems.at[phase, peer],
-            device_id=(section, peer),
-            device_id_type=MESH,
-        )
-
-    def each_peer(act):
+        ).start()
+
+    def loop(low, high, act):
         def body(step, carry):
             act(step)
             return carry
 
-        lax.fori_loop(1, peers, body, 0)
-
-    def to_other(phase, step, source, target):
-        to_section, to_place = other(step)
-        return pltpu.make_async_remote_copy(
-            src_ref=source(to_section, to_place),
-            dst_ref=target.at[section, place],
-            send_sem=all_send.at[phase, step],
-            recv_sem=all_recv.at[phase, section, place],
-            device_id=(to_section, to_place),
-            device_id_type=MESH,
-        )
-
-    def from_other(phase, step, target):
-        its_section, its_place = other(step)
-        return pltpu.make_async_remote_copy(
-            src_ref=target.at[its_section, its_place],
-            dst_ref=target.at[its_section, its_place],
-            send_sem=all_send.at[phase, step],
-            recv_sem=all_recv.at[phase, its_section, its_place],
-            device_id=(its_section, its_place),
-            device_id_type=MESH,
-        )
-
-    def each_other(act):
-        def body(step, carry):
-            act(step)
-            return carry
-
-        lax.fori_loop(1, everyone, body, 0)
-
-    def to_mate(which, source, target):
-        return pltpu.make_async_remote_copy(
-            src_ref=source,
-            dst_ref=target,
-            send_sem=mate_send.at[which],
-            recv_sem=mate_recv.at[which],
+        lax.fori_loop(low, high, body, 0)
+
+    def settle(sems, blocks):
+        whole = pltpu.make_async_remote_copy(
+            src_ref=blocks,
+            dst_ref=blocks,
+            send_sem=send_sems.at[sems],
+            recv_sem=recv_sems.at[sems],
             device_id=(mate, place),
             device_id_type=MESH,
         )
+        sends.append(whole.wait_send)
+        return whole.wait_recv
+
+    def send_peers(sems, source, target):
+        loop(0, NEAR, lambda step: send(sems, beyond(step), source, target.at[place]))
+        loop(1, NEAR, lambda step: send(sems, near(step), source, target.at[place]))
+        return settle(sems, target.at[pl.ds(0, peers - 1)])
+
+    def send_mate(which, source, target, landing):
+        def copy(into):
+            return pltpu.make_async_remote_copy(
+                src_ref=source,
+                dst_ref=into,
+                send_sem=mate_send.at[which],
+                recv_sem=mate_recv.at[which],
+                device_id=(mate, place),
+                device_id_type=MESH,
+            )
+
+        copy(target).start()
+        sends.append(lambda: copy(target).wait_send())
+        return lambda: copy(landing).wait_recv()
 
     upper_lanes = iota((16, 128), 1) >= 64
     counts = sum(
@@ -796,43 +816,73 @@
     ).astype(BF)
     heads_pad = jnp.concatenate([heads_ref[...], jnp.zeros((24, 120), F32)], axis=1)
     heads_pad = jnp.concatenate([heads_pad, jnp.zeros((104, 128), F32)], axis=0).T
-    stage[:, 0:FEAT] = lin_ref[...]
-    stage[:, FEAT:LIN_PAD] = jnp.zeros((8, LIN_PAD - FEAT), F32)
+    last = FEAT - EMB_LANE
+    stage[:, 0:last] = lin_ref[:, 0:last]
+    stage[:, last:LIN_PAD] = jnp.concatenate(
+        [
+            lin_ref[:, last:FEAT],
+            emb_ref[...],
+            heads_pad[0:8, 0 : 3 * GAMES],
+            jnp.zeros((8, 128 - HEAD_LANE - 3 * GAMES), F32),
+        ],
+        axis=1,
+    )
     for k in range(3):
         stage[:, AT_MATS + k * D : AT_MATS + (k + 1) * D] = mats_ref[k]
-    stage[:, AT_EMB:AT_HEADS] = jnp.concatenate(
-        [emb_ref[...], jnp.zeros((8, 128 - OPTS), F32)], axis=1
-    )
-    stage[:, AT_HEADS:AT_END] = heads_pad[0:8]
-    stage[:, AT_END : 2 * HALF] = jnp.zeros((8, 2 * HALF - AT_END), F32)
     first = stage[:, pl.ds(pl.multiple_of(section * HALF, 128), QUARTER)]
     second = stage[:, pl.ds(pl.multiple_of(section * HALF + QUARTER, 128), QUARTER)]
     weight_msg[section, place] = jnp.concatenate([first, second], axis=0).astype(BF)
 
-    pl.semaphore_wait(barrier, everyone - 1)
-    own_kernel = lambda peer: kernel_msg.at[place]
-    own_weight = lambda peer: weight_msg.at[section, place]
-    each_peer(lambda step: to_peer(0, step, own_kernel, kernel_msg).start())
-    each_peer(lambda step: to_peer(1, step, own_weight, weight_msg.at[section]).start())
-
-    bias_one, bias_two, bias_three, bias_four = wide_biases(bias_ref[...])
+    def square_sum(value):
+        return jnp.sum(jnp.sum(value * value, axis=0, keepdims=True), axis=1, keepdims=True)
+
+    weight_squares = [
+        square_sum(conv_pad),
+        square_sum(lin_ref[...]),
+        square_sum(mats_ref[...].reshape(24, D)),
+        square_sum(emb_ref[...]),
+        square_sum(heads_ref[...]),
+    ]
+    stat_line = iota((16, 128), 0)
+    stat = jnp.zeros((16, 128), F32)
+    for which, value in enumerate(weight_squares):
+        at = iota((16, 128), 1) == which
+        rough = value.astype(BF).astype(F32)
+        stat = jnp.where(at & (stat_line == TILES + 1), rough, stat)
+        stat = jnp.where(at & (stat_line == TILES + 2), value - rough, stat)
+    stats_base[...] = stat
+    pl.semaphore_wait(barrier, peers)
+    wait_kernels = send_peers(0, kernel_msg.at[place], kernel_msg)
+    half_msg = weight_msg.at[section]
+    loop(0, 2, lambda step: send(1, across(step, column), half_msg.at[place], half_msg.at[place]))
+    wait_across = settle(1, half_msg.at[pl.ds(0, 2)])
+    loop(1, NEAR, lambda step: send(2, near(step), half_msg.at[place], half_msg.at[place]))
+    wait_near = settle(2, half_msg.at[pl.ds(0, NEAR - 1)])
+
+    clear_bands(band_one, band_two)
+    bias_one, bias_two, bias_three, bias_four = wide_biases(bias_ref[...].reshape(1, BIAS))
     clear_tails(pixels)
     act_two[:, FEAT:LIN_PAD] = jnp.zeros((frames, LIN_PAD - FEAT), BF)
     for which, copy in enumerate(copies):
         copy.wait()
         place_frames(frame_buf, pixels, which * CHUNK, CHUNK, frames)
-    each_peer(lambda step: from_peer(0, step, kernel_msg).wait_recv())
+    wait_kernels()
+    wait_across()
+    for which in range(2):
+        block = half_msg.at[across(which, column)]
+        loop(1, FOUR, lambda step: send(3, beside(step), block, block))
+    wait_beside = settle(3, half_msg.at[pl.ds(0, 2 * (FOUR - 1))])
     kernels = kernel_msg[...].reshape(KERN, 128)
     counted = jnp.where(iota((KERN, 128), 1) >= 64, kernels.astype(F32), 0.0)
     count = jnp.sum(jnp.sum(counted, axis=0, keepdims=True), axis=1, keepdims=True)
     scale = 1.0 / count
     build_bands(kernels, band_one, band_two)
     encode_one(pixels, band_one, bias_one, z_one, act_one, frames, 4)
-    each_peer(lambda step: from_peer(1, step, weight_msg.at[section]).wait_recv())
-    pass_weights = to_mate(0, weight_msg.at[section], weight_msg.at[section])
-    pass_weights.start()
     encode_two(act_one, band_two, bias_two, z_two, act_two, frames, 3)
-    to_mate(0, weight_msg.at[section], weight_msg.at[mate]).wait_recv()
+    wait_near()
+    wait_beside()
+    wait_half = send_mate(0, weight_msg.at[section], weight_msg.at[section], weight_msg.at[mate])
+    wait_half()
     for half in range(2):
         block = weight_msg[half].astype(F32)
         for part in range(2):
@@ -842,11 +892,10 @@
             )
     linear_t = weights[:, 0:LIN_PAD]
     states = (dot(linear_t, act_two[...], 1, 1) + bias_three).astype(BF)
-    d_state, grad_mats, grad_emb, grad_heads, grad_bias, errors = plan(
+    d_state, grad_mats, grad_table, grad_bias, errors = plan(
         states,
         tuple(weights[:, AT_MATS + k * D : AT_MATS + (k + 1) * D] for k in range(3)),
-        weights[:, AT_EMB : AT_EMB + 32],
-        weights[:, AT_HEADS : AT_HEADS + 24],
+        weights[:, LIN_PAD - 128 : LIN_PAD],
         bias_four,
         *frame_rows(
             section, (options_ref, legal_ref, games_ref, valid_ref, rewards_ref, returns_ref)
@@ -857,115 +906,106 @@
     d_state_low = d_state.astype(BF)
     grad_linear = dot(d_state_low, act_two[...])
     grad_own[0] = grad_linear[:, 0:HALF].reshape(peers, 8, HALF)
-    grad_own[1, :, :, 0 : LIN_PAD - HALF] = grad_linear[:, HALF:LIN_PAD].reshape(
-        peers, 8, LIN_PAD - HALF
-    )
-    for k in range(3):
-        lane = AT_MATS - HALF + k * D
-        grad_own[1, :, :, lane : lane + D] = grad_mats[k].reshape(peers, 8, D)
-    lane = AT_EMB - HALF
-    grad_own[1, :, :, lane : lane + 128] = jnp.concatenate(
-        [grad_emb, jnp.zeros((D, 96), F32)], axis=1
-    ).reshape(peers, 8, 128)
-    grad_own[1, :, :, lane + 128 : lane + 256] = jnp.concatenate(
-        [grad_heads, jnp.zeros((D, 104), F32)], axis=1
-    ).reshape(peers, 8, 128)
-    grad_own[1, :, :, lane + 256 : HALF] = jnp.zeros((peers, 8, 2 * HALF - AT_END), F32)
-    pass_grads = to_mate(1, grad_own.at[mate], grad_mate)
-    pass_grads.start()
+    grad_own[1, :, :, 0 : LIN_PAD - 128 - HALF] = grad_linear[:, HALF : LIN_PAD - 128].reshape(
+        peers, 8, LIN_PAD - 128 - HALF
+    )
+    rest = [grad_linear[:, LIN_PAD - 128 : LIN_PAD] + grad_table, *grad_mats]
+    for k in range(4):
+        lane = LIN_PAD - 128 - HALF + k * D
+        grad_own[1, :, :, lane : lane + D] = rest[k].reshape(peers, 8, D)
+    mate_msg[...] = packed(grad_own[mate]).astype(BF)
+    wait_mate = send_mate(1, mate_msg, mate_in, mate_in)
     back_two(d_state_low, linear_t, z_two, dz_two, frames)
     grad_two, bias_two_grad = grad_kernel_two(act_one, dz_two, frames)
-    pass_grads.wait_recv()
-    paired = grad_own[section] + grad_mate[...]
-    grad_msg[...] = jnp.concatenate(
-        [paired[:, :, 0:QUARTER], paired[:, :, QUARTER:HALF]], axis=1
-    ).astype(BF)
-    each_peer(lambda step: to_peer(2, step, lambda peer: grad_msg.at[peer], grad_in).start())
-    grad_in[place] = grad_msg[place]
-    back_one(dz_two, band_two, z_one, dz_one, frames, 5)
-    grad_one, bias_one_grad = grad_kernel_one(pixels, dz_one, frames)
-
-    conv_rows = stack_kernels(grad_one, grad_two).reshape(everyone, 8, 128)
+    wait_mate()
+    grad_msg[...] = (packed(grad_own[section]) + mate_in[...].astype(F32)).astype(BF)
+    for which in range(2):
+
+        def collect(step):
+            peer = beside(step)
+            owner = across(which, lax.rem(peer, FOUR))
+            send(4, peer, grad_msg.at[owner], cross_in.at[which, column])
+
+        loop(1, FOUR, collect)
+        cross_in[which, column] = grad_msg[across(which, column)]
+    wait_cross = settle(4, grad_msg.at[pl.ds(0, 2 * (FOUR - 1))])
+    loop(1, NEAR, lambda step: send(5, near(step), grad_msg.at[near(step)], near_in.at[spot]))
+    wait_grads = settle(5, near_in.at[pl.ds(0, NEAR - 1)])
+    near_in[spot] = grad_msg[place]
     lane = iota((8, 128), 1)
     line = iota((8, 128), 0)
     row_three = row_of(lane_sum(d_state_low))
     row_four = row_of(grad_bias)
+    extra_rows = jnp.zeros((8, 128), F32)
+    for which, entry in (
+        (0, turn(row_three, 64)),
+        (1, row_three),
+        (2, turn(row_four, 64)),
+        (3, row_four),
+        (5, turn(errors, 64)),
+    ):
+        extra_rows = jnp.where(line == which, entry, extra_rows)
+    back_one(dz_two, band_two, z_one, dz_one, frames, 5)
+    grad_one, bias_one_grad = grad_kernel_one(pixels, dz_one, frames)
+    wait_cross()
+    cross_msg[...] = jnp.sum(cross_in[...].astype(F32), axis=1).astype(BF)
+    loop(0, 2, lambda step: send(6, across(step, column), cross_msg.at[step], far_in.at[row]))
+    wait_far = settle(6, far_in)
+
+    conv_rows = stack_kernels(grad_one, grad_two).reshape(2 * peers, 8, 128)
     row_first = jnp.where(
         lane < C1, bias_one_grad, jnp.where(lane < C1 + C2, turn(bias_two_grad, C1), 0.0)
     )
-    rows = [turn(row_three, 64), row_three, turn(row_four, 64), row_four, turn(row_first, 64)[0:1], turn(errors, 64)]
-    extra = jnp.zeros((8, 128), F32)
-    for which, row in enumerate(rows):
-        extra = jnp.where(line == which, row, extra)
-    tiles = jnp.where(iota((everyone, 8, 128), 2) >= 64, extra[None], conv_rows)
-    tile_msg[...] = tiles.reshape(peers, 2, 8, 128)
-    each_other(
-        lambda step: to_other(0, step, lambda s, d: tile_msg.at[d, s], tile_in).start()
-    )
-    tile_in[section, place] = tile_msg[place, section]
-    each_peer(lambda step: from_peer(2, step, grad_in).wait_recv())
-    total = jnp.sum(grad_in[...].astype(F32), axis=0)
+    extra = jnp.where(line == 4, turn(row_first, 64), extra_rows)
+    tiles = jnp.where(iota((2 * peers, 8, 128), 2) >= 64, extra[None], conv_rows)
+    tile_own[0] = tiles.reshape(peers, 2, 8, 128)[:, 0]
+    tile_own[1] = tiles.reshape(peers, 2, 8, 128)[:, 1]
+    wait_pair = send_mate(2, tile_own.at[mate], tile_mate, tile_mate)
+    wait_pair()
+    tile_msg[...] = tile_own[section] + tile_mate[...]
+    loop(
+        0, NEAR, lambda step: send(7, beyond(step), tile_msg.at[beyond(step)], tile_in.at[place])
+    )
+    loop(1, NEAR, lambda step: send(7, near(step), tile_msg.at[near(step)], tile_in.at[place]))
+    wait_tiles = settle(7, tile_in.at[pl.ds(0, peers - 1)])
+    tile_in[place] = tile_msg[place]
+    wait_grads()
+    wait_far()
+    total = jnp.sum(near_in[...].astype(F32), axis=0) + jnp.sum(far_in[...].astype(F32), axis=0)
     squares = total * total
-    stat = jnp.zeros((16, 128), F32)
-    stat_line = iota((16, 128), 0)
+    stat = stats_base[...]
     for part in range(2):
         sums = jnp.sum(squares[part * 8 : (part + 1) * 8], axis=0, keepdims=True)
-        for tile in range(7):
+        for tile in range(TILES // 2):
             stat = jnp.where(
-                stat_line == part * 7 + tile, sums[:, tile * 128 : (tile + 1) * 128], stat
+                stat_line == part * (TILES // 2) + tile, sums[:, tile * 128 : (tile + 1) * 128], stat
             )
-    each_other(lambda step: from_other(0, step, tile_in).wait_recv())
-    tile_total = jnp.sum(tile_in[...].reshape(everyone, 8, 128), axis=0)
+    wait_tiles()
+    tile_total = jnp.sum(tile_in[...], axis=0)
     conv_squares = jnp.where(lane < C1 + C2, tile_total * tile_total, 0.0)
-    stat = jnp.where(stat_line == 14, jnp.sum(conv_squares, axis=0, keepdims=True), stat)
-
-    def square_sum(value):
-        return jnp.sum(jnp.sum(value * value, axis=0, keepdims=True), axis=1, keepdims=True)
-
-    weight_squares = [
-        square_sum(conv_pad),
-        square_sum(lin_ref[...]),
-        sum(square_sum(mats_ref[k]) for k in range(3)),
-        square_sum(emb_ref[...]),
-        square_sum(heads_ref[...]),
-    ]
-    for which, value in enumerate(weight_squares):
-        stat = jnp.where((stat_line == 15) & (iota((16, 128), 1) == which), value, stat)
-    stats_in[section, place] = stat
-    own_half = jnp.concatenate([total[0:8], total[8:16]], axis=1)
-    half_in[section] = own_half
-    conv_half_in[section] = tile_total
-    each_other(
-        lambda step: to_other(
-            1, step, lambda s, d: stats_in.at[section, place], stats_in
-        ).start()
-    )
-    pass_half = to_mate(2, half_in.at[section], half_in.at[section])
-    pass_half.start()
-    pass_conv = to_mate(3, conv_half_in.at[section], conv_half_in.at[section])
-    pass_conv.start()
+    stat = jnp.where(stat_line == TILES, jnp.sum(conv_squares, axis=0, keepdims=True), stat)
+
+    stats_in[place] = stat.astype(BF)
+    half_in[section, :, 0:QUARTER] = total[0:8]
+    half_in[section, :, QUARTER:HALF] = total[8:16]
+    half_in[section, :, HALF : HALF + 128] = tile_total
+    wait_stats = send_peers(8, stats_in.at[place], stats_in)
+    wait_half_grads = send_mate(3, half_in.at[section], half_in.at[section], half_in.at[mate])
     tile_out[...] = tile_total
-    to_mate(2, half_in.at[section], half_in.at[mate]).wait_recv()
-    to_mate(3, conv_half_in.at[section], conv_half_in.at[mate]).wait_recv()
+    wait_stats()
+    stats_both[section] = jnp.sum(stats_in[...].astype(F32), axis=0)
+    wait_half_stats = send_mate(
+        4, stats_both.at[section], stats_both.at[section], stats_both.at[mate]
+    )
+    wait_half_grads()
     for half in range(2):
-        main_out[:, half * HALF : (half + 1) * HALF] = half_in[half]
-        conv_out[half * 8 : (half + 1) * 8] = conv_half_in[half]
-    each_other(lambda step: from_other(1, step, stats_in).wait_recv())
-    stats_out[...] = jnp.sum(stats_in[...], axis=1)
-
-    each_peer(lambda step: to_peer(0, step, own_kernel, kernel_msg).wait_send())
-    each_peer(lambda step: to_peer(1, step, own_weight, weight_msg.at[section]).wait_send())
-    each_peer(lambda step: to_peer(2, step, lambda peer: grad_msg.at[peer], grad_in).wait_send())
-    each_other(
-        lambda step: to_other(0, step, lambda s, d: tile_msg.at[d, s], tile_in).wait_send()
-    )
-    each_other(
-        lambda step: to_other(
-            1, step, lambda s, d: stats_in.at[section, place], stats_in
-        ).wait_send()
-    )
-    for copy in (pass_weights, pass_grads, pass_half, pass_conv):
-        copy.wait_send()
+        main_out[:, half * HALF : (half + 1) * HALF] = half_in[half, :, 0:HALF]
+        conv_out[half * 8 : (half + 1) * 8] = half_in[half, :, HALF : HALF + 128]
+    wait_half_stats()
+    stats_out[...] = stats_both[...]
+
+    for wait in sends:
+        wait()
 
 
 def fused_step(peers, frames, shards, biases, rows):
@@ -979,23 +1019,28 @@
         pltpu.VMEM((2, peers, 16, QUARTER), BF),
         pltpu.VMEM((D, 2 * HALF), BF),
         pltpu.VMEM((2, peers, 8, HALF), F32),
-        pltpu.VMEM((peers, 8, HALF), F32),
         pltpu.VMEM((peers, 16, QUARTER), BF),
         pltpu.VMEM((peers, 16, QUARTER), BF),
-        pltpu.VMEM((peers, 2, 8, 128), F32),
+        pltpu.VMEM((peers, 16, QUARTER), BF),
+        pltpu.VMEM((NEAR, 16, QUARTER), BF),
+        pltpu.VMEM((2, FOUR, 16, QUARTER), BF),
+        pltpu.VMEM((2, 16, QUARTER), BF),
+        pltpu.VMEM((2, 16, QUARTER), BF),
         pltpu.VMEM((2, peers, 8, 128), F32),
-        pltpu.VMEM((2, peers, 16, 128), F32),
-        pltpu.VMEM((2, 8, HALF), F32),
-        pltpu.VMEM((2, 8, 128), F32),
-        pltpu.SemaphoreType.DMA((3, peers)),
-        pltpu.SemaphoreType.DMA((3, peers)),
-        pltpu.SemaphoreType.DMA((2, 2 * peers)),
-        pltpu.SemaphoreType.DMA((2, 2, peers)),
-        pltpu.SemaphoreType.DMA((4,)),
-        pltpu.SemaphoreType.DMA((4,)),
+        pltpu.VMEM((peers, 8, 128), F32),
+        pltpu.VMEM((peers, 8, 128), F32),
+        pltpu.VMEM((peers, 8, 128), F32),
+        pltpu.VMEM((peers, 16, 128), BF),
+        pltpu.VMEM((2, 16, 128), F32),
+        pltpu.VMEM((16, 128), F32),
+        pltpu.VMEM((2, 8, HALF + 128), F32),
+        pltpu.SemaphoreType.DMA((9,)),
+        pltpu.SemaphoreType.DMA((9,)),
+        pltpu.SemaphoreType.DMA((5,)),
+        pltpu.SemaphoreType.DMA((5,)),
     ]
     shapes = [(8, 2 * HALF), (16, 128), (8, 128), (2, 16, 128)]
-    operands = [frames.transpose(0, 2, 1, 3), *shards, biases.reshape(1, BIAS), *rows]
+    operands = [frames.transpose(0, 2, 1, 3), *shards, biases, *rows]
     return pl.pallas_call(
         functools.partial(fused_kernel, peers),
         out_shape=[jax.ShapeDtypeStruct(shape, F32) for shape in shapes],
@@ -1068,9 +1113,9 @@
 ):
     stats = stats_ref[...]
     tile = tile_ref[...]
-    squares = jnp.where(iota((2, 16, 128), 1) < 15, stats, 0.0)
+    squares = jnp.where(iota((2, 16, 128), 1) <= TILES, stats, 0.0)
     squares = total_of(squares[0] + squares[1])
-    scales = 0.5 * (stats[0] + stats[1])[15:16]
+    scales = stats[0, TILES + 1 : TILES + 2] + stats[0, TILES + 2 : TILES + 3]
     bias_raw = jnp.concatenate(
         [tile[4:5, 64 : 64 + C1 + C2]] + [tile[k : k + 1, 64:128] for k in range(4)], axis=1
     )
@@ -1083,9 +1128,8 @@
         new, moment_new = unfactored(
             weight, grad, moment, relative(square_total, weight.size * outs[3])
         )
-        outs[0][...] = new
-        outs[1][...] = grad
-        outs[2][...] = moment_new
+        for out, value in zip(outs, (new, grad, moment_new)):
+            out[...] = value.reshape(out.shape)
         return new
 
     peers = D // lin_ref.shape[0]
@@ -1099,28 +1143,30 @@
     conv_low[...] = conv.astype(BF)
     simple(
         emb_ref[...],
-        factor * main_ref[:, AT_EMB : AT_EMB + OPTS],
+        factor * main_ref[:, AT_EMB:AT_HEADS],
         emb_moment[...],
         scales[:, 3:4],
         (emb_new, emb_grad, emb_moment_new, peers),
     )
-    heads_t = jnp.concatenate([main_ref[:, AT_HEADS:AT_END], jnp.zeros((120, 128), F32)], axis=0).T
+    heads_t = jnp.concatenate(
+        [main_ref[:, LIN_PAD - 128 : LIN_PAD], jnp.zeros((120, 128), F32)], axis=0
+    ).T
     simple(
         heads_ref[...],
-        factor * heads_t[0 : 3 * GAMES, 0:8],
+        factor * heads_t[HEAD_LANE : HEAD_LANE + 3 * GAMES, 0:8],
         head_moment[...],
         scales[:, 4:5],
         (heads_new, heads_grad, head_moment_new, peers),
     )
-    bias = bias_ref[...]
+    bias = bias_ref[...].reshape(1, BIAS)
     simple(
         bias,
         factor * bias_raw,
-        bias_moment[...],
+        bias_moment[...].reshape(1, BIAS),
         total_of(bias * bias),
         (bias_new, bias_grad, bias_moment_new, 1),
     )
-    row_sums = [stats[t // 14, t % 14 : t % 14 + 1] for t in range(24)]
+    row_sums = [stats[t // TILES, t % TILES : t % TILES + 1] for t in range(24)]
 
     def factored(weight, grad, rows_old, cols_old, row_sum, square_total, entries):
         rows = DECAY_RATE * rows_old + (1.0 - DECAY_RATE) * (
@@ -1139,7 +1185,7 @@
     new, rows, cols = factored(
         lin_ref[...],
         grad,
-        lin_rows[...],
+        lin_rows[...].reshape(1, FEAT),
         column_of(lin_cols[...]),
         jnp.concatenate(row_sums[:21], axis=1)[:, 0:FEAT],
         scales[:, 1:2],
@@ -1147,7 +1193,7 @@
     )
     lin_new[...] = new
     lin_grad[...] = grad
-    lin_rows_new[...] = rows
+    lin_rows_new[...] = rows.reshape(FEAT)
     lin_cols_new[...] = row_back(cols)
     lin_low[...] = new.astype(BF)
     for k in range(3):
@@ -1213,22 +1259,22 @@
             returns.transpose(0, 2, 1),
         ),
     )
-    shapes = [(16, 48)] * 3 + [(8, FEAT)] * 2 + [(1, FEAT), (1, 8)] + [(3, 8, D)] * 2 + [(3, D), (3, 8)]
-    shapes += [(8, OPTS)] * 3 + [(24, 8)] * 3 + [(1, BIAS)] * 3 + [(1, 1)] * 2
+    shapes = [(16, 48)] * 3 + [(8, FEAT)] * 2 + [(FEAT,), (1, 8)] + [(3, 8, D)] * 2 + [(3, D), (3, 8)]
+    shapes += [(8, OPTS)] * 3 + [(24, 8)] * 3 + [(BIAS,)] * 3 + [(1, 1)] * 2
     outs = [jax.ShapeDtypeStruct(shape, F32) for shape in shapes]
     outs += [jax.ShapeDtypeStruct((16, 48), BF), jax.ShapeDtypeStruct((8, FEAT), BF)]
     operands = [
         *summed,
         *shards,
-        biases.reshape(1, BIAS),
+        biases,
         conv_moment,
-        lin_rows.reshape(1, FEAT),
+        lin_rows,
         lin_cols.reshape(1, width),
         mats_rows,
         mats_cols,
         emb_moment.T,
         head_moment.reshape(3 * GAMES, width),
-        bias_moment.reshape(1, BIAS),
+        bias_moment,
     ]
     o = pl.pallas_call(
         update_kernel,
@@ -1241,7 +1287,7 @@
         *o[0:3],
         o[3].T,
         o[4].T,
-        o[5].reshape(FEAT),
+        o[5],
         o[6].reshape(width),
         o[7].transpose(0, 2, 1),
         o[8].transpose(0, 2, 1),
@@ -1251,7 +1297,7 @@
         o[12].T,
         o[13].T,
         *flat_heads,
-        *[b.reshape(BIAS) for b in o[17:20]],
+        *o[17:20],
         o[20].reshape(()),
         o[21].reshape(()),
         o[22],
@@ -1311,15 +1357,16 @@
     mats_t = gather_rows(plan_mats.astype(BF).transpose(2, 0, 1)).transpose(1, 0, 2)
     emb_t = gather_rows(option_emb.astype(BF).T)
     heads_t = gather_rows(heads.astype(BF).reshape(3 * GAMES, width).T)
-    emb_t = jnp.pad(emb_t, ((0, 0), (0, 128 - OPTS)))
-    heads_t = jnp.pad(heads_t, ((0, 0), (0, 128 - 3 * GAMES)))
-    lin, mats, emb, hds, conv, small = local_step(
+    table = jnp.pad(
+        jnp.concatenate([emb_t, heads_t], axis=1),
+        ((0, 0), (EMB_LANE, 128 - HEAD_LANE - 3 * GAMES)),
+    )
+    lin, mats, table_grad, conv, small = local_step(
         frames,
         kernels,
         linear_t,
         mats_t,
-        emb_t,
-        heads_t,
+        table,
         biases,
         options,
         legal,
@@ -1329,7 +1376,7 @@
         returns,
     )
     rows = jnp.concatenate(
-        [lin, mats[0], mats[1], mats[2], emb[:, :OPTS], hds[:, : 3 * GAMES]], axis=1
+        [lin, mats[0], mats[1], mats[2], table_grad[:, EMB_LANE : HEAD_LANE + 3 * GAMES]], axis=1
     )
     rows = lax.psum(lax.psum_scatter(rows, "dp", scatter_dimension=0, tiled=True), "section")
     conv = lax.psum(

time: 66.9 us -> 46.4 us (0.69)
  Pallas kernels: 56.9 us -> 45.4 us
  other arithmetic: 5.1 us -> 0 us
  local copies, waits for them, and re-layouts: 3.8 us -> 0 us
    pallas_call x1, Pallas kernels: 54.7 us -> 43.1 us  [fused_step(): pl.pallas_call(functools.partial(fused_kernel, peers), out_shape=[jax.Sha...]
    pallas_call x4 -> x0, other arithmetic: 5.1 us -> none  [fused_device(): pl.pallas_call(update_kernel, out_shape=outs, in_specs=[VMEM_SPEC] * len(...]
    reshape x3 -> x0, local copies, waits for them, and re-layouts: 3.8 us -> none  [the longest x1 1.31 us: fused_device(): lin_rows.reshape(1, FEAT)]
where the time goes in v3:
time: 46.4 us; the launch traced here: 46.2 us
  Pallas kernels  45.4 us (98%)
  between operations  0.83 us (2%)
    pallas_call x1, Pallas kernels, fused_step(): pl.pallas_call(functools.partial(fused_kernel, peers), out_shape=[jax.Sha...  43.1 us
    pallas_call x1, Pallas kernels, fused_device(): pl.pallas_call(update_kernel, out_shape=outs, in_specs=[VMEM_SPEC] * len(...  2.31 us

profile of v3, /device:TPU:0, one launch (start us, length us, event | category | flops | bytes accessed | tf_op | source)
XLA Modules:
  0.0 46.2 jit_solution(14127155575384697557)
XLA Ops:
  0.7 43.1 %shard_map.388 = (f32[8,3072]{1,0:T(8,128)}, f32[16,128]{1,0:T(8,128)}, f32[8,128]{1,0:T(8,128)}, f32[2,16,128]{2,1,0:T(8,128)}) custom-call(bf16[2,84,64,336]{3,2,1,0:T(8,128)(2,1)} %bitcast.27, f32[16,48]{1,0:T(8,128)} %conv_ref.3, f32[8,2592]{1,0:T(8,128)} %bitcast.28, f32[3,8,128]{2,1,0:T(8,128)} %bitcast.30, f32[8,18]{1,0:T(8,128)} %bitcast.35, ...), custom_call_target="tpu_custom_call" | custom-call | tf_op jit(solution)/shard_map/pallas_call | solution.py:1044
  43.8 2.3 %shard_map.389 = (f32[16,48]{1,0:T(8,128)}, f32[16,48]{1,0:T(8,128)}, f32[16,48]{1,0:T(8,128)}, f32[8,2592]{1,0:T(8,128)}, f32[8,2592]{1,0:T(8,128)}, /*index=5*...) custom-call(f32[8,3072]{1,0:T(8,128)} %get-tuple-element.52.main_ref, ...), custom_call_target="tpu_custom_call" | custom-call | tf_op jit(solution)/shard_map/pallas_call | solution.py:1279

commit v4 on v3

--- a/solution.py
+++ b/solution.py
@@ -23,6 +23,7 @@
 EMB_LANE = FEAT % 128
 HEAD_LANE = EMB_LANE + OPTS
 CHUNK = 12
+LATE_POSITIONS = 12
 FEATS_ROW = OUT2 * C2
 
 CLIP_LIMIT = 0.05
@@ -93,38 +94,50 @@
         pixels[block * frames : (block + 1) * frames, part * WIDE : part * WIDE + 336] = frame_buf[row]
 
 
-def build_bands(kernels, band_one, band_two):
+def fill_band(wide, put, width, taps, blocks):
+    per_tile = 128 // width
+    group = iota((width, 128), 1) // width
+    for tap in range(taps):
+        base = 2 * tap * width
+        for block in range(blocks + 1):
+            tile, spot = divmod(block, per_tile)
+            lanes = slice(tile * 128, (tile + 1) * 128)
+            left = jnp.where(group == spot, wide[base : base + width, lanes], 0.0)
+            right = wide[base + width : base + 2 * width]
+            if spot > 0:
+                left = jnp.where(group == spot - 1, right[:, lanes], left)
+            elif block > 0:
+                before = slice((tile - 1) * 128, tile * 128)
+                put(tap, block, before, jnp.where(group == per_tile - 1, right[:, before], 0.0).astype(BF))
+            put(tap, block, lanes, left.astype(BF))
+
+
+def repeat_kernels(kernels, first, width, positions, lanes):
     held = kernels.shape[1]
-    rows48 = iota((held, WIDE), 0)
-    lanes48 = iota((held, WIDE), 1)
-    pick_one = jnp.where((lanes48 % C1 == rows48) & (lanes48 < OUT1 * C1), 1.0, 0.0).astype(BF)
-    pick_two = jnp.where(
-        (lanes48 % C2 + C1 == rows48) & (lanes48 < OUT2 * C2), 1.0, 0.0
-    ).astype(BF)
-    wide_one = dot(kernels, pick_one)
-    wide_two = dot(kernels, pick_two)
-    for wide, band, width, taps, blocks in (
-        (wide_one, band_one, C1, 8, OUT1),
-        (wide_two, band_two, C2, 4, OUT2),
-    ):
-        per_tile = 128 // width
-        group = iota((width, 128), 1) // width
-        for tap in range(taps):
-            base = 2 * tap * width
-            for block in range(blocks + 1):
-                rows = tap * WIDE + block * width
-                tile, spot = divmod(block, per_tile)
-                lanes = slice(tile * 128, (tile + 1) * 128)
-                left = jnp.where(group == spot, wide[base : base + width, lanes], 0.0)
-                right = wide[base + width : base + 2 * width]
-                if spot > 0:
-                    left = jnp.where(group == spot - 1, right[:, lanes], left)
-                elif block > 0:
-                    before = slice((tile - 1) * 128, tile * 128)
-                    band[rows : rows + width, before] = jnp.where(
-                        group == per_tile - 1, right[:, before], 0.0
-                    ).astype(BF)
-                band[rows : rows + width, lanes] = left.astype(BF)
+    rows = iota((held, lanes), 0)
+    cols = iota((held, lanes), 1)
+    pick = jnp.where((cols % width + first == rows) & (cols < positions * width), 1.0, 0.0)
+    return dot(kernels, pick.astype(BF))
+
+
+def build_one(kernels, band):
+    wide = repeat_kernels(kernels, 0, C1, LATE_POSITIONS, 256)
+
+    def put(tap, block, lanes, value):
+        rows = tap * 256 + block * C1
+        band[rows : rows + C1, lanes] = value
+
+    fill_band(wide, put, C1, 4, LATE_POSITIONS)
+
+
+def build_two(kernels, band):
+    wide = repeat_kernels(kernels, C1, C2, OUT2, WIDE)
+
+    def put(tap, block, lanes, value):
+        rows = tap * WIDE + block * C2
+        band[rows : rows + C2, lanes] = value
+
+    fill_band(wide, put, C2, 4, OUT2)
 
 
 def clear_bands(band_one, band_two):
@@ -150,21 +163,28 @@
     )
 
 
-def encode_one(pixels, band_one, bias, z_one, act_one, frames, chunk):
-    half = 4 * WIDE
+def encode_one(pixels, band_one, half, more, bias, z_one, act_one, frames, chunk):
     rows = chunk * frames
+    band = band_one[half]
     for first in range(0, OUT1, chunk):
-        low = first * frames
-        z = dot(pixels[low : low + rows, :], band_one[0:half, :]) + dot(
-            pixels[low + frames : low + frames + rows, :], band_one[half : 2 * half, :]
-        )
-        z = z + bias
-        act = (z * sigmoid(z)).astype(BF)
+        block = pixels[pl.ds(pl.multiple_of((half + first) * frames, frames), rows), :]
+        parts = []
+        for low, wide in ((0, 128), (128, 256)):
+            window = jnp.concatenate(
+                [block[:, tap * WIDE + low : tap * WIDE + low + 256] for tap in range(4)], axis=1
+            )
+            parts.append(dot(window, band[:, 0:wide]))
+        z = jnp.concatenate(parts, axis=1)
         for step in range(chunk):
             at, part = divmod(first + step, 2)
             spot = (slice(at * frames, (at + 1) * frames), slice(part * WIDE, (part + 1) * WIDE))
-            z_one[spot] = z[step * frames : (step + 1) * frames]
-            act_one[spot] = act[step * frames : (step + 1) * frames]
+            z_step = z[step * frames : (step + 1) * frames]
+            if more:
+                z_one[spot] = z_step
+            else:
+                z_step = z_step + z_one[spot] + bias
+                z_one[spot] = z_step
+                act_one[spot] = (z_step * sigmoid(z_step)).astype(BF)
 
 
 def encode_two(act_one, band_two, bias, z_two, act_two, frames, chunk):
@@ -488,13 +508,14 @@
         first = (tap // 4) * frames
         base = (tap % 4) * WIDE
         blocks = []
-        for group, (low, high) in enumerate(((0, 256), (128, 384), (256, 384))):
-            left = turned[group * 128 : min((group + 1) * 128, OUT1 * C1)]
-            blocks.append(dot(left, pixels[first : first + rows, base + low : base + high]))
+        for low, high in ((0, 128), (128, OUT1 * C1)):
+            blocks.append(
+                dot(turned[low:high], pixels[first : first + rows, base + low : base + low + 256])
+            )
 
         def term(position, tile):
-            group, inside = divmod(position, 8)
-            lane = (tile - group) * 128
+            group = min(position // 8, 1)
+            inside, lane = position - 8 * group, (tile - group) * 128
             return blocks[group][inside * C1 : (inside + 1) * C1, lane : lane + 128]
 
         return term
@@ -539,13 +560,17 @@
     for copy in copies:
         copy.start()
     clear_bands(band_one, band_two)
-    build_bands(kernels_ref[...], band_one, band_two)
+    kernels = kernels_ref[...]
+    build_one(kernels[0 : KERN // 2], band_one.at[0])
+    build_one(kernels[KERN // 2 : KERN], band_one.at[1])
+    build_two(kernels, band_two)
     bias_one, bias_two, bias_three, bias_four = wide_biases(bias_ref[...])
     clear_tails(pixels)
     for which, copy in enumerate(copies):
         copy.wait()
         place_frames(frame_buf, pixels, which * CHUNK, CHUNK, frames)
-    encode_one(pixels, band_one, bias_one, z_one, act_one, frames, 4)
+    encode_one(pixels, band_one, 0, True, bias_one, z_one, act_one, frames, 4)
+    encode_one(pixels, band_one, 1, False, bias_one, z_one, act_one, frames, 4)
     encode_two(act_one, band_two, bias_two, z_two, act_two, frames, 3)
     linear_t = linear_ref[...]
     states = (dot(linear_t, act_two[...], 1, 1) + bias_three).astype(BF)
@@ -607,7 +632,7 @@
     return [
         pltpu.VMEM((side, frames, 336), BF),
         pltpu.VMEM(((OUT1 + 1) * frames, 4 * WIDE), BF),
-        pltpu.VMEM((8 * WIDE, WIDE), BF),
+        pltpu.VMEM((2, 4 * 256, 256), BF),
         pltpu.VMEM((4 * WIDE, WIDE), BF),
         pltpu.VMEM((OUT1 // 2 * frames, 2 * WIDE), F32),
         pltpu.VMEM((OUT1 // 2 * frames, 2 * WIDE), BF),
@@ -667,18 +692,18 @@
 def fused_kernel(
     peers,
     frames_hbm,
-    conv_ref,
-    lin_ref,
-    mats_ref,
-    emb_ref,
-    heads_ref,
-    bias_ref,
-    options_ref,
-    legal_ref,
-    games_ref,
-    valid_ref,
-    rewards_ref,
-    returns_ref,
+    conv_hbm,
+    lin_hbm,
+    mats_hbm,
+    emb_hbm,
+    heads_hbm,
+    bias_hbm,
+    options_hbm,
+    legal_hbm,
+    games_hbm,
+    valid_hbm,
+    rewards_hbm,
+    returns_hbm,
     main_out,
     conv_out,
     tile_out,
@@ -718,6 +743,19 @@
     recv_sems,
     mate_send,
     mate_recv,
+    conv_ref,
+    lin_ref,
+    mats_ref,
+    emb_ref,
+    heads_ref,
+    bias_ref,
+    options_ref,
+    legal_ref,
+    games_ref,
+    valid_ref,
+    rewards_ref,
+    returns_ref,
+    operand_sems,
 ):
     section = lax.axis_index("section")
     place = lax.axis_index("dp")
@@ -733,6 +771,27 @@
 
     pl.semaphore_signal(barrier, inc=1, device_id=(mate, place), device_id_type=MESH)
     lax.fori_loop(1, peers, greet, 0)
+    loads = [
+        pltpu.make_async_copy(source, target, operand_sems.at[which])
+        for which, (source, target) in enumerate(
+            (
+                (conv_hbm, conv_ref),
+                (lin_hbm, lin_ref),
+                (mats_hbm, mats_ref),
+                (emb_hbm, emb_ref),
+                (heads_hbm, heads_ref),
+                (bias_hbm, bias_ref),
+                (options_hbm, options_ref),
+                (legal_hbm, legal_ref),
+                (games_hbm, games_ref),
+                (valid_hbm, valid_ref),
+                (rewards_hbm, rewards_ref),
+                (returns_hbm, returns_ref),
+            )
+        )
+    ]
+    for load in loads:
+        load.start()
     copies = load_frames(frames_hbm, section, frame_buf, frame_sems, CHUNK)
     wait_frames = lambda: [copy.wait() for copy in copies]
     for copy in copies:
@@ -804,6 +863,8 @@
         sends.append(lambda: copy(target).wait_send())
         return lambda: copy(landing).wait_recv()
 
+    for load in loads:
+        load.wait()
     upper_lanes = iota((16, 128), 1) >= 64
     counts = sum(
         valid_ref[k, m : m + 1, :].astype(F32)
@@ -852,12 +913,23 @@
         stat = jnp.where(at & (stat_line == TILES + 2), value - rough, stat)
     stats_base[...] = stat
     pl.semaphore_wait(barrier, peers)
-    wait_kernels = send_peers(0, kernel_msg.at[place], kernel_msg)
     half_msg = weight_msg.at[section]
-    loop(0, 2, lambda step: send(1, across(step, column), half_msg.at[place], half_msg.at[place]))
-    wait_across = settle(1, half_msg.at[pl.ds(0, 2)])
-    loop(1, NEAR, lambda step: send(2, near(step), half_msg.at[place], half_msg.at[place]))
-    wait_near = settle(2, half_msg.at[pl.ds(0, NEAR - 1)])
+
+    def spread_own(sems, blocks):
+        own = blocks.at[place]
+        loop(0, 2, lambda step: send(sems, across(step, column), own, own))
+        wait_across = settle(sems, blocks.at[pl.ds(0, 2)])
+        loop(1, NEAR, lambda step: send(sems + 1, near(step), own, own))
+        return wait_across, settle(sems + 1, blocks.at[pl.ds(0, NEAR - 1)])
+
+    def pass_on(sems, blocks):
+        for which in range(2):
+            block = blocks.at[across(which, column)]
+            loop(1, FOUR, lambda step: send(sems, beside(step), block, block))
+        return settle(sems, blocks.at[pl.ds(0, 2 * (FOUR - 1))])
+
+    wait_kernel_across, wait_kernel_near = spread_own(0, kernel_msg)
+    wait_across, wait_near = spread_own(3, half_msg)
 
     clear_bands(band_one, band_two)
     bias_one, bias_two, bias_three, bias_four = wide_biases(bias_ref[...].reshape(1, BIAS))
@@ -866,23 +938,37 @@
     for which, copy in enumerate(copies):
         copy.wait()
         place_frames(frame_buf, pixels, which * CHUNK, CHUNK, frames)
-    wait_kernels()
+    wait_kernel_across()
+    wait_kernel_beside = pass_on(2, kernel_msg)
+    wait_kernel_near()
+
+    def side_kernels(which):
+        return kernel_msg[pl.ds(which * NEAR, NEAR)].reshape(KERN // 2, 128)
+
+    build_one(side_kernels(side), band_one.at[side])
     wait_across()
-    for which in range(2):
-        block = half_msg.at[across(which, column)]
-        loop(1, FOUR, lambda step: send(3, beside(step), block, block))
-    wait_beside = settle(3, half_msg.at[pl.ds(0, 2 * (FOUR - 1))])
+    wait_beside = pass_on(5, half_msg)
+    encode_one(pixels, band_one, side, True, bias_one, z_one, act_one, frames, 4)
+    wait_kernel_beside()
+    build_one(side_kernels(1 - side), band_one.at[1 - side])
     kernels = kernel_msg[...].reshape(KERN, 128)
+    build_two(kernels, band_two)
     counted = jnp.where(iota((KERN, 128), 1) >= 64, kernels.astype(F32), 0.0)
     count = jnp.sum(jnp.sum(counted, axis=0, keepdims=True), axis=1, keepdims=True)
     scale = 1.0 / count
-    build_bands(kernels, band_one, band_two)
-    encode_one(pixels, band_one, bias_one, z_one, act_one, frames, 4)
+    encode_one(pixels, band_one, 1 - side, False, bias_one, z_one, act_one, frames, 4)
+    wait_near()
+    own_side, far_side = pl.ds(side * NEAR, NEAR), pl.ds((1 - side) * NEAR, NEAR)
+    wait_own_side = send_mate(
+        0, half_msg.at[own_side], half_msg.at[own_side], weight_msg.at[mate, own_side]
+    )
     encode_two(act_one, band_two, bias_two, z_two, act_two, frames, 3)
-    wait_near()
     wait_beside()
-    wait_half = send_mate(0, weight_msg.at[section], weight_msg.at[section], weight_msg.at[mate])
-    wait_half()
+    wait_far_side = send_mate(
+        5, half_msg.at[far_side], half_msg.at[far_side], weight_msg.at[mate, far_side]
+    )
+    wait_own_side()
+    wait_far_side()
     for half in range(2):
         block = weight_msg[half].astype(F32)
         for part in range(2):
@@ -916,7 +1002,6 @@
     mate_msg[...] = packed(grad_own[mate]).astype(BF)
     wait_mate = send_mate(1, mate_msg, mate_in, mate_in)
     back_two(d_state_low, linear_t, z_two, dz_two, frames)
-    grad_two, bias_two_grad = grad_kernel_two(act_one, dz_two, frames)
     wait_mate()
     grad_msg[...] = (packed(grad_own[section]) + mate_in[...].astype(F32)).astype(BF)
     for which in range(2):
@@ -924,13 +1009,13 @@
         def collect(step):
             peer = beside(step)
             owner = across(which, lax.rem(peer, FOUR))
-            send(4, peer, grad_msg.at[owner], cross_in.at[which, column])
+            send(6, peer, grad_msg.at[owner], cross_in.at[which, column])
 
         loop(1, FOUR, collect)
         cross_in[which, column] = grad_msg[across(which, column)]
-    wait_cross = settle(4, grad_msg.at[pl.ds(0, 2 * (FOUR - 1))])
-    loop(1, NEAR, lambda step: send(5, near(step), grad_msg.at[near(step)], near_in.at[spot]))
-    wait_grads = settle(5, near_in.at[pl.ds(0, NEAR - 1)])
+    wait_cross = settle(6, grad_msg.at[pl.ds(0, 2 * (FOUR - 1))])
+    loop(1, NEAR, lambda step: send(7, near(step), grad_msg.at[near(step)], near_in.at[spot]))
+    wait_grads = settle(7, near_in.at[pl.ds(0, NEAR - 1)])
     near_in[spot] = grad_msg[place]
     lane = iota((8, 128), 1)
     line = iota((8, 128), 0)
@@ -945,12 +1030,9 @@
         (5, turn(errors, 64)),
     ):
         extra_rows = jnp.where(line == which, entry, extra_rows)
+    grad_two, bias_two_grad = grad_kernel_two(act_one, dz_two, frames)
     back_one(dz_two, band_two, z_one, dz_one, frames, 5)
     grad_one, bias_one_grad = grad_kernel_one(pixels, dz_one, frames)
-    wait_cross()
-    cross_msg[...] = jnp.sum(cross_in[...].astype(F32), axis=1).astype(BF)
-    loop(0, 2, lambda step: send(6, across(step, column), cross_msg.at[step], far_in.at[row]))
-    wait_far = settle(6, far_in)
 
     conv_rows = stack_kernels(grad_one, grad_two).reshape(2 * peers, 8, 128)
     row_first = jnp.where(
@@ -961,13 +1043,17 @@
     tile_own[0] = tiles.reshape(peers, 2, 8, 128)[:, 0]
     tile_own[1] = tiles.reshape(peers, 2, 8, 128)[:, 1]
     wait_pair = send_mate(2, tile_own.at[mate], tile_mate, tile_mate)
+    wait_cross()
+    cross_msg[...] = jnp.sum(cross_in[...].astype(F32), axis=1).astype(BF)
+    loop(0, 2, lambda step: send(8, across(step, column), cross_msg.at[step], far_in.at[row]))
+    wait_far = settle(8, far_in)
     wait_pair()
     tile_msg[...] = tile_own[section] + tile_mate[...]
     loop(
-        0, NEAR, lambda step: send(7, beyond(step), tile_msg.at[beyond(step)], tile_in.at[place])
-    )
-    loop(1, NEAR, lambda step: send(7, near(step), tile_msg.at[near(step)], tile_in.at[place]))
-    wait_tiles = settle(7, tile_in.at[pl.ds(0, peers - 1)])
+        0, NEAR, lambda step: send(9, beyond(step), tile_msg.at[beyond(step)], tile_in.at[place])
+    )
+    loop(1, NEAR, lambda step: send(9, near(step), tile_msg.at[near(step)], tile_in.at[place]))
+    wait_tiles = settle(9, tile_in.at[pl.ds(0, peers - 1)])
     tile_in[place] = tile_msg[place]
     wait_grads()
     wait_far()
@@ -989,7 +1075,7 @@
     half_in[section, :, 0:QUARTER] = total[0:8]
     half_in[section, :, QUARTER:HALF] = total[8:16]
     half_in[section, :, HALF : HALF + 128] = tile_total
-    wait_stats = send_peers(8, stats_in.at[place], stats_in)
+    wait_stats = send_peers(10, stats_in.at[place], stats_in)
     wait_half_grads = send_mate(3, half_in.at[section], half_in.at[section], half_in.at[mate])
     tile_out[...] = tile_total
     wait_stats()
@@ -1034,17 +1120,19 @@
         pltpu.VMEM((2, 16, 128), F32),
         pltpu.VMEM((16, 128), F32),
         pltpu.VMEM((2, 8, HALF + 128), F32),
-        pltpu.SemaphoreType.DMA((9,)),
-        pltpu.SemaphoreType.DMA((9,)),
-        pltpu.SemaphoreType.DMA((5,)),
-        pltpu.SemaphoreType.DMA((5,)),
+        pltpu.SemaphoreType.DMA((11,)),
+        pltpu.SemaphoreType.DMA((11,)),
+        pltpu.SemaphoreType.DMA((6,)),
+        pltpu.SemaphoreType.DMA((6,)),
     ]
     shapes = [(8, 2 * HALF), (16, 128), (8, 128), (2, 16, 128)]
     operands = [frames.transpose(0, 2, 1, 3), *shards, biases, *rows]
+    scratch += [pltpu.VMEM(operand.shape, operand.dtype) for operand in operands[1:]]
+    scratch += [pltpu.SemaphoreType.DMA((len(operands) - 1,))]
     return pl.pallas_call(
         functools.partial(fused_kernel, peers),
         out_shape=[jax.ShapeDtypeStruct(shape, F32) for shape in shapes],
-        in_specs=[ANY_SPEC] + [VMEM_SPEC] * (len(operands) - 1),
+        in_specs=[ANY_SPEC] * len(operands),
         out_specs=[VMEM_SPEC] * len(shapes),
         scratch_shapes=scratch,
         compiler_params=pltpu.CompilerParams(

time: 46.4 us -> 44 us (0.948)
  Pallas kernels: 45.4 us -> 42.9 us
    pallas_call x1, Pallas kernels: 43.1 us -> 40.6 us  [fused_step(): pl.pallas_call(functools.partial(fused_kernel, peers), out_shape=[jax.Sha...]
where the time goes in v4:
time: 44 us; the launch traced here: 43.7 us
  Pallas kernels  42.9 us (98%)
  between operations  0.83 us (2%)
    pallas_call x1, Pallas kernels, fused_step(): pl.pallas_call(functools.partial(fused_kernel, peers), out_shape=[jax.Sha...  40.6 us
    pallas_call x1, Pallas kernels, fused_device(): pl.pallas_call(update_kernel, out_shape=outs, in_specs=[VMEM_SPEC] * len(...  2.31 us

profile of v4, /device:TPU:0, one launch (start us, length us, event | category | flops | bytes accessed | tf_op | source)
XLA Modules:
  0.0 43.7 jit_solution(5528388356647171713)
XLA Ops:
  0.7 40.6 %shard_map.388 = (f32[8,3072]{1,0:T(8,128)}, f32[16,128]{1,0:T(8,128)}, f32[8,128]{1,0:T(8,128)}, f32[2,16,128]{2,1,0:T(8,128)}) custom-call(bf16[2,84,64,336]{3,2,1,0:T(8,128)(2,1)} %bitcast.27, f32[16,48]{1,0:T(8,128)} %conv_ref.1, f32[8,2592]{1,0:T(8,128)} %bitcast.28, f32[3,8,128]{2,1,0:T(8,128)} %bitcast.30, f32[8,18]{1,0:T(8,128)} %bitcast.35, ...), custom_call_target="tpu_custom_call" | custom-call | tf_op jit(solution)/shard_map/pallas_call | solution.py:1132
  41.3 2.3 %shard_map.389 = (f32[16,48]{1,0:T(8,128)}, f32[16,48]{1,0:T(8,128)}, f32[16,48]{1,0:T(8,128)}, f32[8,2592]{1,0:T(8,128)}, f32[8,2592]{1,0:T(8,128)}, /*index=5*...) custom-call(f32[8,3072]{1,0:T(8,128)} %get-tuple-element.52.main_ref, ...), custom_call_target="tpu_custom_call" | custom-call | tf_op jit(solution)/shard_map/pallas_call | solution.py:1367

commit v5 on v4

--- a/solution.py
+++ b/solution.py
@@ -51,8 +51,8 @@
     return 0.5 * jnp.tanh(0.5 * value) + 0.5
 
 
-def slope(value, sigma):
-    return sigma * (1.0 + value * (1.0 - sigma))
+def slope(active, sigma):
+    return sigma + active * (1.0 - sigma)
 
 
 def iota(shape, axis):
@@ -95,21 +95,25 @@
 
 
 def fill_band(wide, put, width, taps, blocks):
+    for tap in taps:
+        fill_tap(wide, put, width, tap, blocks)
+
+
+def fill_tap(wide, put, width, tap, blocks):
     per_tile = 128 // width
     group = iota((width, 128), 1) // width
-    for tap in range(taps):
-        base = 2 * tap * width
-        for block in range(blocks + 1):
-            tile, spot = divmod(block, per_tile)
-            lanes = slice(tile * 128, (tile + 1) * 128)
-            left = jnp.where(group == spot, wide[base : base + width, lanes], 0.0)
-            right = wide[base + width : base + 2 * width]
-            if spot > 0:
-                left = jnp.where(group == spot - 1, right[:, lanes], left)
-            elif block > 0:
-                before = slice((tile - 1) * 128, tile * 128)
-                put(tap, block, before, jnp.where(group == per_tile - 1, right[:, before], 0.0).astype(BF))
-            put(tap, block, lanes, left.astype(BF))
+    base = 2 * tap * width
+    for block in range(blocks + 1):
+        tile, spot = divmod(block, per_tile)
+        lanes = slice(tile * 128, (tile + 1) * 128)
+        left = jnp.where(group == spot, wide[base : base + width, lanes], 0.0)
+        right = wide[base + width : base + 2 * width]
+        if spot > 0:
+            left = jnp.where(group == spot - 1, right[:, lanes], left)
+        elif block > 0:
+            before = slice((tile - 1) * 128, tile * 128)
+            put(tap, block, before, jnp.where(group == per_tile - 1, right[:, before], 0.0).astype(BF))
+        put(tap, block, lanes, left.astype(BF))
 
 
 def repeat_kernels(kernels, first, width, positions, lanes):
@@ -127,7 +131,7 @@
         rows = tap * 256 + block * C1
         band[rows : rows + C1, lanes] = value
 
-    fill_band(wide, put, C1, 4, LATE_POSITIONS)
+    fill_band(wide, put, C1, range(4), LATE_POSITIONS)
 
 
 def build_two(kernels, band):
@@ -137,7 +141,7 @@
         rows = tap * WIDE + block * C2
         band[rows : rows + C2, lanes] = value
 
-    fill_band(wide, put, C2, 4, OUT2)
+    return [lambda tap=tap: fill_tap(wide, put, C2, tap, OUT2) for tap in range(4)]
 
 
 def clear_bands(band_one, band_two):
@@ -163,7 +167,9 @@
     )
 
 
-def encode_one(pixels, band_one, half, more, bias, z_one, act_one, frames, chunk):
+def encode_one(
+    pixels, band_one, half, more, bias, slope_one, act_one, frames, chunk, beside=()
+):
     rows = chunk * frames
     band = band_one[half]
     for first in range(0, OUT1, chunk):
@@ -174,56 +180,100 @@
                 [block[:, tap * WIDE + low : tap * WIDE + low + 256] for tap in range(4)], axis=1
             )
             parts.append(dot(window, band[:, 0:wide]))
+        if first // chunk < len(beside):
+            beside[first // chunk]()
         z = jnp.concatenate(parts, axis=1)
         for step in range(chunk):
             at, part = divmod(first + step, 2)
             spot = (slice(at * frames, (at + 1) * frames), slice(part * WIDE, (part + 1) * WIDE))
             z_step = z[step * frames : (step + 1) * frames]
             if more:
-                z_one[spot] = z_step
+                slope_one[spot] = z_step
             else:
-                z_step = z_step + z_one[spot] + bias
-                z_one[spot] = z_step
-                act_one[spot] = (z_step * sigmoid(z_step)).astype(BF)
-
-
-def encode_two(act_one, band_two, bias, z_two, act_two, frames, chunk):
-    half = 2 * WIDE
+                z_step = z_step + slope_one[spot] + bias
+                sigma = sigmoid(z_step)
+                active = z_step * sigma
+                slope_one[spot] = slope(active, sigma)
+                act_one[spot] = active.astype(BF)
+
+
+def encode_two(act_one, band_two, bias, slope_two, act_two, frames, chunk):
     rows = chunk * frames
+    bands = []
+    for low, high in ((0, 128), (128, WIDE)):
+        bands.append(
+            jnp.concatenate(
+                [band_two[tap * WIDE + low : tap * WIDE + low + 256, low:high] for tap in range(4)],
+                axis=0,
+            )
+        )
     for first in range(0, OUT2, chunk):
-        low = first * frames
-        z = dot(act_one[low : low + rows, :], band_two[0:half, :]) + dot(
-            act_one[low + frames : low + frames + rows, :], band_two[half : 2 * half, :]
-        )
-        z = z + bias
-        z_two[low : low + rows] = z
-        act = (z * sigmoid(z)).astype(BF)
+        at = first * frames
+        parts = []
+        for low, band in zip((0, 128), bands):
+            window = jnp.concatenate(
+                [
+                    act_one[
+                        at + tap // 2 * frames : at + tap // 2 * frames + rows,
+                        tap % 2 * WIDE + low : tap % 2 * WIDE + low + 256,
+                    ]
+                    for tap in range(4)
+                ],
+                axis=1,
+            )
+            parts.append(dot(window, band))
+        z = jnp.concatenate(parts, axis=1) + bias
+        sigma = sigmoid(z)
+        active = z * sigma
+        slope_two[at : at + rows] = slope(active, sigma)
+        act = active.astype(BF)
         for step in range(chunk):
-            at = (first + step) * FEATS_ROW
-            act_two[:, at : at + FEATS_ROW] = act[step * frames : (step + 1) * frames, :FEATS_ROW]
-
-
-def back_two(dstate_t, linear_t, z_two, dz_two, frames):
+            lane = (first + step) * FEATS_ROW
+            act_two[:, lane : lane + FEATS_ROW] = act[step * frames : (step + 1) * frames, :FEATS_ROW]
+
+
+def back_two(dstate_t, linear_t, slope_two, dz_two, frames):
     dact = dot(dstate_t, linear_t, 0, 0)
     dz_two[0:frames] = jnp.zeros((frames, WIDE), BF)
     dz_two[(OUT2 + 1) * frames : (OUT2 + 2) * frames] = jnp.zeros((frames, WIDE), BF)
     blank = jnp.zeros((frames, WIDE - FEATS_ROW), F32)
     for at in range(OUT2):
-        z = z_two[at * frames : (at + 1) * frames]
         part = jnp.concatenate([dact[:, at * FEATS_ROW : (at + 1) * FEATS_ROW], blank], axis=1)
-        dz_two[(at + 1) * frames : (at + 2) * frames] = (part * slope(z, sigmoid(z))).astype(BF)
-
-
-def back_one(dz_two, band_two, z_one, dz_one, frames, chunk):
-    half = 2 * WIDE
+        dz_two[(at + 1) * frames : (at + 2) * frames] = (
+            part * slope_two[at * frames : (at + 1) * frames]
+        ).astype(BF)
+
+
+def back_one(dz_two, band_two, slope_one, dz_one, frames, chunk):
     rows = chunk * frames
+
+    def rows_of(tap, low, high):
+        return slice(tap * WIDE + low, tap * WIDE + high)
+
     for first in range(0, OUT1 // 2, chunk):
         low = first * frames
-        dact = dot(dz_two[low + frames : low + frames + rows], band_two[0:half], 1, 1) + dot(
-            dz_two[low : low + rows], band_two[half : 2 * half], 1, 1
+        sides = [dz_two[low + frames : low + frames + rows], dz_two[low : low + rows]]
+        left = [
+            sum(
+                dot(sides[at][:, 0:256], band_two[rows_of(2 * at + part, 0, 256), 0:256], 1, 1)
+                for at in range(2)
+            )
+            for part in range(2)
+        ]
+        right = sum(
+            dot(
+                sides[at][:, 128:WIDE],
+                jnp.concatenate(
+                    [band_two[rows_of(2 * at + part, 256, WIDE), 128:WIDE] for part in range(2)],
+                    axis=0,
+                ),
+                1,
+                1,
+            )
+            for at in range(2)
         )
-        z = z_one[low : low + rows]
-        dz = (dact * slope(z, sigmoid(z))).astype(BF)
+        dact = jnp.concatenate([left[0], right[:, 0:128], left[1], right[:, 128:256]], axis=1)
+        dz = (dact * slope_one[low : low + rows]).astype(BF)
         for step in range(chunk):
             for part in range(2):
                 at = (2 * (first + step) + part) * frames
@@ -388,12 +438,12 @@
     d_hd = jnp.zeros((D, 128), F32)
     d_hv = jnp.zeros((D, 128), F32)
     for k in range(steps - 1, 0, -1):
-        d_judge_low[k] = (d_value_k[k] * hv * slope(judge_k[k], sig_jk[k])).astype(BF)
+        d_judge_low[k] = (d_value_k[k] * hv * slope(judged_k[k], sig_jk[k])).astype(BF)
         term = through(value_in, d_judge_low[k])
         d_roll = term if d_roll is None else d_roll + term
         d_step_low[k] = d_roll.astype(BF)
         d_hid = through(trans_out, d_step_low[k]) + d_reward_k[k] * hr
-        d_pre_low[k] = (d_hid * slope(pre_k[k], sig_k[k])).astype(BF)
+        d_pre_low[k] = (d_hid * slope(hid_k[k], sig_k[k])).astype(BF)
         d_roll = d_roll + through(trans_in, d_pre_low[k])
         d_hr = d_hr + (half * d_reward_k[k]) * hid_k[k]
         d_hv = d_hv + (half * d_value_k[k]) * judged_k[k]
@@ -407,7 +457,7 @@
     ]
     d_gamma = [d_backed[k] * value[k] * gamma[k] * (1.0 - gamma[k]) for k in range(pairs)]
     d_judge = [
-        (d_value[k] * hv * slope(tile_of(judge_pre, k), tile_of(sig_j, k))).astype(BF)
+        (d_value[k] * hv * slope(tile_of(judged, k), tile_of(sig_j, k))).astype(BF)
         for k in range(pairs)
     ]
     d_judge_all = jnp.concatenate(d_judge, axis=1)
@@ -420,7 +470,7 @@
     d_pre = [
         (
             (tile_of(d_hid_all, k) + d_reward[k] * hr + d_gamma[k] * hd)
-            * slope(tile_of(pre, k), tile_of(sig_h, k))
+            * slope(tile_of(hid, k), tile_of(sig_h, k))
         ).astype(BF)
         for k in range(pairs)
     ]
@@ -486,12 +536,20 @@
 def grad_kernel_two(act_one, dz_two, frames):
     rows = OUT2 * frames
     d_two = dz_two[frames : frames + rows]
-    full = [dot(d_two, act_one[0:rows], 0, 0), dot(d_two, act_one[frames : frames + rows], 0, 0)]
+    turned = d_two.T
 
     def term_of(tap):
+        first, base = (tap // 2) * frames, (tap % 2) * WIDE
+        blocks = []
+        for low, high in ((0, 128), (128, OUT2 * C2)):
+            blocks.append(
+                dot(turned[low:high], act_one[first : first + rows, base + low : base + low + 256])
+            )
+
         def term(position, tile):
-            lane = (tap % 2) * WIDE + tile * 128
-            return full[tap // 2][position * C2 : (position + 1) * C2, lane : lane + 128]
+            group = min(position // 4, 1)
+            inside, lane = position - 4 * group, (tile - group) * 128
+            return blocks[group][inside * C2 : (inside + 1) * C2, lane : lane + 128]
 
         return term
 
@@ -546,9 +604,9 @@
     pixels,
     band_one,
     band_two,
-    z_one,
+    slope_one,
     act_one,
-    z_two,
+    slope_two,
     act_two,
     dz_two,
     dz_one,
@@ -563,15 +621,16 @@
     kernels = kernels_ref[...]
     build_one(kernels[0 : KERN // 2], band_one.at[0])
     build_one(kernels[KERN // 2 : KERN], band_one.at[1])
-    build_two(kernels, band_two)
+    for fill in build_two(kernels, band_two):
+        fill()
     bias_one, bias_two, bias_three, bias_four = wide_biases(bias_ref[...])
     clear_tails(pixels)
     for which, copy in enumerate(copies):
         copy.wait()
         place_frames(frame_buf, pixels, which * CHUNK, CHUNK, frames)
-    encode_one(pixels, band_one, 0, True, bias_one, z_one, act_one, frames, 4)
-    encode_one(pixels, band_one, 1, False, bias_one, z_one, act_one, frames, 4)
-    encode_two(act_one, band_two, bias_two, z_two, act_two, frames, 3)
+    encode_one(pixels, band_one, 0, True, bias_one, slope_one, act_one, frames, 4)
+    encode_one(pixels, band_one, 1, False, bias_one, slope_one, act_one, frames, 4)
+    encode_two(act_one, band_two, bias_two, slope_two, act_two, frames, 3)
     linear_t = linear_ref[...]
     states = (dot(linear_t, act_two[...], 1, 1) + bias_three).astype(BF)
     d_state, grad_mats, grad_table, grad_bias, errors = plan(
@@ -589,9 +648,9 @@
     table_out[...] = grad_table
     d_state_low = d_state.astype(BF)
     lin_out[...] = dot(d_state_low, act_two[...])
-    back_two(d_state_low, linear_t, z_two, dz_two, frames)
+    back_two(d_state_low, linear_t, slope_two, dz_two, frames)
     grad_two, bias_two_grad = grad_kernel_two(act_one, dz_two, frames)
-    back_one(dz_two, band_two, z_one, dz_one, frames, 5)
+    back_one(dz_two, band_two, slope_one, dz_one, frames, 5)
     grad_one, bias_one_grad = grad_kernel_one(pixels, dz_one, frames)
     conv_out[...] = stack_kernels(grad_one, grad_two)
     lane = iota((8, 128), 1)
@@ -674,17 +733,13 @@
 MESH = pl.DeviceIdType.MESH
 
 
-def packed(value):
-    axis = value.ndim - 2
-    return jnp.concatenate([value[..., 0:QUARTER], value[..., QUARTER:HALF]], axis=axis)
-
-
 QUARTER = 768
 HALF = 2 * QUARTER
 AT_EMB = FEAT
 AT_HEADS = AT_EMB + OPTS
 AT_MATS = LIN_PAD
 TILES = HALF // 128
+SCALE_LANE = C1 + C2
 NEAR = 8
 FOUR = 4
 
@@ -706,15 +761,14 @@
     returns_hbm,
     main_out,
     conv_out,
-    tile_out,
     stats_out,
     frame_buf,
     pixels,
     band_one,
     band_two,
-    z_one,
+    slope_one,
     act_one,
-    z_two,
+    slope_two,
     act_two,
     dz_two,
     dz_one,
@@ -724,19 +778,18 @@
     weight_msg,
     weights,
     grad_own,
-    mate_msg,
     mate_in,
     grad_msg,
     near_in,
     cross_in,
     cross_msg,
     far_in,
-    tile_own,
-    tile_mate,
-    tile_msg,
-    tile_in,
+    taps_msg,
+    row_in,
+    rows_in,
+    taps_turned,
     stats_in,
-    stats_both,
+    final,
     stats_base,
     half_in,
     send_sems,
@@ -769,8 +822,13 @@
         pl.semaphore_signal(barrier, inc=1, device_id=(section, peer), device_id_type=MESH)
         return carry
 
-    pl.semaphore_signal(barrier, inc=1, device_id=(mate, place), device_id_type=MESH)
+    def greet_row(step, carry):
+        peer = place - lax.rem(place, FOUR) + lax.rem(place + step, FOUR)
+        pl.semaphore_signal(barrier, inc=1, device_id=(mate, peer), device_id_type=MESH)
+        return carry
+
     lax.fori_loop(1, peers, greet, 0)
+    lax.fori_loop(0, FOUR, greet_row, 0)
     loads = [
         pltpu.make_async_copy(source, target, operand_sems.at[which])
         for which, (source, target) in enumerate(
@@ -814,13 +872,13 @@
     def across(step, where):
         return (1 - side) * NEAR + lax.rem(row + step, 2) * FOUR + where
 
-    def send(sems, peer, source, target):
+    def send(sems, peer, source, target, core=section):
         pltpu.make_async_remote_copy(
             src_ref=source,
             dst_ref=target,
             send_sem=send_sems.at[sems],
             recv_sem=recv_sems.at[sems],
-            device_id=(section, peer),
+            device_id=(core, peer),
             device_id_type=MESH,
         ).start()
 
@@ -907,12 +965,13 @@
     stat_line = iota((16, 128), 0)
     stat = jnp.zeros((16, 128), F32)
     for which, value in enumerate(weight_squares):
-        at = iota((16, 128), 1) == which
+        at = iota((16, 128), 1) - SCALE_LANE
         rough = value.astype(BF).astype(F32)
-        stat = jnp.where(at & (stat_line == TILES + 1), rough, stat)
-        stat = jnp.where(at & (stat_line == TILES + 2), value - rough, stat)
+        mixed = stat_line == TILES + 2
+        stat = jnp.where(mixed & (at == which), rough, stat)
+        stat = jnp.where(mixed & (at == which + 5), value - rough, stat)
     stats_base[...] = stat
-    pl.semaphore_wait(barrier, peers)
+    pl.semaphore_wait(barrier, peers - 1 + FOUR)
     half_msg = weight_msg.at[section]
 
     def spread_own(sems, blocks):
@@ -948,25 +1007,25 @@
     build_one(side_kernels(side), band_one.at[side])
     wait_across()
     wait_beside = pass_on(5, half_msg)
-    encode_one(pixels, band_one, side, True, bias_one, z_one, act_one, frames, 4)
+    encode_one(pixels, band_one, side, True, bias_one, slope_one, act_one, frames, 4)
     wait_kernel_beside()
     build_one(side_kernels(1 - side), band_one.at[1 - side])
     kernels = kernel_msg[...].reshape(KERN, 128)
-    build_two(kernels, band_two)
+    fills = build_two(kernels, band_two)
     counted = jnp.where(iota((KERN, 128), 1) >= 64, kernels.astype(F32), 0.0)
     count = jnp.sum(jnp.sum(counted, axis=0, keepdims=True), axis=1, keepdims=True)
     scale = 1.0 / count
-    encode_one(pixels, band_one, 1 - side, False, bias_one, z_one, act_one, frames, 4)
+    encode_one(pixels, band_one, 1 - side, False, bias_one, slope_one, act_one, frames, 4, fills)
     wait_near()
     own_side, far_side = pl.ds(side * NEAR, NEAR), pl.ds((1 - side) * NEAR, NEAR)
     wait_own_side = send_mate(
         0, half_msg.at[own_side], half_msg.at[own_side], weight_msg.at[mate, own_side]
     )
-    encode_two(act_one, band_two, bias_two, z_two, act_two, frames, 3)
     wait_beside()
     wait_far_side = send_mate(
         5, half_msg.at[far_side], half_msg.at[far_side], weight_msg.at[mate, far_side]
     )
+    encode_two(act_one, band_two, bias_two, slope_two, act_two, frames, 3)
     wait_own_side()
     wait_far_side()
     for half in range(2):
@@ -991,19 +1050,24 @@
 
     d_state_low = d_state.astype(BF)
     grad_linear = dot(d_state_low, act_two[...])
-    grad_own[0] = grad_linear[:, 0:HALF].reshape(peers, 8, HALF)
-    grad_own[1, :, :, 0 : LIN_PAD - 128 - HALF] = grad_linear[:, HALF : LIN_PAD - 128].reshape(
-        peers, 8, LIN_PAD - 128 - HALF
-    )
-    rest = [grad_linear[:, LIN_PAD - 128 : LIN_PAD] + grad_table, *grad_mats]
-    for k in range(4):
-        lane = LIN_PAD - 128 - HALF + k * D
-        grad_own[1, :, :, lane : lane + D] = rest[k].reshape(peers, 8, D)
-    mate_msg[...] = packed(grad_own[mate]).astype(BF)
-    wait_mate = send_mate(1, mate_msg, mate_in, mate_in)
-    back_two(d_state_low, linear_t, z_two, dz_two, frames)
+    parts = [grad_linear[:, at * QUARTER : (at + 1) * QUARTER] for at in range(3)]
+    parts.append(
+        jnp.concatenate(
+            [
+                grad_linear[:, 3 * QUARTER : LIN_PAD - 128],
+                grad_linear[:, LIN_PAD - 128 : LIN_PAD] + grad_table,
+                *grad_mats,
+            ],
+            axis=1,
+        )
+    )
+    parts = [part.reshape(peers, 8, QUARTER) for part in parts]
+    for half in range(2):
+        grad_own[half] = jnp.concatenate(parts[2 * half : 2 * half + 2], axis=1).astype(BF)
+    wait_mate = send_mate(1, grad_own.at[mate], mate_in, mate_in)
+    back_two(d_state_low, linear_t, slope_two, dz_two, frames)
     wait_mate()
-    grad_msg[...] = (packed(grad_own[section]) + mate_in[...].astype(F32)).astype(BF)
+    grad_msg[...] = (grad_own[section].astype(F32) + mate_in[...].astype(F32)).astype(BF)
     for which in range(2):
 
         def collect(step):
@@ -1017,44 +1081,35 @@
     loop(1, NEAR, lambda step: send(7, near(step), grad_msg.at[near(step)], near_in.at[spot]))
     wait_grads = settle(7, near_in.at[pl.ds(0, NEAR - 1)])
     near_in[spot] = grad_msg[place]
-    lane = iota((8, 128), 1)
-    line = iota((8, 128), 0)
     row_three = row_of(lane_sum(d_state_low))
     row_four = row_of(grad_bias)
-    extra_rows = jnp.zeros((8, 128), F32)
-    for which, entry in (
-        (0, turn(row_three, 64)),
-        (1, row_three),
-        (2, turn(row_four, 64)),
-        (3, row_four),
-        (5, turn(errors, 64)),
-    ):
-        extra_rows = jnp.where(line == which, entry, extra_rows)
     grad_two, bias_two_grad = grad_kernel_two(act_one, dz_two, frames)
-    back_one(dz_two, band_two, z_one, dz_one, frames, 5)
+    back_one(dz_two, band_two, slope_one, dz_one, frames, 5)
     grad_one, bias_one_grad = grad_kernel_one(pixels, dz_one, frames)
 
-    conv_rows = stack_kernels(grad_one, grad_two).reshape(2 * peers, 8, 128)
-    row_first = jnp.where(
-        lane < C1, bias_one_grad, jnp.where(lane < C1 + C2, turn(bias_two_grad, C1), 0.0)
-    )
-    extra = jnp.where(line == 4, turn(row_first, 64), extra_rows)
-    tiles = jnp.where(iota((2 * peers, 8, 128), 2) >= 64, extra[None], conv_rows)
-    tile_own[0] = tiles.reshape(peers, 2, 8, 128)[:, 0]
-    tile_own[1] = tiles.reshape(peers, 2, 8, 128)[:, 1]
-    wait_pair = send_mate(2, tile_own.at[mate], tile_mate, tile_mate)
+    kernel_grads = jnp.concatenate([grad_one, grad_two], axis=0).astype(BF)
+    for half in range(2):
+        taps_msg[half] = kernel_grads[:, half * 128 : (half + 1) * 128]
+    own = section * FOUR + column
+    loop(1, FOUR, lambda step: send(9, beside(step), taps_msg.at[section], row_in.at[own]))
+    loop(0, FOUR, lambda step: send(9, beside(step), taps_msg.at[mate], row_in.at[own], mate))
+    wait_row = settle(9, row_in.at[pl.ds(0, 2 * FOUR - 1)])
+    row_in[own] = taps_msg[section]
     wait_cross()
     cross_msg[...] = jnp.sum(cross_in[...].astype(F32), axis=1).astype(BF)
     loop(0, 2, lambda step: send(8, across(step, column), cross_msg.at[step], far_in.at[row]))
     wait_far = settle(8, far_in)
-    wait_pair()
-    tile_msg[...] = tile_own[section] + tile_mate[...]
+    wait_row()
+    level = place // FOUR
+    rows_in[level] = jnp.sum(row_in[...].astype(F32), axis=0).astype(BF)
     loop(
-        0, NEAR, lambda step: send(9, beyond(step), tile_msg.at[beyond(step)], tile_in.at[place])
-    )
-    loop(1, NEAR, lambda step: send(9, near(step), tile_msg.at[near(step)], tile_in.at[place]))
-    wait_tiles = settle(9, tile_in.at[pl.ds(0, peers - 1)])
-    tile_in[place] = tile_msg[place]
+        1,
+        peers // FOUR,
+        lambda step: send(
+            11, lax.rem(place + step * FOUR, peers), rows_in.at[level], rows_in.at[level]
+        ),
+    )
+    wait_rows = settle(11, rows_in.at[pl.ds(0, peers // FOUR - 1)])
     wait_grads()
     wait_far()
     total = jnp.sum(near_in[...].astype(F32), axis=0) + jnp.sum(far_in[...].astype(F32), axis=0)
@@ -1066,29 +1121,36 @@
             stat = jnp.where(
                 stat_line == part * (TILES // 2) + tile, sums[:, tile * 128 : (tile + 1) * 128], stat
             )
-    wait_tiles()
-    tile_total = jnp.sum(tile_in[...], axis=0)
-    conv_squares = jnp.where(lane < C1 + C2, tile_total * tile_total, 0.0)
-    stat = jnp.where(stat_line == TILES, jnp.sum(conv_squares, axis=0, keepdims=True), stat)
-
+    lane = iota((1, 128), 1)
+    row_first = jnp.where(
+        lane < C1, bias_one_grad[0:1], jnp.where(lane < C1 + C2, turn(bias_two_grad, C1)[0:1], 0.0)
+    )
+    row_first = row_first + turn(errors, 64)
+    stat = jnp.where(stat_line == TILES, row_three, stat)
+    stat = jnp.where(stat_line == TILES + 1, row_four, stat)
+    stat = stat + jnp.where(stat_line == TILES + 2, row_first, 0.0)
     stats_in[place] = stat.astype(BF)
+    wait_stats = send_peers(10, stats_in.at[place], stats_in)
     half_in[section, :, 0:QUARTER] = total[0:8]
     half_in[section, :, QUARTER:HALF] = total[8:16]
-    half_in[section, :, HALF : HALF + 128] = tile_total
-    wait_stats = send_peers(10, stats_in.at[place], stats_in)
     wait_half_grads = send_mate(3, half_in.at[section], half_in.at[section], half_in.at[mate])
-    tile_out[...] = tile_total
-    wait_stats()
-    stats_both[section] = jnp.sum(stats_in[...].astype(F32), axis=0)
-    wait_half_stats = send_mate(
-        4, stats_both.at[section], stats_both.at[section], stats_both.at[mate]
+    wait_rows()
+    taps = jnp.sum(rows_in[...].astype(F32), axis=0)
+    taps = jnp.concatenate([taps, jnp.zeros((128 - C1 - C2, 128), F32)], axis=0)
+    taps_turned[...] = taps.T
+    final[section, 16:32] = taps_turned[pl.ds(pl.multiple_of(spot * 16, 16), 16)]
+    final[section, 32:40] = jnp.broadcast_to(
+        jnp.sum(taps * taps, axis=0, keepdims=True), (8, 128)
     )
     wait_half_grads()
     for half in range(2):
-        main_out[:, half * HALF : (half + 1) * HALF] = half_in[half, :, 0:HALF]
-        conv_out[half * 8 : (half + 1) * 8] = half_in[half, :, HALF : HALF + 128]
-    wait_half_stats()
-    stats_out[...] = stats_both[...]
+        main_out[:, half * HALF : (half + 1) * HALF] = half_in[half]
+    wait_stats()
+    final[section, 0:16] = jnp.sum(stats_in[...].astype(F32), axis=0)
+    wait_final = send_mate(4, final.at[section], final.at[section], final.at[mate])
+    wait_final()
+    conv_out[...] = final[side, 16:32]
+    stats_out[...] = final[...]
 
     for wait in sends:
         wait()
@@ -1104,28 +1166,27 @@
         pltpu.VMEM((peers, 16, 128), BF),
         pltpu.VMEM((2, peers, 16, QUARTER), BF),
         pltpu.VMEM((D, 2 * HALF), BF),
-        pltpu.VMEM((2, peers, 8, HALF), F32),
-        pltpu.VMEM((peers, 16, QUARTER), BF),
+        pltpu.VMEM((2, peers, 16, QUARTER), BF),
         pltpu.VMEM((peers, 16, QUARTER), BF),
         pltpu.VMEM((peers, 16, QUARTER), BF),
         pltpu.VMEM((NEAR, 16, QUARTER), BF),
         pltpu.VMEM((2, FOUR, 16, QUARTER), BF),
         pltpu.VMEM((2, 16, QUARTER), BF),
         pltpu.VMEM((2, 16, QUARTER), BF),
-        pltpu.VMEM((2, peers, 8, 128), F32),
-        pltpu.VMEM((peers, 8, 128), F32),
-        pltpu.VMEM((peers, 8, 128), F32),
-        pltpu.VMEM((peers, 8, 128), F32),
+        pltpu.VMEM((2, C1 + C2, 128), BF),
+        pltpu.VMEM((2 * FOUR, C1 + C2, 128), BF),
+        pltpu.VMEM((peers // FOUR, C1 + C2, 128), BF),
+        pltpu.VMEM((128, 128), F32),
         pltpu.VMEM((peers, 16, 128), BF),
-        pltpu.VMEM((2, 16, 128), F32),
+        pltpu.VMEM((2, 40, 128), F32),
         pltpu.VMEM((16, 128), F32),
-        pltpu.VMEM((2, 8, HALF + 128), F32),
-        pltpu.SemaphoreType.DMA((11,)),
-        pltpu.SemaphoreType.DMA((11,)),
+        pltpu.VMEM((2, 8, HALF), F32),
+        pltpu.SemaphoreType.DMA((12,)),
+        pltpu.SemaphoreType.DMA((12,)),
         pltpu.SemaphoreType.DMA((6,)),
         pltpu.SemaphoreType.DMA((6,)),
     ]
-    shapes = [(8, 2 * HALF), (16, 128), (8, 128), (2, 16, 128)]
+    shapes = [(8, 2 * HALF), (16, 128), (2, 40, 128)]
     operands = [frames.transpose(0, 2, 1, 3), *shards, biases, *rows]
     scratch += [pltpu.VMEM(operand.shape, operand.dtype) for operand in operands[1:]]
     scratch += [pltpu.SemaphoreType.DMA((len(operands) - 1,))]
@@ -1158,7 +1219,6 @@
 def update_kernel(
     main_ref,
     convg_ref,
-    tile_ref,
     stats_ref,
     conv_ref,
     lin_ref,
@@ -1200,17 +1260,22 @@
     lin_low,
 ):
     stats = stats_ref[...]
-    tile = tile_ref[...]
-    squares = jnp.where(iota((2, 16, 128), 1) <= TILES, stats, 0.0)
-    squares = total_of(squares[0] + squares[1])
-    scales = stats[0, TILES + 1 : TILES + 2] + stats[0, TILES + 2 : TILES + 3]
+    both = stats[0] + stats[1]
+    squares = total_of(both[0:TILES]) + total_of(both[32:33])
+    scales = stats[0, TILES + 2 : TILES + 3]
+    scales = [
+        scales[:, SCALE_LANE + k : SCALE_LANE + k + 1]
+        + scales[:, SCALE_LANE + k + 5 : SCALE_LANE + k + 6]
+        for k in range(5)
+    ]
     bias_raw = jnp.concatenate(
-        [tile[4:5, 64 : 64 + C1 + C2]] + [tile[k : k + 1, 64:128] for k in range(4)], axis=1
+        [both[TILES + 2 : TILES + 3, 0 : C1 + C2], both[TILES : TILES + 1], both[TILES + 1 : TILES + 2]],
+        axis=1,
     )
     norm = jnp.sqrt(squares + total_of(bias_raw * bias_raw))
     factor = jnp.minimum(1.0, CLIP_LIMIT / norm)
     norm_out[...] = norm
-    loss_out[...] = total_of(tile[5:6, 64:128])
+    loss_out[...] = total_of(both[TILES + 2 : TILES + 3, 64:128])
 
     def simple(weight, grad, moment, square_total, outs):
         new, moment_new = unfactored(
@@ -1225,7 +1290,7 @@
         conv_ref[...],
         factor * convg_ref[:, 0 : C1 + C2],
         conv_moment[...],
-        scales[:, 0:1],
+        scales[0],
         (conv_new, conv_grad, conv_moment_new, peers),
     )
     conv_low[...] = conv.astype(BF)
@@ -1233,7 +1298,7 @@
         emb_ref[...],
         factor * main_ref[:, AT_EMB:AT_HEADS],
         emb_moment[...],
-        scales[:, 3:4],
+        scales[3],
         (emb_new, emb_grad, emb_moment_new, peers),
     )
     heads_t = jnp.concatenate(
@@ -1243,7 +1308,7 @@
         heads_ref[...],
         factor * heads_t[HEAD_LANE : HEAD_LANE + 3 * GAMES, 0:8],
         head_moment[...],
-        scales[:, 4:5],
+        scales[4],
         (heads_new, heads_grad, head_moment_new, peers),
     )
     bias = bias_ref[...].reshape(1, BIAS)
@@ -1276,7 +1341,7 @@
         lin_rows[...].reshape(1, FEAT),
         column_of(lin_cols[...]),
         jnp.concatenate(row_sums[:21], axis=1)[:, 0:FEAT],
-        scales[:, 1:2],
+        scales[1],
         FEAT * D,
     )
     lin_new[...] = new
@@ -1292,7 +1357,7 @@
             mats_rows[k : k + 1],
             column_of(mats_cols[k : k + 1]),
             row_sums[21 + k],
-            scales[:, 2:3],
+            scales[2],
             3 * D * D,
         )
         mats_new[k] = new

time: 44 us -> 42 us (0.955)
  Pallas kernels: 42.9 us -> 41 us
    pallas_call x1, Pallas kernels: 40.6 us -> 38.7 us  [fused_step(): pl.pallas_call(functools.partial(fused_kernel, peers), out_shape=[jax.Sha...]
where the time goes in v5:
time: 42 us; the launch traced here: 41.7 us
  Pallas kernels  41 us (98%)
  between operations  0.67 us (2%)
    pallas_call x1, Pallas kernels, fused_step(): pl.pallas_call(functools.partial(fused_kernel, peers), out_shape=[jax.Sha...  38.7 us
    pallas_call x1, Pallas kernels, fused_device(): pl.pallas_call(update_kernel, out_shape=outs, in_specs=[VMEM_SPEC] * len(...  2.36 us

profile of v5, /device:TPU:0, one launch (start us, length us, event | category | flops | bytes accessed | tf_op | source)
XLA Modules:
  0.0 41.7 jit_solution(1968164756878361866)
XLA Ops:
  0.7 38.7 %shard_map.388 = (f32[8,3072]{1,0:T(8,128)}, f32[16,128]{1,0:T(8,128)}, f32[2,40,128]{2,1,0:T(8,128)}) custom-call(bf16[2,84,64,336]{3,2,1,0:T(8,128)(2,1)} %bitcast.27, f32[16,48]{1,0:T(8,128)} %conv_ref.1, f32[8,2592]{1,0:T(8,128)} %bitcast.28, f32[3,8,128]{2,1,0:T(8,128)} %bitcast.30, f32[8,18]{1,0:T(8,128)} %bitcast.35, f32[24,8]{1,0:T(8,128)} %bitcast.32, ...), custom_call_target="tpu_custom_call" | custom-call | tf_op jit(solution)/shard_map/pallas_call | solution.py:1193
  39.3 2.4 %shard_map.389 = (f32[16,48]{1,0:T(8,128)}, f32[16,48]{1,0:T(8,128)}, f32[16,48]{1,0:T(8,128)}, f32[8,2592]{1,0:T(8,128)}, f32[8,2592]{1,0:T(8,128)}, /*index=5*...) custom-call(f32[8,3072]{1,0:T(8,128)} %get-tuple-element.51.main_ref, ...), custom_call_target="tpu_custom_call" | custom-call | tf_op jit(solution)/shard_map/pallas_call | solution.py:1432

commit v6 on v5

--- a/solution.py
+++ b/solution.py
@@ -1068,16 +1068,15 @@
     back_two(d_state_low, linear_t, slope_two, dz_two, frames)
     wait_mate()
     grad_msg[...] = (grad_own[section].astype(F32) + mate_in[...].astype(F32)).astype(BF)
-    for which in range(2):
-
-        def collect(step):
-            peer = beside(step)
-            owner = across(which, lax.rem(peer, FOUR))
-            send(6, peer, grad_msg.at[owner], cross_in.at[which, column])
-
-        loop(1, FOUR, collect)
-        cross_in[which, column] = grad_msg[across(which, column)]
-    wait_cross = settle(6, grad_msg.at[pl.ds(0, 2 * (FOUR - 1))])
+    twin = beyond(0)
+
+    def collect(step):
+        peer = near(step)
+        send(6, peer, grad_msg.at[lax.rem(peer + NEAR, peers)], cross_in.at[spot])
+
+    loop(1, NEAR, collect)
+    cross_in[spot] = grad_msg[twin]
+    wait_cross = settle(6, cross_in.at[pl.ds(0, NEAR - 1)])
     loop(1, NEAR, lambda step: send(7, near(step), grad_msg.at[near(step)], near_in.at[spot]))
     wait_grads = settle(7, near_in.at[pl.ds(0, NEAR - 1)])
     near_in[spot] = grad_msg[place]
@@ -1096,8 +1095,8 @@
     wait_row = settle(9, row_in.at[pl.ds(0, 2 * FOUR - 1)])
     row_in[own] = taps_msg[section]
     wait_cross()
-    cross_msg[...] = jnp.sum(cross_in[...].astype(F32), axis=1).astype(BF)
-    loop(0, 2, lambda step: send(8, across(step, column), cross_msg.at[step], far_in.at[row]))
+    cross_msg[...] = jnp.sum(cross_in[...].astype(F32), axis=0).astype(BF)
+    send(8, twin, cross_msg, far_in)
     wait_far = settle(8, far_in)
     wait_row()
     level = place // FOUR
@@ -1112,7 +1111,7 @@
     wait_rows = settle(11, rows_in.at[pl.ds(0, peers // FOUR - 1)])
     wait_grads()
     wait_far()
-    total = jnp.sum(near_in[...].astype(F32), axis=0) + jnp.sum(far_in[...].astype(F32), axis=0)
+    total = jnp.sum(near_in[...].astype(F32), axis=0) + far_in[...].astype(F32)
     squares = total * total
     stat = stats_base[...]
     for part in range(2):
@@ -1170,9 +1169,9 @@
         pltpu.VMEM((peers, 16, QUARTER), BF),
         pltpu.VMEM((peers, 16, QUARTER), BF),
         pltpu.VMEM((NEAR, 16, QUARTER), BF),
-        pltpu.VMEM((2, FOUR, 16, QUARTER), BF),
-        pltpu.VMEM((2, 16, QUARTER), BF),
-        pltpu.VMEM((2, 16, QUARTER), BF),
+        pltpu.VMEM((NEAR, 16, QUARTER), BF),
+        pltpu.VMEM((16, QUARTER), BF),
+        pltpu.VMEM((16, QUARTER), BF),
         pltpu.VMEM((2, C1 + C2, 128), BF),
         pltpu.VMEM((2 * FOUR, C1 + C2, 128), BF),
         pltpu.VMEM((peers // FOUR, C1 + C2, 128), BF),

time: 42 us -> 40.8 us (0.971)
  Pallas kernels: 41 us -> 39.9 us
    pallas_call x1, Pallas kernels: 38.7 us -> 37.6 us  [fused_step(): pl.pallas_call(functools.partial(fused_kernel, peers), out_shape=[jax.Sha...]
where the time goes in v6:
time: 40.8 us; the launch traced here: 40.6 us
  Pallas kernels  39.9 us (98%)
  between operations  0.67 us (2%)
    pallas_call x1, Pallas kernels, fused_step(): pl.pallas_call(functools.partial(fused_kernel, peers), out_shape=[jax.Sha...  37.6 us
    pallas_call x1, Pallas kernels, fused_device(): pl.pallas_call(update_kernel, out_shape=outs, in_specs=[VMEM_SPEC] * len(...  2.36 us

profile of v6, /device:TPU:0, one launch (start us, length us, event | category | flops | bytes accessed | tf_op | source)
XLA Modules:
  0.0 40.6 jit_solution(1961015151680780118)
XLA Ops:
  0.7 37.6 %shard_map.388 = (f32[8,3072]{1,0:T(8,128)}, f32[16,128]{1,0:T(8,128)}, f32[2,40,128]{2,1,0:T(8,128)}) custom-call(bf16[2,84,64,336]{3,2,1,0:T(8,128)(2,1)} %bitcast.27, f32[16,48]{1,0:T(8,128)} %conv_ref.1, f32[8,2592]{1,0:T(8,128)} %bitcast.28, f32[3,8,128]{2,1,0:T(8,128)} %bitcast.30, f32[8,18]{1,0:T(8,128)} %bitcast.35, f32[24,8]{1,0:T(8,128)} %bitcast.32, ...), custom_call_target="tpu_custom_call" | custom-call | tf_op jit(solution)/shard_map/pallas_call | solution.py:1192
  38.2 2.4 %shard_map.389 = (f32[16,48]{1,0:T(8,128)}, f32[16,48]{1,0:T(8,128)}, f32[16,48]{1,0:T(8,128)}, f32[8,2592]{1,0:T(8,128)}, f32[8,2592]{1,0:T(8,128)}, /*index=5*...) custom-call(f32[8,3072]{1,0:T(8,128)} %get-tuple-element.51.main_ref, ...), custom_call_target="tpu_custom_call" | custom-call | tf_op jit(solution)/shard_map/pallas_call | solution.py:1431

commit v7 on v6

--- a/solution.py
+++ b/solution.py
@@ -1064,10 +1064,18 @@
     parts = [part.reshape(peers, 8, QUARTER) for part in parts]
     for half in range(2):
         grad_own[half] = jnp.concatenate(parts[2 * half : 2 * half + 2], axis=1).astype(BF)
-    wait_mate = send_mate(1, grad_own.at[mate], mate_in, mate_in)
+    wait_mate_far, wait_mate_near = (
+        send_mate(which, grad_own.at[mate, part], mate_in.at[part], mate_in.at[part])
+        for which, part in ((1, far_side), (2, own_side))
+    )
     back_two(d_state_low, linear_t, slope_two, dz_two, frames)
-    wait_mate()
-    grad_msg[...] = (grad_own[section].astype(F32) + mate_in[...].astype(F32)).astype(BF)
+
+    def pair_up(part):
+        paired = grad_own[section, part].astype(F32) + mate_in[part].astype(F32)
+        grad_msg[part] = paired.astype(BF)
+
+    wait_mate_far()
+    pair_up(far_side)
     twin = beyond(0)
 
     def collect(step):
@@ -1077,6 +1085,8 @@
     loop(1, NEAR, collect)
     cross_in[spot] = grad_msg[twin]
     wait_cross = settle(6, cross_in.at[pl.ds(0, NEAR - 1)])
+    wait_mate_near()
+    pair_up(own_side)
     loop(1, NEAR, lambda step: send(7, near(step), grad_msg.at[near(step)], near_in.at[spot]))
     wait_grads = settle(7, near_in.at[pl.ds(0, NEAR - 1)])
     near_in[spot] = grad_msg[place]

time: 40.8 us -> 40.6 us (level)
  no operation moved by 1% of the time
where the time goes in v7:
time: 40.6 us; the launch traced here: 40.3 us
  Pallas kernels  39.6 us (98%)
  between operations  0.67 us (2%)
    pallas_call x1, Pallas kernels, fused_step(): pl.pallas_call(functools.partial(fused_kernel, peers), out_shape=[jax.Sha...  37.3 us
    pallas_call x1, Pallas kernels, fused_device(): pl.pallas_call(update_kernel, out_shape=outs, in_specs=[VMEM_SPEC] * len(...  2.36 us

profile of v7, /device:TPU:0, one launch (start us, length us, event | category | flops | bytes accessed | tf_op | source)
XLA Modules:
  0.0 40.3 jit_solution(15029352296284687023)
XLA Ops:
  0.7 37.3 %shard_map.388 = (f32[8,3072]{1,0:T(8,128)}, f32[16,128]{1,0:T(8,128)}, f32[2,40,128]{2,1,0:T(8,128)}) custom-call(bf16[2,84,64,336]{3,2,1,0:T(8,128)(2,1)} %bitcast.27, f32[16,48]{1,0:T(8,128)} %conv_ref.1, f32[8,2592]{1,0:T(8,128)} %bitcast.28, f32[3,8,128]{2,1,0:T(8,128)} %bitcast.30, f32[8,18]{1,0:T(8,128)} %bitcast.35, f32[24,8]{1,0:T(8,128)} %bitcast.32, ...), custom_call_target="tpu_custom_call" | custom-call | tf_op jit(solution)/shard_map/pallas_call | solution.py:1202
  37.9 2.4 %shard_map.389 = (f32[16,48]{1,0:T(8,128)}, f32[16,48]{1,0:T(8,128)}, f32[16,48]{1,0:T(8,128)}, f32[8,2592]{1,0:T(8,128)}, f32[8,2592]{1,0:T(8,128)}, /*index=5*...) custom-call(f32[8,3072]{1,0:T(8,128)} %get-tuple-element.51.main_ref, ...), custom_call_target="tpu_custom_call" | custom-call | tf_op jit(solution)/shard_map/pallas_call | solution.py:1441
